TPU v7x, 512 devices: a whole 4x8x8 slice. The times are simulated.
512 devices in a mesh: gx: 4 (over y_hi), gy: 8 (over z), gz: 16 (over x, y_lo, core).
Axes of the slice: x: 4, y: 8 (y_hi: 4, y_lo: 2; y = y_hi * 2 + y_lo), z: 8, core: 2. Of those that a mesh axis runs over, the one named last changes fastest.
Arguments:
- fine_source_field: float32 [20, 80, 5120], P('gx', 'gy', 'gz'), may hold values from -6 to 6
- scaling: float32 [4, 16, 1024], P('gx', 'gy', 'gz'), may hold values from 0.5 to 2
- block_fine: float32 [125, 125], replicated, may hold values from -5 to 16, as said below
- block_mid: float32 [27, 27], replicated, may hold values from -5 to 32, as said below
- block_coarse: float32 [8, 8], replicated, may hold values from -1 to 4, as said below
Outputs:
- solution: float32 [20, 80, 5120], P('gx', 'gy', 'gz')
Inputs may be any that keep to these rules, and one draw needn't show every extreme that they name: `block_fine`: symmetric positive definite. `block_mid`: symmetric positive definite. `block_coarse`: symmetric positive definite.
All inputs are finite; a program needn't handle non-finite values.
Results may differ from a plain program's by a relative error of at most 0.0001.
Values sent between devices are 32-bit elements; how exact they have to be, the bound alone decides.
No kernel may reach another device: no remote copies, remote signals or barrier semaphores. Data moves between devices by JAX's collectives and lax.ppermute only.
A program may use at most 64 MiB of HBM per device.

v0:
```python
import math

import jax
import jax.numpy as jnp
import numpy as np
from jax import lax
from jax.experimental import pallas as pl
from jax.experimental.pallas import tpu as pltpu
from jax.sharding import PartitionSpec as P

FINE = 5
MID = 3
COARSE = 2
CSWEEPS = 4
RADIUS = 15
WINDOW = 32
EX = 4
EY = 16
ROWS = WINDOW * EY
LANES = 128

f32 = jnp.float32
bf16 = jnp.bfloat16
HIGHEST = lax.Precision.HIGHEST
MIB = 1 << 20


def gll_points(points):
    if points == 5:
        return np.array([-1.0, -math.sqrt(3.0 / 7.0), 0.0, math.sqrt(3.0 / 7.0), 1.0])
    if points == 3:
        return np.array([-1.0, 0.0, 1.0])
    return np.array([-1.0, 1.0])


def lagrange(fine_points, coarse_points):
    fine_nodes = gll_points(fine_points)
    coarse_nodes = gll_points(coarse_points)
    table = np.ones((fine_points, coarse_points))
    for column in range(coarse_points):
        for other in range(coarse_points):
            if other != column:
                table[:, column] *= (fine_nodes - coarse_nodes[other]) / (
                    coarse_nodes[column] - coarse_nodes[other]
                )
    return table


def halves(table):
    table = np.asarray(table, np.float32)
    hi = table.astype(jnp.bfloat16)
    lo = (table - hi.astype(np.float32)).astype(jnp.bfloat16)
    return np.block([[hi, lo], [hi, np.zeros_like(lo)]])


def transfer_tables():
    fine_mid = np.kron(np.kron(lagrange(5, 3), lagrange(5, 3)), lagrange(5, 3))
    mid_coarse = np.kron(np.kron(lagrange(3, 2), lagrange(3, 2)), lagrange(3, 2))
    down, up = [], []
    for place in range(EX):
        table = np.zeros((LANES, LANES))
        table[:125, place * 32 : place * 32 + 27] = fine_mid
        down.append(halves(table))
        up.append(halves(table.T))
    middle = np.zeros((LANES, LANES))
    for place in range(EX):
        middle[place * 32 : place * 32 + 27, place * 32 : place * 32 + 8] = mid_coarse
    return np.stack(down), np.stack(up), halves(middle), halves(middle.T)


def spread_tables(count_z):
    tables = []
    for y in range(2):
        table = np.zeros((FINE * count_z, FINE * LANES), np.float32)
        for z in range(count_z):
            for k in range(FINE):
                table[z * FINE + k, k * LANES + y * count_z + z] = 1.0
        tables.append(table)
    return tables


def three_way(values):
    one = values.astype(bf16)
    rest = values - one.astype(f32)
    two = rest.astype(bf16)
    three = (rest - two.astype(f32)).astype(bf16)
    return jnp.concatenate([one, two, three], axis=0)


def pack_body(field_ref, scale_ref, table_ref, out_ref, above, below, nodes):
    for i in range(FINE):
        above[i * FINE : (i + 1) * FINE, :] = field_ref[i, 0:FINE, :]
        below[i * FINE : (i + 1) * FINE, :] = field_ref[i, FINE : 2 * FINE, :]
    spread = jnp.dot(three_way(above[...]), table_ref[0], preferred_element_type=f32)
    spread = spread + jnp.dot(three_way(below[...]), table_ref[1], preferred_element_type=f32)
    spread = spread[0:32] + spread[32:64] + spread[64:96]
    nodes[...] = jnp.zeros((LANES, LANES), f32)
    for k in range(FINE):
        nodes[pl.ds(k, FINE * FINE, stride=FINE), :] = spread[
            0 : FINE * FINE, k * LANES : (k + 1) * LANES
        ]
    out_ref[...] = (nodes[...] / scale_ref[...]).T


def pack(field, scale_row, tables):
    return pl.pallas_call(
        pack_body,
        out_shape=jax.ShapeDtypeStruct((LANES, LANES), f32),
        scratch_shapes=[
            pltpu.VMEM((32, field.shape[2]), f32),
            pltpu.VMEM((32, field.shape[2]), f32),
            pltpu.VMEM((LANES, LANES), f32),
        ],
        compiler_params=pltpu.CompilerParams(vmem_limit_bytes=8 * MIB),
        name="pack",
    )(field, scale_row, tables)


def unpack_body(back_ref, scale_ref, table_ref, out_ref, nodes):
    half = back_ref.shape[0] // 2
    upper = back_ref[pl.ds(0, half, stride=2), :]
    lower = back_ref[pl.ds(1, half, stride=2), :]
    nodes[...] = jnp.concatenate([upper, lower], axis=0).T / scale_ref[...]
    grouped = [nodes[pl.ds(k, FINE * FINE, stride=FINE), :] for k in range(FINE)]
    grouped = jnp.concatenate(grouped, axis=1)
    grouped = jnp.concatenate([grouped, jnp.zeros((7, FINE * LANES), f32)], axis=0)
    split = three_way(grouped)
    for y in range(2):
        lines = jnp.dot(split, table_ref[y], preferred_element_type=f32)
        lines = lines[0:32] + lines[32:64] + lines[64:96]
        for i in range(FINE):
            out_ref[i, y * FINE : (y + 1) * FINE, :] = lines[i * FINE : (i + 1) * FINE]


def unpack(back, scale_row, tables, shape):
    return pl.pallas_call(
        unpack_body,
        out_shape=jax.ShapeDtypeStruct(shape, f32),
        scratch_shapes=[pltpu.VMEM((LANES, LANES), f32)],
        compiler_params=pltpu.CompilerParams(vmem_limit_bytes=8 * MIB),
        name="unpack",
    )(back, scale_row, tables)


def window_body(own_ref, before_ref, after_ref, out_ref, line, *, count_z, parts):
    for y in range(2):
        line[y, 0:16, :] = before_ref[y]
        line[y, 16 : 16 + count_z, :] = own_ref[y * count_z : (y + 1) * count_z, :]
        line[y, 16 + count_z : 32 + count_z, :] = after_ref[y]
    for part in range(parts):
        for y in range(2):
            start = 16 + 2 * part - RADIUS
            out_ref[part, y * WINDOW : (y + 1) * WINDOW, :] = line[y, start : start + WINDOW, :]


def window(own, before, after, parts):
    count_z = own.shape[0] // 2

    def body(*refs):
        window_body(*refs, count_z=count_z, parts=parts)

    return pl.pallas_call(
        body,
        out_shape=jax.ShapeDtypeStruct((parts, 2 * WINDOW, LANES), f32),
        scratch_shapes=[pltpu.VMEM((2, count_z + 32, LANES), f32)],
        compiler_params=pltpu.CompilerParams(vmem_limit_bytes=8 * MIB),
        name="window",
    )(own, before, after)


def iota(shape, dimension):
    return lax.broadcasted_iota(jnp.int32, shape, dimension)


def shifted_block(ref, pad, points):
    nodes = points**3
    pad[...] = jnp.zeros((LANES, LANES), f32)
    pad[0:nodes, 0:nodes] = ref[...]
    lane, row = iota((LANES, LANES), 1), iota((LANES, LANES), 0)
    count = jnp.zeros((LANES, LANES), f32)
    for stride in (points * points, points, 1):
        index = (lane // stride) % points
        count = count + jnp.where((index == 0) | (index == points - 1), 0.5, 0.0)
    diagonal = jnp.where(lane < nodes, count, 1.0)
    return pad[...] + jnp.where(lane == row, diagonal, 0.0)


def invert(matrix, panels):
    lane, row = iota((LANES, LANES), 1), iota((LANES, LANES), 0)
    lane16, row16 = iota((16, LANES), 1), iota((16, LANES), 0)
    for panel in range(panels):
        top = panel * 16
        rows = matrix[top : top + 16, :]
        for step in range(16):
            pivot = top + step
            column = rows[:, pivot : pivot + 1]
            scale = 1.0 / rows[step : step + 1, pivot : pivot + 1]
            scaled = jnp.where(lane16[0:1] == pivot, scale, rows[step : step + 1, :] * scale)
            others = jnp.where(lane16 == pivot, 0.0, rows) - column * scaled
            rows = jnp.where(row16 == step, scaled, others)
        stacked = jnp.concatenate([rows] * 8, axis=0)
        inside = (lane >= top) & (lane < top + 16)
        update = jnp.dot(
            jnp.where(inside, matrix, 0.0), stacked, precision=HIGHEST, preferred_element_type=f32
        )
        matrix = jnp.where(
            (row >= top) & (row < top + 16), stacked, jnp.where(inside, 0.0, matrix) - update
        )
    return matrix


def repeated(matrix):
    lane, row = iota((LANES, LANES), 1), iota((LANES, LANES), 0)
    pick = jnp.where((row % 32 == lane) & (lane < 32), 1.0, 0.0)
    put = jnp.where((lane % 32 == row) & (row < 32), 1.0, 0.0)
    tall = jnp.dot(pick, matrix, precision=HIGHEST, preferred_element_type=f32)
    wide = jnp.dot(tall, put, precision=HIGHEST, preferred_element_type=f32)
    return jnp.where(row // 32 == lane // 32, wide, 0.0)


def inverses_body(fine_ref, mid_ref, coarse_ref, fine_out, mid_out, coarse_out, pad):
    coarse = invert(shifted_block(coarse_ref, pad, COARSE), 1)
    mid = invert(shifted_block(mid_ref, pad, MID), 2)
    fine = invert(shifted_block(fine_ref, pad, FINE), 8)
    fine_out[...] = 0.35 * fine
    mid_out[...] = 0.35 * repeated(mid)
    coarse_out[...] = 0.35 * repeated(coarse)


def inverses(block_fine, block_mid, block_coarse):
    square = jax.ShapeDtypeStruct((LANES, LANES), f32)
    return pl.pallas_call(
        inverses_body,
        out_shape=(square, square, square),
        scratch_shapes=[pltpu.VMEM((LANES, LANES), f32)],
        compiler_params=pltpu.CompilerParams(vmem_limit_bytes=8 * MIB),
        cost_estimate=pl.CostEstimate(
            flops=2_000_000_000, bytes_accessed=20_000_000, transcendentals=0
        ),
        name="inverses",
    )(block_fine, block_mid, block_coarse)


def two_way(values):
    hi = values.astype(bf16)
    lo = (values - hi.astype(f32)).astype(bf16)
    return jnp.concatenate([hi, lo], axis=1)


def two_way_table(table):
    hi = table.astype(bf16)
    lo = (table - hi.astype(f32)).astype(bf16)
    return jnp.concatenate(
        [jnp.concatenate([hi, lo], axis=1), jnp.concatenate([hi, jnp.zeros_like(lo)], axis=1)],
        axis=0,
    )


def times(values, table):
    result = jnp.dot(two_way(values), table, preferred_element_type=f32)
    return result[:, 0:LANES] + result[:, LANES : 2 * LANES]


class Faces:
    def __init__(self, points, in_lanes):
        nodes = points**3
        lane, row = iota((EY, LANES), 1), iota((EY, LANES), 0)
        local = lane % 32 if in_lanes else lane
        place = lane // 32
        self.turns = []
        for dimension, stride in enumerate((points * points, points, 1)):
            index = (local // stride) % points
            first = (index == 0) & (local < nodes)
            last = (index == points - 1) & (local < nodes)
            reach = (points - 1) * stride
            if dimension == 0 and in_lanes:
                first, last = first & (place > 0), last & (place < EX - 1)
                reach = reach - 32
            if dimension == 1:
                first, last = first & (row > 0), last & (row < EY - 1)
            self.turns.append((first[None], last[None], (-reach) % LANES, reach % LANES))

    def gather(self, pairs):
        total = None
        for (before, after), (first, last, down, up) in zip(pairs, self.turns):
            part = 0.0
            if after is not None:
                slabs = after.shape[0] // EY
                turned = pltpu.roll(after, up, 1).reshape(slabs, EY, LANES)
                part = jnp.where(last, turned, part)
            if before is not None:
                slabs = before.shape[0] // EY
                turned = pltpu.roll(before, down, 1).reshape(slabs, EY, LANES)
                part = jnp.where(first, turned, part)
            total = part if total is None else total + part
        return total.reshape(-1, LANES)


CHUNK = 8


def cuts(start, stop):
    count = -(-(stop - start) // CHUNK)
    edges = [start + (stop - start) * piece // count for piece in range(count + 1)]
    return list(zip(edges[:-1], edges[1:]))


def cycle_body(
    bounds_ref,
    recv_ref,
    fine_ref,
    mid_ref,
    coarse_ref,
    down_ref,
    up_ref,
    low_ref,
    high_ref,
    out_ref,
    start,
    ping,
    pong,
    left,
    mid_start,
    mid_ping,
    mid_pong,
    mid_left,
    mask,
):
    fine_faces = Faces(FINE, False)
    mid_faces = Faces(MID, True)
    coarse_faces = Faces(COARSE, True)
    fine_table = two_way_table(fine_ref[...])
    mid_table = two_way_table(mid_ref[...])
    coarse_table = two_way_table(coarse_ref[...])

    slab = iota((ROWS, LANES), 0) // EY
    mask[...] = jnp.where((slab >= bounds_ref[0]) & (slab < bounds_ref[1]), 1.0, 0.0)

    def at(x, a, b, offset=0):
        return slice(x * ROWS + a * EY + offset, x * ROWS + b * EY + offset)

    def fine_gather(ref, x, a, b):
        return fine_faces.gather(
            (
                (
                    ref[at(x - 1, a, b), :] if x > 0 else None,
                    ref[at(x + 1, a, b), :] if x < EX - 1 else None,
                ),
                (ref[at(x, a, b, -1), :], ref[at(x, a, b, 1), :]),
                (ref[at(x, a - 1, b - 1), :], ref[at(x, a + 1, b + 1), :]),
            )
        )

    def fine_sweep(source, target, a, b, keep):
        for x in range(EX):
            for c, d in cuts(a, b):
                rows = at(x, c, d)
                faces = fine_gather(source, x, c, d)
                if keep is not None:
                    left[rows, :] = left[rows, :] + keep * faces
                moved = 0.3 * source[rows, :] + start[rows, :] + times(faces, fine_table)
                target[rows, :] = moved * mask[at(0, c, d), :]

    for x in range(EX):
        for c, d in cuts(0, WINDOW):
            values = jnp.concatenate(
                [recv_ref[pl.ds(x * ROWS + z, EY, stride=WINDOW), :] for z in range(c, d)], axis=0
            )
            rows = at(x, c, d)
            left[rows, :] = 0.027 * values
            start[rows, :] = 2.0 * times(values, fine_table)

    fine_sweep(start, ping, 1, 31, -0.105)
    fine_sweep(ping, pong, 2, 30, -0.35)

    def mid_gather(faces, ref, a, b):
        here = ref[at(0, a, b), :]
        return faces.gather(
            (
                (here, here),
                (ref[at(0, a, b, -1), :], ref[at(0, a, b, 1), :]),
                (ref[at(0, a - 1, b - 1), :], ref[at(0, a + 1, b + 1), :]),
            )
        )

    for c, d in cuts(3, 29):
        total = None
        for x in range(EX):
            rest = left[at(x, c, d), :] + 0.5 * fine_gather(pong, x, c, d)
            part = times(rest, down_ref[x])
            total = part if total is None else total + part
        rows = at(0, c, d)
        total = total * mask[rows, :]
        mid_left[rows, :] = 0.027 * total
        mid_start[rows, :] = 2.0 * times(total, mid_table)

    def mid_sweep(faces, table, base, source, target, a, b, keep=None):
        for c, d in cuts(a, b):
            rows = at(0, c, d)
            values = mid_gather(faces, source, c, d)
            if keep is not None:
                mid_left[rows, :] = mid_left[rows, :] + keep * values
            moved = 0.3 * source[rows, :] + base[rows, :] + times(values, table)
            target[rows, :] = moved * mask[rows, :]

    mid_sweep(mid_faces, mid_table, mid_start, mid_start, mid_ping, 4, 28, -0.105)
    mid_sweep(mid_faces, mid_table, mid_start, mid_ping, mid_pong, 5, 27, -0.35)

    base = ping.at[0:ROWS]
    even = ping.at[ROWS : 2 * ROWS]
    odd = ping.at[2 * ROWS : 3 * ROWS]
    for c, d in cuts(6, 26):
        rows = at(0, c, d)
        rest = mid_left[rows, :] + 0.5 * mid_gather(mid_faces, mid_pong, c, d)
        low = times(rest * mask[rows, :], low_ref[...])
        base[rows, :] = 2.0 * times(low, coarse_table)
    mid_sweep(coarse_faces, coarse_table, base, base, even, 7, 25)
    mid_sweep(coarse_faces, coarse_table, base, even, odd, 8, 24)
    mid_sweep(coarse_faces, coarse_table, base, odd, even, 9, 23)

    for c, d in cuts(9, 23):
        rows = at(0, c, d)
        mid_pong[rows, :] = mid_pong[rows, :] + times(even[rows, :], high_ref[...])
    mid_sweep(mid_faces, mid_table, mid_start, mid_pong, mid_ping, 10, 22)
    mid_sweep(mid_faces, mid_table, mid_start, mid_ping, mid_pong, 11, 21)
    mid_sweep(mid_faces, mid_table, mid_start, mid_pong, mid_ping, 12, 20)

    lifted = two_way(mid_ping[at(0, 12, 20), :])
    for x in range(EX):
        rows = at(x, 12, 20)
        added = jnp.dot(lifted, up_ref[x], preferred_element_type=f32)
        added = added[:, 0:LANES] + added[:, LANES : 2 * LANES]
        pong[rows, :] = pong[rows, :] + added
    fine_sweep(pong, ping, 13, 19, None)
    fine_sweep(ping, pong, 14, 18, None)
    fine_sweep(pong, ping, 15, 17, None)

    for x in range(EX):
        for z in range(2):
            for y in range(2):
                values = ping[pl.ds(x * ROWS + (15 + z) * EY + y, 8, stride=2), :]
                out_ref[pl.ds(x * 32 + z * 2 + y, 8, stride=4), :] = values


def cycle(bounds, recv, fine, mid, coarse, down, up, low, high):
    big = pltpu.VMEM((EX * ROWS, LANES), f32)
    small = pltpu.VMEM((ROWS, LANES), f32)
    vmem = pl.BlockSpec(memory_space=pltpu.VMEM)
    return pl.pallas_call(
        cycle_body,
        out_shape=jax.ShapeDtypeStruct((LANES, LANES), f32),
        in_specs=[pl.BlockSpec(memory_space=pltpu.SMEM)] + [vmem] * 8,
        out_specs=vmem,
        scratch_shapes=[big, big, big, big, small, small, small, small, small],
        compiler_params=pltpu.CompilerParams(vmem_limit_bytes=32 * MIB),
        name="cycle",
    )(bounds, recv, fine, mid, coarse, down, up, low, high)


def per_device(fine_source_field, scaling, block_fine, block_mid, block_coarse):
    count_z = scaling.shape[2]
    parts = lax.axis_size("gx") * lax.axis_size("gy")
    groups = lax.axis_size("gz")
    down, up, low, high = transfer_tables()
    tables = np.stack(spread_tables(count_z)).astype(jnp.bfloat16)
    back_tables = np.ascontiguousarray(tables.transpose(0, 2, 1))
    scale_row = scaling.reshape(1, 2 * count_z)

    own = pack(fine_source_field, scale_row, tables)
    lines = own.reshape(2, count_z, LANES)
    before = lax.ppermute(lines[:, count_z - 16 :], "gz", [(i, i + 1) for i in range(groups - 1)])
    after = lax.ppermute(lines[:, :16], "gz", [(i + 1, i) for i in range(groups - 1)])
    chunks = window(own, before, after, parts)
    recv = lax.all_to_all(chunks, ("gx", "gy"), 0, 0, tiled=True)
    fine, mid, coarse = inverses(block_fine, block_mid, block_coarse)

    part = lax.axis_index("gx") * lax.axis_size("gy") + lax.axis_index("gy")
    first = lax.axis_index("gz") * count_z + 2 * part - RADIUS
    bounds = jnp.stack([jnp.maximum(0, -first), jnp.minimum(WINDOW, groups * count_z - first)])
    result = cycle(
        bounds.astype(jnp.int32),
        recv.reshape(EX * ROWS, LANES),
        fine,
        mid,
        coarse,
        down,
        up,
        low,
        high,
    )
    back = lax.all_to_all(result.reshape(parts, 4, LANES), ("gx", "gy"), 0, 0, tiled=True)
    return unpack(back.reshape(LANES, LANES), scale_row, back_tables, fine_source_field.shape)


def solution(mesh):
    in_specs = (P("gx", "gy", "gz"), P("gx", "gy", "gz"), P(), P(), P())
    out_specs = P("gx", "gy", "gz")
    return jax.shard_map(
        per_device, mesh=mesh, in_specs=in_specs, out_specs=out_specs, check_vma=False
    )
```

profile of v0, /device:TPU:14, one launch (start us, length us, event | category | flops | bytes accessed | tf_op | source)
XLA Modules:
  0.0 90.3 jit_solution(9592004946873441192)
XLA Ops:
  0.0 0.8 reshape.15.scale_ref
  0.8 0.0 copy-start.1
  0.8 1.1 %copy-done.1 = bf16[2,320,640]{2,1,0:T(8,128)(2,1)S(1)} copy-done((bf16[2,320,640]{2,1,0:T(8,128)(2,1)S(1)}, bf16[2,320,640]{2,1,0:T(8,128)(2,1)}, u32[]{:S(2)}) %copy-start.1) | copy-done | bytes 819224
  1.9 0.0 copy-start.6
  1.9 0.9 copy-done.6
  2.8 0.4 pack.1.refs_0_
  3.2 1.9 %collective-permute-start = (f32[2,16,128]{2,1,0:T(8,128)S(1)}, f32[2,16,128]{2,1,0:T(8,128)S(1)}, u32[]{:S(2)}, u32[]{:S(2)}) collective-permute-start(f32[2,16,128]{2,1,0:T(8,128)S(1)} %get-tuple-element.12), channel_id=1, source_target_pairs={{0,1},{1,2},{2,3},{3,4},{4,5},{5,6},{6,7},{7,8},{8,9},{9,10},{10,1... | collective-permute-start | bytes 49160 | tf_op jit(solution)/shard_map/ppermute | solution.py:471
  5.2 3.6 %collective-permute-start.1 = (f32[2,16,128]{2,1,0:T(8,128)S(1)}, f32[2,16,128]{2,1,0:T(8,128)S(1)}, u32[]{:S(2)}, u32[]{:S(2)}) collective-permute-start(f32[2,16,128]{2,1,0:T(8,128)S(1)} %get-tuple-element.11), channel_id=1, source_target_pairs={{1,0},{2,1},{3,2},{4,3},{5,4},{6,5},{7,6},{8,7},{9,8},{10,9},{11,1... | collective-permute-start | bytes 49160 | tf_op jit(solution)/shard_map/ppermute | solution.py:472
  8.8 0.0 collective-permute-done.refs_1_
  8.8 1.4 %collective-permute-done.1.refs_2_ = f32[2,16,128]{2,1,0:T(8,128)S(1)} collective-permute-done((f32[2,16,128]{2,1,0:T(8,128)S(1)}, f32[2,16,128]{2,1,0:T(8,128)S(1)}, u32[]{:S(2)}, u32[]{:S(2)}) %collective-permute-start.1) | collective-permute-done | bytes 16416 | tf_op jit(solution)/shard_map/ppermute | solution.py:472
  10.2 1.1 %window.1 = f32[32,64,128]{2,1,0:T(8,128)} custom-call(f32[128,128]{1,0:T(8,128)S(1)} %pack.1.refs_0_, f32[2,16,128]{2,1,0:T(8,128)S(1)} %collective-permute-done.refs_1_, f32[2,16,128]{2,1,0:T(8,128)S(1)} %collective-permute-done.1.refs_2_), custom_call_target="tpu_custom_call" | custom-call | tf_op jit(solution)/shard_map/window/pallas_call | solution.py:162
  11.3 0.0 copy-start.7
  11.3 15.2 %all-to-all-start = ((f32[32,64,128]{2,1,0:T(8,128)}), f32[32,64,128]{2,1,0:T(8,128)S(1)}, u32[]{:S(2)}, u32[]{:S(2)}) async-start(f32[32,64,128]{2,1,0:T(8,128)} %window.1), calls=%async_computation | async-start | bytes 2097152 | tf_op jit(solution)/shard_map/all_to_all | solution.py:474
  26.5 0.0 copy-start.8
  26.5 0.0 copy-start.9
  26.6 0.1 pad_add_fusion.bounds_ref
  26.6 0.0 copy-done.7
  26.6 0.6 copy-done.8
  27.2 0.0 copy-done.9
  27.2 0.0 copy-start.2
  27.2 0.0 copy-start.3
  27.2 0.0 copy-start.4
  27.3 0.0 copy-start.5
  27.3 12.8 %inverses.1 = (f32[128,128]{1,0:T(8,128)S(1)}, f32[128,128]{1,0:T(8,128)S(1)}, f32[128,128]{1,0:T(8,128)S(1)}) custom-call(f32[125,125]{1,0:T(8,128)S(1)} %copy-done.7, f32[27,27]{1,0:T(8,128)S(1)} %copy-done.8, f32[8,8]{1,0:T(8,128)S(1)} %copy-done.9), custom_call_target="tpu_custom_call" | custom-call | flops 2000000000 | bytes 20000000 | tf_op jit(solution)/shard_map/inverses/pallas_call | solution.py:232
  40.0 18.7 %all-to-all-done = f32[32,64,128]{2,1,0:T(8,128)S(1)} async-done(((f32[32,64,128]{2,1,0:T(8,128)}), f32[32,64,128]{2,1,0:T(8,128)S(1)}, u32[]{:S(2)}, u32[]{:S(2)}) %all-to-all-start) | async-done | bytes 1048608 | tf_op jit(solution)/shard_map/all_to_all | solution.py:474
  58.7 0.0 copy-done.2
  58.7 0.0 copy-done.3
  58.7 0.0 copy-done.4
  58.8 0.0 copy-done.5
  58.8 0.0 copy-start
  58.8 8.8 %cycle.1 = f32[128,128]{1,0:T(8,128)S(1)} custom-call(s32[2]{0:T(128)S(1)} %pad_add_fusion.bounds_ref, f32[2048,128]{1,0:T(8,128)S(1)} %bitcast.6, f32[128,128]{1,0:T(8,128)S(1)} %get-tuple-element.8.fine_ref, f32[128,128]{1,0:T(8,128)S(1)} %get-tuple-element.9.mid_ref, f32[128,128]{1,0:T(8,128)S(1)} %get-tuple-element.10.coarse_ref, ...), custom_call_target="tpu_custom_call" | custom-call | tf_op jit(solution)/shard_map/cycle/pallas_call | solution.py:449
  67.6 21.7 %all_to_all.10 = f32[32,4,128]{2,1,0:T(4,128)S(1)} all-to-all(f32[32,4,128]{2,1,0:T(4,128)S(1)} %bitcast.8), channel_id=1, replica_groups=mesh['gx'=4,'gy'=8,'gz'=16] {'gx','gy'}, dimensions={0} | all-to-all | bytes 131072 | tf_op jit(solution)/shard_map/all_to_all | solution.py:491
  89.2 0.0 copy-done
  89.2 1.1 %unpack.1 = f32[5,10,320]{2,1,0:T(8,128)} custom-call(f32[128,128]{1,0:T(8,128)S(1)} %bitcast.9, f32[1,128]{1,0:T(1,128)S(1)} %reshape.15.scale_ref, bf16[2,640,320]{2,1,0:T(8,128)(2,1)S(1)} %copy-done), custom_call_target="tpu_custom_call" | custom-call | tf_op jit(solution)/shard_map/unpack/pallas_call | solution.py:136
  (1 shorter events, 0.0 us)
Async XLA Ops:
  0.8 1.1 %copy-start.1 = (bf16[2,320,640]{2,1,0:T(8,128)(2,1)S(1)}, bf16[2,320,640]{2,1,0:T(8,128)(2,1)}, u32[]{:S(2)}) copy-start(bf16[2,320,640]{2,1,0:T(8,128)(2,1)} %constant.41.clone.table_ref) | copy-start | bytes 2457604
  1.9 0.9 copy-start.6
  3.2 5.6 %collective-permute-start = (f32[2,16,128]{2,1,0:T(8,128)S(1)}, f32[2,16,128]{2,1,0:T(8,128)S(1)}, u32[]{:S(2)}, u32[]{:S(2)}) collective-permute-start(f32[2,16,128]{2,1,0:T(8,128)S(1)} %get-tuple-element.12), channel_id=1, source_target_pairs={{0,1},{1,2},{2,3},{3,4},{4,5},{5,6},{6,7},{7,8},{8,9},{9,10},{10,1... | collective-permute-start | bytes 49160 | tf_op jit(solution)/shard_map/ppermute | solution.py:471
  5.2 5.1 %collective-permute-start.1 = (f32[2,16,128]{2,1,0:T(8,128)S(1)}, f32[2,16,128]{2,1,0:T(8,128)S(1)}, u32[]{:S(2)}, u32[]{:S(2)}) collective-permute-start(f32[2,16,128]{2,1,0:T(8,128)S(1)} %get-tuple-element.11), channel_id=1, source_target_pairs={{1,0},{2,1},{3,2},{4,3},{5,4},{6,5},{7,6},{8,7},{9,8},{10,9},{11,1... | collective-permute-start | bytes 49160 | tf_op jit(solution)/shard_map/ppermute | solution.py:472
  11.3 15.3 %copy-start.7 = (f32[125,125]{1,0:T(8,128)S(1)}, f32[125,125]{1,0:T(8,128)}, u32[]{:S(2)}) copy-start(f32[125,125]{1,0:T(8,128)} %fine_ref.1) | copy-start | bytes 187504
  11.3 47.4 %all-to-all-start = ((f32[32,64,128]{2,1,0:T(8,128)}), f32[32,64,128]{2,1,0:T(8,128)S(1)}, u32[]{:S(2)}, u32[]{:S(2)}) async-start(f32[32,64,128]{2,1,0:T(8,128)} %window.1), calls=%async_computation | async-start | bytes 2097152 | tf_op jit(solution)/shard_map/all_to_all | solution.py:474
  26.5 0.7 copy-start.8
  26.5 0.7 copy-start.9
  27.2 31.5 %copy-start.2 = (bf16[4,256,256]{2,1,0:T(8,128)(2,1)S(1)}, bf16[4,256,256]{2,1,0:T(8,128)(2,1)}, u32[]{:S(2)}) copy-start(bf16[4,256,256]{2,1,0:T(8,128)(2,1)} %constant.42.clone.down_ref) | copy-start | bytes 1572868
  27.2 31.5 %copy-start.3 = (bf16[4,256,256]{2,1,0:T(8,128)(2,1)S(1)}, bf16[4,256,256]{2,1,0:T(8,128)(2,1)}, u32[]{:S(2)}) copy-start(bf16[4,256,256]{2,1,0:T(8,128)(2,1)} %constant.43.clone.up_ref) | copy-start | bytes 1572868
  27.2 31.5 %copy-start.4 = (bf16[256,256]{1,0:T(8,128)(2,1)S(1)}, bf16[256,256]{1,0:T(8,128)(2,1)}, u32[]{:S(2)}) copy-start(bf16[256,256]{1,0:T(8,128)(2,1)} %constant.44.clone.low_ref) | copy-start | bytes 393220
  27.3 31.5 %copy-start.5 = (bf16[256,256]{1,0:T(8,128)(2,1)S(1)}, bf16[256,256]{1,0:T(8,128)(2,1)}, u32[]{:S(2)}) copy-start(bf16[256,256]{1,0:T(8,128)(2,1)} %constant.45.clone.high_ref) | copy-start | bytes 393220
  58.8 30.5 %copy-start = (bf16[2,640,320]{2,1,0:T(8,128)(2,1)S(1)}, bf16[2,640,320]{2,1,0:T(8,128)(2,1)}, u32[]{:S(2)}) copy-start(bf16[2,640,320]{2,1,0:T(8,128)(2,1)} %constant.46.clone.table_ref) | copy-start | bytes 2457604
where the time goes:
time: 90.7 us; the launch traced here: 90.3 us
  Pallas kernels  24.1 us (27%)
  blocking collectives  21.7 us (24%)
  starting transfers between devices  20.8 us (23%)
  waiting for transfers between devices  20.1 us (22%)
  local copies, waits for them, and re-layouts  3.46 us (4%)
    all_to_all x1, blocking collectives, per_device(): lax.all_to_all(result.reshape(parts, 4, LANES), ('gx', 'gy'), 0, 0, tiled...  21.7 us
    all_to_all x1, waiting for transfers between devices, per_device(): recv = lax.all_to_all(chunks, ('gx', 'gy'), 0, 0, tiled=True)  18.7 us
    all_to_all x1, starting transfers between devices, per_device(): recv = lax.all_to_all(chunks, ('gx', 'gy'), 0, 0, tiled=True)  15.2 us
    pallas_call x1, Pallas kernels, inverses(): pl.pallas_call(inverses_body, out_shape=(square, square, square), scratch...  12.8 us
    pallas_call x1, Pallas kernels, cycle(): pl.pallas_call(cycle_body, out_shape=jax.ShapeDtypeStruct((LANES, LANES),...  8.78 us
    ppermute x1, starting transfers between devices, per_device(): lax.ppermute(lines[:, :16], 'gz', [(i + 1, i) for i in range(groups - 1)])  3.64 us
    unnamed x20, local copies, waits for them, and re-layouts  2.69 us
    ppermute x1, starting transfers between devices, per_device(): lax.ppermute(lines[:, count_z - 16:], 'gz', [(i, i + 1) for i in range(gr...  1.92 us
  transfers between devices with their start and end apart: 3, of which 2 were waited for; matrix products, arithmetic and copies ran while one was open for 0% of the time, Pallas kernels for 14%

commit v1 on v0

v1 whole, which is shorter than its diff:
```python
import math

import jax
import jax.numpy as jnp
import numpy as np
from jax import lax
from jax.experimental import pallas as pl
from jax.experimental.pallas import tpu as pltpu
from jax.sharding import PartitionSpec as P

FINE = 5
MID = 3
COARSE = 2
CSWEEPS = 4
RADIUS = 15
HALO = 16
OWN = 4
WINDOW = OWN + 2 * RADIUS
EX = 4
EY = 16
HALF = EY // 2
LANES = 128

f32 = jnp.float32
bf16 = jnp.bfloat16
HIGHEST = lax.Precision.HIGHEST
MIB = 1 << 20


def gll_points(points):
    if points == 5:
        return np.array([-1.0, -math.sqrt(3.0 / 7.0), 0.0, math.sqrt(3.0 / 7.0), 1.0])
    if points == 3:
        return np.array([-1.0, 0.0, 1.0])
    return np.array([-1.0, 1.0])


def lagrange(fine_points, coarse_points):
    fine_nodes = gll_points(fine_points)
    coarse_nodes = gll_points(coarse_points)
    table = np.ones((fine_points, coarse_points))
    for column in range(coarse_points):
        for other in range(coarse_points):
            if other != column:
                table[:, column] *= (fine_nodes - coarse_nodes[other]) / (
                    coarse_nodes[column] - coarse_nodes[other]
                )
    return table


def halves(table):
    table = np.asarray(table, np.float32)
    hi = table.astype(jnp.bfloat16)
    lo = (table - hi.astype(np.float32)).astype(jnp.bfloat16)
    return np.block([[hi, lo], [hi, np.zeros_like(lo)]])


def transfer_tables():
    fine_mid = np.kron(np.kron(lagrange(5, 3), lagrange(5, 3)), lagrange(5, 3))
    mid_coarse = np.kron(np.kron(lagrange(3, 2), lagrange(3, 2)), lagrange(3, 2))
    down, up = [], []
    for place in range(EX):
        table = np.zeros((LANES, LANES))
        table[:125, place * 32 : place * 32 + 27] = fine_mid
        down.append(halves(table))
        up.append(halves(table.T))
    middle = np.zeros((LANES, LANES))
    for place in range(EX):
        middle[place * 32 : place * 32 + 27, place * 32 : place * 32 + 8] = mid_coarse
    return np.stack(down), np.stack(up), halves(middle), halves(middle.T)


def iota(shape, dimension):
    return lax.broadcasted_iota(jnp.int32, shape, dimension)


def three_way(values):
    one = values.astype(bf16)
    rest = values - one.astype(f32)
    two = rest.astype(bf16)
    three = (rest - two.astype(f32)).astype(bf16)
    return jnp.concatenate([one, two, three], axis=0)


def place_of(lane, y):
    i, j, k = lane // (FINE * FINE), (lane // FINE) % FINE, lane % FINE
    return jnp.where(lane < FINE**3, k * LANES + i * 2 * FINE + y * FINE + j, -1)


def pack_body(core_ref, field_ref, scale_ref, own_ref, edge_ref, lines, turned, *, count_z):
    lines[...] = jnp.zeros_like(lines)
    for i in range(FINE):
        lines[i * 2 * FINE : (i + 1) * 2 * FINE, 0 : count_z * FINE] = field_ref[i]
    for part in range(lines.shape[1] // LANES):
        lanes = slice(part * LANES, (part + 1) * LANES)
        turned[lanes, :] = lines[:, lanes].T
    lane = iota((1, 2 * LANES), 1)
    place = place_of(lane % LANES, lane // LANES)
    table = jnp.where(iota((FINE * LANES, 2 * LANES), 0) == place, 1.0, 0.0).astype(bf16)
    values = [turned[pl.ds(k, count_z, stride=FINE), :] for k in range(FINE)]
    nodes = jnp.dot(
        three_way(jnp.concatenate(values, axis=1)), table, preferred_element_type=f32
    )
    nodes = nodes[0:count_z] + nodes[count_z : 2 * count_z] + nodes[2 * count_z : 3 * count_z]
    scale = scale_ref[0].T
    for y in range(2):
        own_ref[y] = nodes[:, y * LANES : (y + 1) * LANES] / scale[:, y : y + 1]
    start = pl.multiple_of(core_ref[0] * (count_z - HALO), HALO)
    for y in range(2):
        edge_ref[y] = own_ref[y, pl.ds(start, HALO), :]


def pack(core, field, scaling):
    count_z = scaling.shape[2]
    width = -(-count_z * FINE // LANES) * LANES

    def body(*refs):
        pack_body(*refs, count_z=count_z)

    vmem = pl.BlockSpec(memory_space=pltpu.VMEM)
    return pl.pallas_call(
        body,
        out_shape=(
            jax.ShapeDtypeStruct((2, count_z, LANES), f32),
            jax.ShapeDtypeStruct((2, HALO, LANES), f32),
        ),
        in_specs=[pl.BlockSpec(memory_space=pltpu.SMEM), vmem, vmem],
        out_specs=(vmem, vmem),
        scratch_shapes=[pltpu.VMEM((LANES, width), f32), pltpu.VMEM((width, LANES), f32)],
        compiler_params=pltpu.CompilerParams(vmem_limit_bytes=8 * MIB),
        name="pack",
    )(core, field, scaling)


def join_body(core_ref, own_ref, halo_ref, mine_ref, give_ref, *, count_z):
    core = core_ref[0]
    own_at = pl.multiple_of((1 - core) * HALO, HALO)
    halo_at = pl.multiple_of(core * count_z, HALO)
    for ref, y in ((mine_ref, core), (give_ref, 1 - core)):
        ref[pl.ds(own_at, count_z), :] = own_ref[y]
        ref[pl.ds(halo_at, HALO), :] = halo_ref[y]


def join(core, own, halo):
    count_z = own.shape[1]

    def body(*refs):
        join_body(*refs, count_z=count_z)

    vmem = pl.BlockSpec(memory_space=pltpu.VMEM)
    line = jax.ShapeDtypeStruct((count_z + HALO, LANES), f32)
    return pl.pallas_call(
        body,
        out_shape=(line, line),
        in_specs=[pl.BlockSpec(memory_space=pltpu.SMEM), vmem, vmem],
        out_specs=(vmem, vmem),
        compiler_params=pltpu.CompilerParams(vmem_limit_bytes=8 * MIB),
        name="join",
    )(core, own, halo)


def window_body(core_ref, mine_ref, other_ref, out_ref, line, *, parts):
    length = mine_ref.shape[0]
    core = core_ref[0]
    line[pl.ds(pl.multiple_of(core * length, HALO), length), :] = mine_ref[...]
    line[pl.ds(pl.multiple_of((1 - core) * length, HALO), length), :] = other_ref[...]
    for part in range(parts):
        start = HALO - RADIUS + OWN * part
        out_ref[part * WINDOW : (part + 1) * WINDOW, :] = line[start : start + WINDOW, :]


def window(core, mine, other, parts):
    def body(*refs):
        window_body(*refs, parts=parts)

    vmem = pl.BlockSpec(memory_space=pltpu.VMEM)
    return pl.pallas_call(
        body,
        out_shape=jax.ShapeDtypeStruct((parts * WINDOW, LANES), f32),
        in_specs=[pl.BlockSpec(memory_space=pltpu.SMEM), vmem, vmem],
        out_specs=vmem,
        scratch_shapes=[pltpu.VMEM((2 * mine.shape[0], LANES), f32)],
        compiler_params=pltpu.CompilerParams(vmem_limit_bytes=8 * MIB),
        name="window",
    )(core, mine, other)


def unpack_body(core_ref, back_ref, scale_ref, out_ref, turned, *, count_z):
    scale = scale_ref[0].T
    base = core_ref[0] * (2 * count_z)
    rows = [
        back_ref[pl.ds(base + y, count_z, stride=2), :] / scale[:, y : y + 1] for y in range(2)
    ]
    table = jnp.concatenate(
        [
            jnp.where(
                iota((LANES, FINE * LANES), 1) == place_of(iota((LANES, 1), 0), y), 1.0, 0.0
            )
            for y in range(2)
        ],
        axis=0,
    ).astype(bf16)
    spread = jnp.dot(
        three_way(jnp.concatenate(rows, axis=1)), table, preferred_element_type=f32
    )
    spread = spread[0:count_z] + spread[count_z : 2 * count_z] + spread[2 * count_z : 3 * count_z]
    for k in range(FINE):
        turned[pl.ds(k, count_z, stride=FINE), :] = spread[:, k * LANES : (k + 1) * LANES]
    lines = [
        turned[part * LANES : (part + 1) * LANES, :].T for part in range(turned.shape[0] // LANES)
    ]
    lines = jnp.concatenate(lines, axis=1)
    for i in range(FINE):
        out_ref[i] = lines[i * 2 * FINE : (i + 1) * 2 * FINE, 0 : count_z * FINE]


def unpack(core, back, scaling, shape):
    count_z = scaling.shape[2]
    width = -(-count_z * FINE // LANES) * LANES

    def body(*refs):
        unpack_body(*refs, count_z=count_z)

    vmem = pl.BlockSpec(memory_space=pltpu.VMEM)
    return pl.pallas_call(
        body,
        out_shape=jax.ShapeDtypeStruct(shape, f32),
        in_specs=[pl.BlockSpec(memory_space=pltpu.SMEM), vmem, vmem],
        out_specs=vmem,
        scratch_shapes=[pltpu.VMEM((width, LANES), f32)],
        compiler_params=pltpu.CompilerParams(vmem_limit_bytes=8 * MIB),
        name="unpack",
    )(core, back, scaling)


def shifted_block(ref, pad, points):
    nodes = points**3
    pad[...] = jnp.zeros((LANES, LANES), f32)
    pad[0:nodes, 0:nodes] = ref[...]
    lane, row = iota((LANES, LANES), 1), iota((LANES, LANES), 0)
    count = jnp.zeros((LANES, LANES), f32)
    for stride in (points * points, points, 1):
        index = (lane // stride) % points
        count = count + jnp.where((index == 0) | (index == points - 1), 0.5, 0.0)
    diagonal = jnp.where(lane < nodes, count, 1.0)
    return pad[...] + jnp.where(lane == row, diagonal, 0.0)


def invert(matrix, panels):
    lane, row = iota((LANES, LANES), 1), iota((LANES, LANES), 0)
    lane16, row16 = iota((16, LANES), 1), iota((16, LANES), 0)
    for panel in range(panels):
        top = panel * 16
        rows = matrix[top : top + 16, :]
        for step in range(16):
            pivot = top + step
            column = rows[:, pivot : pivot + 1]
            scale = 1.0 / rows[step : step + 1, pivot : pivot + 1]
            scaled = jnp.where(lane16[0:1] == pivot, scale, rows[step : step + 1, :] * scale)
            others = jnp.where(lane16 == pivot, 0.0, rows) - column * scaled
            rows = jnp.where(row16 == step, scaled, others)
        stacked = jnp.concatenate([rows] * 8, axis=0)
        inside = (lane >= top) & (lane < top + 16)
        update = jnp.dot(
            jnp.where(inside, matrix, 0.0), stacked, precision=HIGHEST, preferred_element_type=f32
        )
        matrix = jnp.where(
            (row >= top) & (row < top + 16), stacked, jnp.where(inside, 0.0, matrix) - update
        )
    return matrix


def repeated(matrix):
    lane, row = iota((LANES, LANES), 1), iota((LANES, LANES), 0)
    pick = jnp.where((row % 32 == lane) & (lane < 32), 1.0, 0.0)
    put = jnp.where((lane % 32 == row) & (row < 32), 1.0, 0.0)
    tall = jnp.dot(pick, matrix, precision=HIGHEST, preferred_element_type=f32)
    wide = jnp.dot(tall, put, precision=HIGHEST, preferred_element_type=f32)
    return jnp.where(row // 32 == lane // 32, wide, 0.0)


def inverses_body(fine_ref, mid_ref, coarse_ref, fine_out, mid_out, coarse_out, pad):
    coarse = invert(shifted_block(coarse_ref, pad, COARSE), 1)
    mid = invert(shifted_block(mid_ref, pad, MID), 2)
    fine = invert(shifted_block(fine_ref, pad, FINE), 8)
    fine_out[...] = 0.35 * fine
    mid_out[...] = 0.35 * repeated(mid)
    coarse_out[...] = 0.35 * repeated(coarse)


def inverses(block_fine, block_mid, block_coarse):
    square = jax.ShapeDtypeStruct((LANES, LANES), f32)
    return pl.pallas_call(
        inverses_body,
        out_shape=(square, square, square),
        scratch_shapes=[pltpu.VMEM((LANES, LANES), f32)],
        compiler_params=pltpu.CompilerParams(vmem_limit_bytes=8 * MIB),
        cost_estimate=pl.CostEstimate(
            flops=2_000_000_000, bytes_accessed=20_000_000, transcendentals=0
        ),
        name="inverses",
    )(block_fine, block_mid, block_coarse)


def two_way(values):
    hi = values.astype(bf16)
    lo = (values - hi.astype(f32)).astype(bf16)
    return jnp.concatenate([hi, lo], axis=1)


def two_way_table(table):
    hi = table.astype(bf16)
    lo = (table - hi.astype(f32)).astype(bf16)
    return jnp.concatenate(
        [jnp.concatenate([hi, lo], axis=1), jnp.concatenate([hi, jnp.zeros_like(lo)], axis=1)],
        axis=0,
    )


def times(values, table):
    result = jnp.dot(two_way(values), table, preferred_element_type=f32)
    return result[:, 0:LANES] + result[:, LANES : 2 * LANES]


class Faces:
    def __init__(self, points, in_lanes):
        nodes = points**3
        lane, row = iota((EY, LANES), 1), iota((EY, LANES), 0)
        local = lane % 32 if in_lanes else lane
        place = lane // 32
        self.turns = []
        for dimension, stride in enumerate((points * points, points, 1)):
            index = (local // stride) % points
            first = (index == 0) & (local < nodes)
            last = (index == points - 1) & (local < nodes)
            reach = (points - 1) * stride
            if dimension == 0 and in_lanes:
                first, last = first & (place > 0), last & (place < EX - 1)
                reach = reach - 32
            if dimension == 1:
                first, last = first & (row > 0), last & (row < EY - 1)
            self.turns.append((first[None], last[None], (-reach) % LANES, reach % LANES))

    def gather(self, pairs):
        total = None
        for (before, after), (first, last, down, up) in zip(pairs, self.turns):
            part = 0.0
            if after is not None:
                slabs = after.shape[0] // EY
                turned = pltpu.roll(after, up, 1).reshape(slabs, EY, LANES)
                part = jnp.where(last, turned, part)
            if before is not None:
                slabs = before.shape[0] // EY
                turned = pltpu.roll(before, down, 1).reshape(slabs, EY, LANES)
                part = jnp.where(first, turned, part)
            total = part if total is None else total + part
        return total.reshape(-1, LANES)


CHUNK = 8


def cuts(start, stop):
    count = -(-(stop - start) // CHUNK)
    edges = [start + (stop - start) * piece // count for piece in range(count + 1)]
    return list(zip(edges[:-1], edges[1:]))


def flat(values):
    return values.reshape(-1, LANES)


def beside(ref, rows):
    before = jnp.concatenate([ref[rows, HALF - 1 : EY - 1, :], ref[rows, 0:HALF, :]], axis=1)
    after = jnp.concatenate([ref[rows, HALF:EY, :], ref[rows, 1 : HALF + 1, :]], axis=1)
    return flat(before), flat(after)


def cycle_body(
    bounds_ref,
    mine_ref,
    other_ref,
    fine_ref,
    mid_ref,
    coarse_ref,
    down_ref,
    up_ref,
    low_ref,
    high_ref,
    out_ref,
    start,
    ping,
    pong,
    left,
    mid_start,
    mid_ping,
    mid_pong,
    mid_left,
    mask,
):
    fine_faces = Faces(FINE, False)
    mid_faces = Faces(MID, True)
    coarse_faces = Faces(COARSE, True)
    fine_table = two_way_table(fine_ref[...])
    mid_table = two_way_table(mid_ref[...])
    coarse_table = two_way_table(coarse_ref[...])

    slab = iota((WINDOW, EY, LANES), 0)
    mask[...] = jnp.where((slab >= bounds_ref[0]) & (slab < bounds_ref[1]), 1.0, 0.0)
    even_is_mine = bounds_ref[2] == 0

    def at(x, a, b):
        return slice(x * WINDOW + a, x * WINDOW + b)

    def get(ref, rows):
        return flat(ref[rows, :, :])

    def put(ref, rows, values):
        ref[rows, :, :] = values.reshape(-1, EY, LANES)

    def fine_gather(ref, x, a, b):
        return fine_faces.gather(
            (
                (
                    get(ref, at(x - 1, a, b)) if x > 0 else None,
                    get(ref, at(x + 1, a, b)) if x < EX - 1 else None,
                ),
                beside(ref, at(x, a, b)),
                (get(ref, at(x, a - 1, b - 1)), get(ref, at(x, a + 1, b + 1))),
            )
        )

    def fine_sweep(source, target, a, b, keep):
        for x in range(EX):
            for c, d in cuts(a, b):
                rows = at(x, c, d)
                faces = fine_gather(source, x, c, d)
                if keep is not None:
                    put(left, rows, get(left, rows) + keep * faces)
                moved = 0.3 * get(source, rows) + get(start, rows) + times(faces, fine_table)
                put(target, rows, moved * get(mask, at(0, c, d)))

    for x in range(EX):
        for c, d in cuts(0, WINDOW):
            values = []
            for z in range(c, d):
                place = pl.ds(x * HALF * WINDOW + z, HALF, stride=WINDOW)
                mine, other = mine_ref[place, :], other_ref[place, :]
                values.append(jnp.where(even_is_mine, mine, other))
                values.append(jnp.where(even_is_mine, other, mine))
            values = jnp.concatenate(values, axis=0)
            rows = at(x, c, d)
            put(left, rows, 0.027 * values)
            put(start, rows, 2.0 * times(values, fine_table))

    fine_sweep(start, ping, 1, WINDOW - 1, -0.105)
    fine_sweep(ping, pong, 2, WINDOW - 2, -0.35)

    def mid_gather(faces, ref, a, b):
        here = get(ref, at(0, a, b))
        return faces.gather(
            (
                (here, here),
                beside(ref, at(0, a, b)),
                (get(ref, at(0, a - 1, b - 1)), get(ref, at(0, a + 1, b + 1))),
            )
        )

    for c, d in cuts(3, WINDOW - 3):
        total = None
        for x in range(EX):
            rest = get(left, at(x, c, d)) + 0.5 * fine_gather(pong, x, c, d)
            part = times(rest, down_ref[x])
            total = part if total is None else total + part
        rows = at(0, c, d)
        total = total * get(mask, rows)
        put(mid_left, rows, 0.027 * total)
        put(mid_start, rows, 2.0 * times(total, mid_table))

    def mid_sweep(faces, table, base, source, target, margin, keep=None):
        for c, d in cuts(margin, WINDOW - margin):
            rows = at(0, c, d)
            values = mid_gather(faces, source, c, d)
            if keep is not None:
                put(mid_left, rows, get(mid_left, rows) + keep * values)
            moved = 0.3 * get(source, rows) + get(base, rows) + times(values, table)
            put(target, rows, moved * get(mask, rows))

    mid_sweep(mid_faces, mid_table, mid_start, mid_start, mid_ping, 4, -0.105)
    mid_sweep(mid_faces, mid_table, mid_start, mid_ping, mid_pong, 5, -0.35)

    base = ping.at[0:WINDOW]
    even = ping.at[WINDOW : 2 * WINDOW]
    odd = ping.at[2 * WINDOW : 3 * WINDOW]
    for c, d in cuts(6, WINDOW - 6):
        rows = at(0, c, d)
        rest = get(mid_left, rows) + 0.5 * mid_gather(mid_faces, mid_pong, c, d)
        low = times(rest * get(mask, rows), low_ref[...])
        put(base, rows, 2.0 * times(low, coarse_table))
    mid_sweep(coarse_faces, coarse_table, base, base, even, 7)
    mid_sweep(coarse_faces, coarse_table, base, even, odd, 8)
    mid_sweep(coarse_faces, coarse_table, base, odd, even, 9)

    for c, d in cuts(9, WINDOW - 9):
        rows = at(0, c, d)
        put(mid_pong, rows, get(mid_pong, rows) + times(get(even, rows), high_ref[...]))
    mid_sweep(mid_faces, mid_table, mid_start, mid_pong, mid_ping, 10)
    mid_sweep(mid_faces, mid_table, mid_start, mid_ping, mid_pong, 11)
    mid_sweep(mid_faces, mid_table, mid_start, mid_pong, mid_ping, 12)

    lifted = two_way(get(mid_ping, at(0, 12, WINDOW - 12)))
    for x in range(EX):
        rows = at(x, 12, WINDOW - 12)
        added = jnp.dot(lifted, up_ref[x], preferred_element_type=f32)
        added = added[:, 0:LANES] + added[:, LANES : 2 * LANES]
        put(pong, rows, get(pong, rows) + added)
    fine_sweep(pong, ping, 13, WINDOW - 13, None)
    fine_sweep(ping, pong, 14, WINDOW - 14, None)
    fine_sweep(pong, ping, RADIUS, WINDOW - RADIUS, None)

    for x in range(EX):
        for z in range(OWN):
            for y in range(2):
                values = ping[x * WINDOW + RADIUS + z, y * HALF : (y + 1) * HALF, :]
                first = x * HALF * OWN * 2 + z * 2 + y
                out_ref[pl.ds(first, HALF, stride=2 * OWN), :] = values


def cycle(bounds, mine, other, fine, mid, coarse, down, up, low, high):
    big = pltpu.VMEM((EX * WINDOW, EY, LANES), f32)
    small = pltpu.VMEM((WINDOW, EY, LANES), f32)
    vmem = pl.BlockSpec(memory_space=pltpu.VMEM)
    return pl.pallas_call(
        cycle_body,
        out_shape=jax.ShapeDtypeStruct((EX * HALF * 2 * OWN, LANES), f32),
        in_specs=[pl.BlockSpec(memory_space=pltpu.SMEM)] + [vmem] * 9,
        out_specs=vmem,
        scratch_shapes=[big, big, big, big, small, small, small, small, small],
        compiler_params=pltpu.CompilerParams(vmem_limit_bytes=32 * MIB),
        name="cycle",
    )(bounds, mine, other, fine, mid, coarse, down, up, low, high)


def per_device(fine_source_field, scaling, block_fine, block_mid, block_coarse):
    count_z = scaling.shape[2]
    parts = lax.axis_size("gx") * lax.axis_size("gy")
    groups = lax.axis_size("gz")
    down, up, low, high = transfer_tables()
    group = lax.axis_index("gz")
    core = group % 2
    cores = core.astype(jnp.int32).reshape(1)

    own, edge = pack(cores, fine_source_field, scaling)
    ties = [(i, i + 1) for i in range(1, groups - 1, 2)]
    halo = lax.ppermute(edge, "gz", ties + [(j, i) for i, j in ties])
    pairs = [(i, i ^ 1) for i in range(groups)]
    mine, give = join(cores, own, halo)
    other = lax.ppermute(give, "gz", pairs)
    chunks = window(cores, mine, other, parts)
    recv = lax.all_to_all(
        chunks.reshape(parts, WINDOW, LANES), ("gx", "gy"), 0, 0, tiled=True
    ).reshape(parts * WINDOW, LANES)
    fine, mid, coarse = inverses(block_fine, block_mid, block_coarse)
    other = lax.ppermute(recv, "gz", pairs)

    part = lax.axis_index("gx") * lax.axis_size("gy") + lax.axis_index("gy")
    first = (group - core) * count_z + OWN * part - RADIUS
    bounds = jnp.stack(
        [jnp.maximum(0, -first), jnp.minimum(WINDOW, groups * count_z - first), core]
    )
    result = cycle(
        bounds.astype(jnp.int32), recv, other, fine, mid, coarse, down, up, low, high
    )
    back = lax.all_to_all(
        result.reshape(parts, 2 * OWN, LANES), ("gx", "gy"), 0, 0, tiled=True
    ).reshape(parts * 2 * OWN, LANES)
    return unpack(cores, back, scaling, fine_source_field.shape)


def solution(mesh):
    in_specs = (P("gx", "gy", "gz"), P("gx", "gy", "gz"), P(), P(), P())
    out_specs = P("gx", "gy", "gz")
    return jax.shard_map(
        per_device, mesh=mesh, in_specs=in_specs, out_specs=out_specs, check_vma=False
    )
```

time: 90.7 us -> 94.6 us (1.043)
  the two profiles are of different devices: /device:TPU:14 before, /device:TPU:2 now
where the time goes in v1:
time: 94.6 us; the launch traced here: 94.2 us
  blocking collectives  57.1 us (60%)
  Pallas kernels  23.6 us (25%)
  starting transfers between devices  6.73 us (7%)
  waiting for transfers between devices  4.24 us (4%)
  local copies, waits for them, and re-layouts  2.31 us (2%)
    all_to_all x1, blocking collectives, per_device(): lax.all_to_all(chunks.reshape(parts, WINDOW, LANES), ('gx', 'gy'), 0, 0,...  38.8 us
    all_to_all x1, blocking collectives, per_device(): lax.all_to_all(result.reshape(parts, 2 * OWN, LANES), ('gx', 'gy'), 0, 0,...  18.4 us
    pallas_call x1, Pallas kernels, inverses(): pl.pallas_call(inverses_body, out_shape=(square, square, square), scratch...  12.8 us
    pallas_call x1, Pallas kernels, cycle(): pl.pallas_call(cycle_body, out_shape=jax.ShapeDtypeStruct((EX * HALF * 2...  9.3 us
    ppermute x1, waiting for transfers between devices, per_device(): halo = lax.ppermute(edge, 'gz', ties + [(j, i) for i, j in ties])  3.05 us
    ppermute x1, starting transfers between devices, per_device(): halo = lax.ppermute(edge, 'gz', ties + [(j, i) for i, j in ties])  2.9 us
    unnamed x18, local copies, waits for them, and re-layouts  2.22 us
    ppermute x1, starting transfers between devices, per_device(): other = lax.ppermute(recv, 'gz', pairs)  1.92 us
  transfers between devices with their start and end apart: 3, of which 2 were waited for; matrix products, arithmetic and copies ran while one was open for 0% of the time, Pallas kernels for 14%

profile of v1, /device:TPU:2, one launch (start us, length us, event | category | flops | bytes accessed | tf_op | source)
XLA Modules:
  0.0 94.2 jit_solution(2959285409615989217)
XLA Ops:
  0.0 0.0 copy-start.5
  0.0 0.7 copy-done.5
  0.7 0.0 copy-start.4
  0.7 0.9 copy-done.4
  1.6 0.3 pack.1
  1.9 2.9 %collective-permute-start = (f32[2,16,128]{2,1,0:T(8,128)S(1)}, f32[2,16,128]{2,1,0:T(8,128)S(1)}, u32[]{:S(2)}, u32[]{:S(2)}) collective-permute-start(f32[2,16,128]{2,1,0:T(8,128)S(1)} %get-tuple-element.13), channel_id=1, source_target_pairs={{1,2},{3,4},{5,6},{7,8},{9,10},{11,12},{13,14},{2,1},{4,3},{6,5},{... | collective-permute-start | bytes 49160 | tf_op jit(solution)/shard_map/ppermute | solution.py:555
  4.8 3.1 %collective-permute-done.refs_2_ = f32[2,16,128]{2,1,0:T(8,128)S(1)} collective-permute-done((f32[2,16,128]{2,1,0:T(8,128)S(1)}, f32[2,16,128]{2,1,0:T(8,128)S(1)}, u32[]{:S(2)}, u32[]{:S(2)}) %collective-permute-start) | collective-permute-done | bytes 16416 | tf_op jit(solution)/shard_map/ppermute | solution.py:555
  7.9 1.9 %collective-permute-start.1 = (f32[80,128]{1,0:T(8,128)S(1)}, f32[80,128]{1,0:T(8,128)S(1)}, u32[]{:S(2)}, u32[]{:S(2)}) collective-permute-start(f32[80,128]{1,0:T(8,128)S(1)} %get-tuple-element.15), channel_id=1, source_target_pairs={{0,1},{1,0},{2,3},{3,2},{4,5},{5,4},{6,7},{7,6},{8,9},{9,8},{10,11... | collective-permute-start | bytes 122888 | tf_op jit(solution)/shard_map/ppermute | solution.py:558
  9.8 1.2 %collective-permute-done.1.refs_2_ = f32[80,128]{1,0:T(8,128)S(1)} collective-permute-done((f32[80,128]{1,0:T(8,128)S(1)}, f32[80,128]{1,0:T(8,128)S(1)}, u32[]{:S(2)}, u32[]{:S(2)}) %collective-permute-start.1) | collective-permute-done | bytes 40992 | tf_op jit(solution)/shard_map/ppermute | solution.py:558
  11.0 0.1 window.1
  11.1 38.8 %all_to_all.10 = f32[32,34,128]{2,1,0:T(8,128)S(1)} all-to-all(f32[32,34,128]{2,1,0:T(8,128)S(1)} %reshape.16), channel_id=1, replica_groups=mesh['gx'=4,'gy'=8,'gz'=16] {'gx','gy'}, dimensions={0} | all-to-all | bytes 1114112 | tf_op jit(solution)/shard_map/all_to_all | solution.py:560
  49.9 0.0 copy-start.6
  49.9 1.9 %collective-permute-start.2 = (f32[1088,128]{1,0:T(8,128)S(1)}, f32[1088,128]{1,0:T(8,128)S(1)}, u32[]{:S(2)}, u32[]{:S(2)}) collective-permute-start(f32[1088,128]{1,0:T(8,128)S(1)} %reshape.17.mine_ref), channel_id=1, source_target_pairs={{0,1},{1,0},{2,3},{3,2},{4,5},{5,4},{6,7},{7,6},{8,9},{9,8},{10,11... | collective-permute-start | bytes 1671176 | tf_op jit(solution)/shard_map/ppermute | solution.py:564
  51.8 0.0 copy-start.7
  51.9 0.0 copy-start.8
  51.9 0.1 pad_add_fusion.bounds_ref
  52.0 0.0 copy-done.6
  52.0 0.6 copy-done.7
  52.6 0.0 copy-done.8
  52.6 0.0 copy-start
  52.6 0.0 copy-start.1
  52.6 0.0 copy-start.2
  52.6 0.0 copy-start.3
  52.6 12.8 %inverses.1 = (f32[128,128]{1,0:T(8,128)S(1)}, f32[128,128]{1,0:T(8,128)S(1)}, f32[128,128]{1,0:T(8,128)S(1)}) custom-call(f32[125,125]{1,0:T(8,128)S(1)} %copy-done.6, f32[27,27]{1,0:T(8,128)S(1)} %copy-done.7, f32[8,8]{1,0:T(8,128)S(1)} %copy-done.8), custom_call_target="tpu_custom_call" | custom-call | flops 2000000000 | bytes 20000000 | tf_op jit(solution)/shard_map/inverses/pallas_call | solution.py:293
  65.4 0.0 collective-permute-done.2.other_ref
  65.4 0.0 copy-done
  65.4 0.0 copy-done.1
  65.4 0.0 copy-done.2
  65.4 0.0 copy-done.3
  65.4 9.3 %cycle.1 = f32[256,128]{1,0:T(8,128)S(1)} custom-call(s32[3]{0:T(128)S(1)} %pad_add_fusion.bounds_ref, f32[1088,128]{1,0:T(8,128)S(1)} %reshape.17.mine_ref, f32[1088,128]{1,0:T(8,128)S(1)} %collective-permute-done.2.other_ref, f32[128,128]{1,0:T(8,128)S(1)} %get-tuple-element.16.fine_ref, f32[128,128]{1,0:T(8,128)S(1)} %get-tuple-element.17.mid_ref, ...), custom_call_target="tpu_custom_call" | custom-call | tf_op jit(solution)/shard_map/cycle/pallas_call | solution.py:533
  74.7 18.4 %all_to_all.11 = f32[32,8,128]{2,1,0:T(8,128)S(1)} all-to-all(f32[32,8,128]{2,1,0:T(8,128)S(1)} %bitcast.5), channel_id=1, replica_groups=mesh['gx'=4,'gy'=8,'gz'=16] {'gx','gy'}, dimensions={0} | all-to-all | bytes 262144 | tf_op jit(solution)/shard_map/all_to_all | solution.py:574
  93.1 1.1 %unpack.1 = f32[5,10,320]{2,1,0:T(8,128)} custom-call(s32[1]{0:T(128)} %bitcast.refs_0_, f32[256,128]{1,0:T(8,128)S(1)} %bitcast.6, f32[1,2,64]{2,1,0:T(2,128)S(1)} %copy-done.5), custom_call_target="tpu_custom_call" | custom-call | tf_op jit(solution)/shard_map/unpack/pallas_call | solution.py:225
  (3 shorter events, 0.1 us)
Async XLA Ops:
  0.0 0.7 copy-start.5
  0.7 0.9 copy-start.4
  1.9 6.0 %collective-permute-start = (f32[2,16,128]{2,1,0:T(8,128)S(1)}, f32[2,16,128]{2,1,0:T(8,128)S(1)}, u32[]{:S(2)}, u32[]{:S(2)}) collective-permute-start(f32[2,16,128]{2,1,0:T(8,128)S(1)} %get-tuple-element.13), channel_id=1, source_target_pairs={{1,2},{3,4},{5,6},{7,8},{9,10},{11,12},{13,14},{2,1},{4,3},{6,5},{... | collective-permute-start | bytes 49160 | tf_op jit(solution)/shard_map/ppermute | solution.py:555
  7.9 3.1 %collective-permute-start.1 = (f32[80,128]{1,0:T(8,128)S(1)}, f32[80,128]{1,0:T(8,128)S(1)}, u32[]{:S(2)}, u32[]{:S(2)}) collective-permute-start(f32[80,128]{1,0:T(8,128)S(1)} %get-tuple-element.15), channel_id=1, source_target_pairs={{0,1},{1,0},{2,3},{3,2},{4,5},{5,4},{6,7},{7,6},{8,9},{9,8},{10,11... | collective-permute-start | bytes 122888 | tf_op jit(solution)/shard_map/ppermute | solution.py:558
  49.9 2.1 %copy-start.6 = (f32[125,125]{1,0:T(8,128)S(1)}, f32[125,125]{1,0:T(8,128)}, u32[]{:S(2)}) copy-start(f32[125,125]{1,0:T(8,128)} %fine_ref.1) | copy-start | bytes 187504
  49.9 15.5 %collective-permute-start.2 = (f32[1088,128]{1,0:T(8,128)S(1)}, f32[1088,128]{1,0:T(8,128)S(1)}, u32[]{:S(2)}, u32[]{:S(2)}) collective-permute-start(f32[1088,128]{1,0:T(8,128)S(1)} %reshape.17.mine_ref), channel_id=1, source_target_pairs={{0,1},{1,0},{2,3},{3,2},{4,5},{5,4},{6,7},{7,6},{8,9},{9,8},{10,11... | collective-permute-start | bytes 1671176 | tf_op jit(solution)/shard_map/ppermute | solution.py:564
  51.8 0.7 copy-start.7
  51.9 0.7 copy-start.8
  52.6 12.8 %copy-start = (bf16[4,256,256]{2,1,0:T(8,128)(2,1)S(1)}, bf16[4,256,256]{2,1,0:T(8,128)(2,1)}, u32[]{:S(2)}) copy-start(bf16[4,256,256]{2,1,0:T(8,128)(2,1)} %constant.49.clone.down_ref) | copy-start | bytes 1572868
  52.6 12.8 %copy-start.1 = (bf16[4,256,256]{2,1,0:T(8,128)(2,1)S(1)}, bf16[4,256,256]{2,1,0:T(8,128)(2,1)}, u32[]{:S(2)}) copy-start(bf16[4,256,256]{2,1,0:T(8,128)(2,1)} %constant.50.clone.up_ref) | copy-start | bytes 1572868
  52.6 12.8 %copy-start.2 = (bf16[256,256]{1,0:T(8,128)(2,1)S(1)}, bf16[256,256]{1,0:T(8,128)(2,1)}, u32[]{:S(2)}) copy-start(bf16[256,256]{1,0:T(8,128)(2,1)} %constant.51.clone.low_ref) | copy-start | bytes 393220
  52.6 12.8 %copy-start.3 = (bf16[256,256]{1,0:T(8,128)(2,1)S(1)}, bf16[256,256]{1,0:T(8,128)(2,1)}, u32[]{:S(2)}) copy-start(bf16[256,256]{1,0:T(8,128)(2,1)} %constant.52.clone.high_ref) | copy-start | bytes 393220

commit v2 on v1

--- a/solution.py
+++ b/solution.py
@@ -557,10 +557,13 @@
     mine, give = join(cores, own, halo)
     other = lax.ppermute(give, "gz", pairs)
     chunks = window(cores, mine, other, parts)
+    chunks, *matrices = lax.optimization_barrier((chunks, block_fine, block_mid, block_coarse))
     recv = lax.all_to_all(
         chunks.reshape(parts, WINDOW, LANES), ("gx", "gy"), 0, 0, tiled=True
     ).reshape(parts * WINDOW, LANES)
-    fine, mid, coarse = inverses(block_fine, block_mid, block_coarse)
+    recv, fine, mid, coarse = lax.optimization_barrier(
+        (recv, *inverses(*matrices))
+    )
     other = lax.ppermute(recv, "gz", pairs)
 
     part = lax.axis_index("gx") * lax.axis_size("gy") + lax.axis_index("gy")

time: 94.6 us -> 84 us (0.89)
  blocking collectives: 57.1 us -> 18.2 us
  starting transfers between devices: 6.73 us -> 23.1 us
  waiting for transfers between devices: 4.24 us -> 16 us
    all_to_all x1 -> x0, blocking collectives: 38.8 us -> none  [per_device(): lax.all_to_all(chunks.reshape(parts, WINDOW, LANES), ('gx', 'gy'), 0, 0,...]
    all_to_all x0 -> x1, starting transfers between devices: none -> 16.1 us  [per_device(): lax.all_to_all(chunks.reshape(parts, WINDOW, LANES), ('gx', 'gy'), 0, 0,...]
    all_to_all x0 -> x1, waiting for transfers between devices: none -> 10.1 us  [per_device(): lax.all_to_all(chunks.reshape(parts, WINDOW, LANES), ('gx', 'gy'), 0, 0,...]
    ppermute x1, waiting for transfers between devices: 0.01 us -> 1.65 us  [per_device(): other = lax.ppermute(recv, 'gz', pairs)]
  transfers between devices with their start and end apart: 3 -> 4, of which waited for: 2 -> 4; matrix products, arithmetic and copies ran while one was open for 0% -> 0% of each run, Pallas kernels for 14% -> 15%
where the time goes in v2:
time: 84 us; the launch traced here: 83.7 us
  Pallas kernels  23.6 us (28%)
  starting transfers between devices  23.1 us (28%)
  blocking collectives  18.2 us (22%)
  waiting for transfers between devices  16 us (19%)
  local copies, waits for them, and re-layouts  2.55 us (3%)
    all_to_all x1, blocking collectives, per_device(): lax.all_to_all(result.reshape(parts, 2 * OWN, LANES), ('gx', 'gy'), 0, 0,...  18.2 us
    all_to_all x1, starting transfers between devices, per_device(): lax.all_to_all(chunks.reshape(parts, WINDOW, LANES), ('gx', 'gy'), 0, 0,...  16.1 us
    pallas_call x1, Pallas kernels, inverses(): pl.pallas_call(inverses_body, out_shape=(square, square, square), scratch...  12.8 us
    all_to_all x1, waiting for transfers between devices, per_device(): lax.all_to_all(chunks.reshape(parts, WINDOW, LANES), ('gx', 'gy'), 0, 0,...  10.1 us
    pallas_call x1, Pallas kernels, cycle(): pl.pallas_call(cycle_body, out_shape=jax.ShapeDtypeStruct((EX * HALF * 2...  9.25 us
    ppermute x1, waiting for transfers between devices, per_device(): halo = lax.ppermute(edge, 'gz', ties + [(j, i) for i, j in ties])  3.05 us
    ppermute x1, starting transfers between devices, per_device(): halo = lax.ppermute(edge, 'gz', ties + [(j, i) for i, j in ties])  2.9 us
    ppermute x1, starting transfers between devices, per_device(): other = lax.ppermute(recv, 'gz', pairs)  2.23 us
  transfers between devices with their start and end apart: 4, of which 4 were waited for; matrix products, arithmetic and copies ran while one was open for 0% of the time, Pallas kernels for 15%

profile of v2, /device:TPU:2, one launch (start us, length us, event | category | flops | bytes accessed | tf_op | source)
XLA Modules:
  0.0 83.7 jit_solution(11724094862991940840)
XLA Ops:
  0.0 0.0 copy-start.5
  0.0 0.7 copy-done.5
  0.7 0.0 copy-start.4
  0.7 0.9 %copy-done.4 = f32[5,10,320]{2,1,0:T(8,128)S(1)} copy-done((f32[5,10,320]{2,1,0:T(8,128)S(1)}, f32[5,10,320]{2,1,0:T(8,128)}, u32[]{:S(2)}) %copy-start.4) | copy-done | bytes 64024
  1.6 0.3 pack.1
  1.9 2.9 %collective-permute-start = (f32[2,16,128]{2,1,0:T(8,128)S(1)}, f32[2,16,128]{2,1,0:T(8,128)S(1)}, u32[]{:S(2)}, u32[]{:S(2)}) collective-permute-start(f32[2,16,128]{2,1,0:T(8,128)S(1)} %get-tuple-element.21), channel_id=1, source_target_pairs={{1,2},{3,4},{5,6},{7,8},{9,10},{11,12},{13,14},{2,1},{4,3},{6,5},{... | collective-permute-start | bytes 49160 | tf_op jit(solution)/shard_map/ppermute | solution.py:555
  4.8 3.1 %collective-permute-done.refs_2_ = f32[2,16,128]{2,1,0:T(8,128)S(1)} collective-permute-done((f32[2,16,128]{2,1,0:T(8,128)S(1)}, f32[2,16,128]{2,1,0:T(8,128)S(1)}, u32[]{:S(2)}, u32[]{:S(2)}) %collective-permute-start) | collective-permute-done | bytes 16416 | tf_op jit(solution)/shard_map/ppermute | solution.py:555
  7.9 1.9 %collective-permute-start.1 = (f32[80,128]{1,0:T(8,128)S(1)}, f32[80,128]{1,0:T(8,128)S(1)}, u32[]{:S(2)}, u32[]{:S(2)}) collective-permute-start(f32[80,128]{1,0:T(8,128)S(1)} %get-tuple-element.23), channel_id=1, source_target_pairs={{0,1},{1,0},{2,3},{3,2},{4,5},{5,4},{6,7},{7,6},{8,9},{9,8},{10,11... | collective-permute-start | bytes 122888 | tf_op jit(solution)/shard_map/ppermute | solution.py:558
  9.8 1.2 %collective-permute-done.1.refs_2_ = f32[80,128]{1,0:T(8,128)S(1)} collective-permute-done((f32[80,128]{1,0:T(8,128)S(1)}, f32[80,128]{1,0:T(8,128)S(1)}, u32[]{:S(2)}, u32[]{:S(2)}) %collective-permute-start.1) | collective-permute-done | bytes 40992 | tf_op jit(solution)/shard_map/ppermute | solution.py:558
  11.0 0.1 window.1
  11.1 0.9 %reshape.16 = f32[32,34,128]{2,1,0:T(8,128)} reshape(f32[1088,128]{1,0:T(8,128)S(1)} %window.1) | data formatting | bytes 1114112 | tf_op jit(solution)/shard_map/reshape | solution.py:562
  11.9 0.0 copy-start.6
  11.9 0.0 copy-start.7
  11.9 0.0 copy-start.8
  12.0 16.1 %all-to-all-start = ((f32[32,34,128]{2,1,0:T(8,128)}), f32[32,34,128]{2,1,0:T(8,128)S(1)}, u32[]{:S(2)}, u32[]{:S(2)}) async-start(f32[32,34,128]{2,1,0:T(8,128)} %reshape.16), calls=%async_computation | async-start | bytes 1310720 | tf_op jit(solution)/shard_map/all_to_all | solution.py:561
  28.1 0.0 copy-done.6
  28.1 0.0 copy-done.7
  28.1 0.0 copy-done.8
  28.1 0.0 copy-start.3
  28.1 12.8 %inverses.1 = (f32[128,128]{1,0:T(8,128)S(1)}, f32[128,128]{1,0:T(8,128)S(1)}, f32[128,128]{1,0:T(8,128)S(1)}) custom-call(f32[125,125]{1,0:T(8,128)S(1)} %copy-done.6, f32[27,27]{1,0:T(8,128)S(1)} %copy-done.7, f32[8,8]{1,0:T(8,128)S(1)} %copy-done.8), custom_call_target="tpu_custom_call" | custom-call | flops 2000000000 | bytes 20000000 | tf_op jit(solution)/shard_map/inverses/pallas_call | solution.py:293
  40.9 0.0 copy-start
  40.9 0.0 copy-start.1
  40.9 10.1 %all-to-all-done = f32[32,34,128]{2,1,0:T(8,128)S(1)} async-done(((f32[32,34,128]{2,1,0:T(8,128)}), f32[32,34,128]{2,1,0:T(8,128)S(1)}, u32[]{:S(2)}, u32[]{:S(2)}) %all-to-all-start) | async-done | bytes 557088 | tf_op jit(solution)/shard_map/all_to_all | solution.py:561
  51.0 0.0 copy-start.2
  51.1 2.2 %collective-permute-start.2 = (f32[1088,128]{1,0:T(8,128)S(1)}, f32[1088,128]{1,0:T(8,128)S(1)}, u32[]{:S(2)}, u32[]{:S(2)}) collective-permute-start(f32[1088,128]{1,0:T(8,128)S(1)} %reshape.17.mine_ref), channel_id=1, source_target_pairs={{0,1},{1,0},{2,3},{3,2},{4,5},{5,4},{6,7},{7,6},{8,9},{9,8},{10,11... | collective-permute-start | bytes 1671176 | tf_op jit(solution)/shard_map/ppermute | solution.py:567
  53.3 0.1 pad_add_fusion.bounds_ref
  53.4 1.7 %collective-permute-done.2.other_ref = f32[1088,128]{1,0:T(8,128)S(1)} collective-permute-done((f32[1088,128]{1,0:T(8,128)S(1)}, f32[1088,128]{1,0:T(8,128)S(1)}, u32[]{:S(2)}, u32[]{:S(2)}) %collective-permute-start.2) | collective-permute-done | bytes 557088 | tf_op jit(solution)/shard_map/ppermute | solution.py:567
  55.1 0.0 copy-done.3
  55.1 0.0 copy-done
  55.1 0.0 copy-done.1
  55.1 0.0 copy-done.2
  55.1 9.3 %cycle.1 = f32[256,128]{1,0:T(8,128)S(1)} custom-call(s32[3]{0:T(128)S(1)} %pad_add_fusion.bounds_ref, f32[1088,128]{1,0:T(8,128)S(1)} %reshape.17.mine_ref, f32[1088,128]{1,0:T(8,128)S(1)} %collective-permute-done.2.other_ref, f32[128,128]{1,0:T(8,128)S(1)} %get-tuple-element.32.fine_ref, f32[128,128]{1,0:T(8,128)S(1)} %get-tuple-element.33.mid_ref, ...), custom_call_target="tpu_custom_call" | custom-call | tf_op jit(solution)/shard_map/cycle/pallas_call | solution.py:533
  64.4 18.2 %all_to_all.10 = f32[32,8,128]{2,1,0:T(8,128)S(1)} all-to-all(f32[32,8,128]{2,1,0:T(8,128)S(1)} %bitcast.5), channel_id=1, replica_groups=mesh['gx'=4,'gy'=8,'gz'=16] {'gx','gy'}, dimensions={0} | all-to-all | bytes 262144 | tf_op jit(solution)/shard_map/all_to_all | solution.py:577
  82.5 1.1 %unpack.1 = f32[5,10,320]{2,1,0:T(8,128)} custom-call(s32[1]{0:T(128)} %bitcast.refs_0_, f32[256,128]{1,0:T(8,128)S(1)} %bitcast.6, f32[1,2,64]{2,1,0:T(2,128)S(1)} %copy-done.5), custom_call_target="tpu_custom_call" | custom-call | tf_op jit(solution)/shard_map/unpack/pallas_call | solution.py:225
  (2 shorter events, 0.1 us)
Async XLA Ops:
  0.0 0.7 copy-start.5
  0.7 0.9 %copy-start.4 = (f32[5,10,320]{2,1,0:T(8,128)S(1)}, f32[5,10,320]{2,1,0:T(8,128)}, u32[]{:S(2)}) copy-start(f32[5,10,320]{2,1,0:T(8,128)} %refs_1_.1) | copy-start | bytes 192004
  1.9 6.0 %collective-permute-start = (f32[2,16,128]{2,1,0:T(8,128)S(1)}, f32[2,16,128]{2,1,0:T(8,128)S(1)}, u32[]{:S(2)}, u32[]{:S(2)}) collective-permute-start(f32[2,16,128]{2,1,0:T(8,128)S(1)} %get-tuple-element.21), channel_id=1, source_target_pairs={{1,2},{3,4},{5,6},{7,8},{9,10},{11,12},{13,14},{2,1},{4,3},{6,5},{... | collective-permute-start | bytes 49160 | tf_op jit(solution)/shard_map/ppermute | solution.py:555
  7.9 3.1 %collective-permute-start.1 = (f32[80,128]{1,0:T(8,128)S(1)}, f32[80,128]{1,0:T(8,128)S(1)}, u32[]{:S(2)}, u32[]{:S(2)}) collective-permute-start(f32[80,128]{1,0:T(8,128)S(1)} %get-tuple-element.23), channel_id=1, source_target_pairs={{0,1},{1,0},{2,3},{3,2},{4,5},{5,4},{6,7},{7,6},{8,9},{9,8},{10,11... | collective-permute-start | bytes 122888 | tf_op jit(solution)/shard_map/ppermute | solution.py:558
  11.9 16.1 %copy-start.6 = (f32[125,125]{1,0:T(8,128)S(1)}, f32[125,125]{1,0:T(8,128)}, u32[]{:S(2)}) copy-start(f32[125,125]{1,0:T(8,128)} %fine_ref) | copy-start | bytes 187504
  11.9 16.1 %copy-start.7 = (f32[27,27]{1,0:T(8,128)S(1)}, f32[27,27]{1,0:T(8,128)}, u32[]{:S(2)}) copy-start(f32[27,27]{1,0:T(8,128)} %mid_ref) | copy-start | bytes 8752
  11.9 16.1 %copy-start.8 = (f32[8,8]{1,0:T(8,128)S(1)}, f32[8,8]{1,0:T(8,128)}, u32[]{:S(2)}) copy-start(f32[8,8]{1,0:T(8,128)} %coarse_ref) | copy-start | bytes 772
  12.0 39.1 %all-to-all-start = ((f32[32,34,128]{2,1,0:T(8,128)}), f32[32,34,128]{2,1,0:T(8,128)S(1)}, u32[]{:S(2)}, u32[]{:S(2)}) async-start(f32[32,34,128]{2,1,0:T(8,128)} %reshape.16), calls=%async_computation | async-start | bytes 1310720 | tf_op jit(solution)/shard_map/all_to_all | solution.py:561
  28.1 27.0 %copy-start.3 = (bf16[256,256]{1,0:T(8,128)(2,1)S(1)}, bf16[256,256]{1,0:T(8,128)(2,1)}, u32[]{:S(2)}) copy-start(bf16[256,256]{1,0:T(8,128)(2,1)} %constant.51.clone.low_ref) | copy-start | bytes 393220
  40.9 14.2 %copy-start = (bf16[4,256,256]{2,1,0:T(8,128)(2,1)S(1)}, bf16[4,256,256]{2,1,0:T(8,128)(2,1)}, u32[]{:S(2)}) copy-start(bf16[4,256,256]{2,1,0:T(8,128)(2,1)} %constant.50.clone.up_ref) | copy-start | bytes 1572868
  40.9 14.2 %copy-start.1 = (bf16[4,256,256]{2,1,0:T(8,128)(2,1)S(1)}, bf16[4,256,256]{2,1,0:T(8,128)(2,1)}, u32[]{:S(2)}) copy-start(bf16[4,256,256]{2,1,0:T(8,128)(2,1)} %constant.49.clone.down_ref) | copy-start | bytes 1572868
  51.0 4.0 %copy-start.2 = (bf16[256,256]{1,0:T(8,128)(2,1)S(1)}, bf16[256,256]{1,0:T(8,128)(2,1)}, u32[]{:S(2)}) copy-start(bf16[256,256]{1,0:T(8,128)(2,1)} %constant.52.clone.high_ref) | copy-start | bytes 393220
  51.1 4.0 %collective-permute-start.2 = (f32[1088,128]{1,0:T(8,128)S(1)}, f32[1088,128]{1,0:T(8,128)S(1)}, u32[]{:S(2)}, u32[]{:S(2)}) collective-permute-start(f32[1088,128]{1,0:T(8,128)S(1)} %reshape.17.mine_ref), channel_id=1, source_target_pairs={{0,1},{1,0},{2,3},{3,2},{4,5},{5,4},{6,7},{7,6},{8,9},{9,8},{10,11... | collective-permute-start | bytes 1671176 | tf_op jit(solution)/shard_map/ppermute | solution.py:567

commit v3 on v2

--- a/solution.py
+++ b/solution.py
@@ -67,7 +67,9 @@
     middle = np.zeros((LANES, LANES))
     for place in range(EX):
         middle[place * 32 : place * 32 + 27, place * 32 : place * 32 + 8] = mid_coarse
-    return np.stack(down), np.stack(up), halves(middle), halves(middle.T)
+    low = [halves(0.027 * middle)]
+    low += [halves(0.5 * np.dot(move, middle)) for move in exchanges(MID, True)]
+    return np.stack(down), np.stack(up), np.stack(low), halves(middle.T)
 
 
 def iota(shape, dimension):
@@ -279,17 +281,28 @@
     return jnp.where(row // 32 == lane // 32, wide, 0.0)
 
 
-def inverses_body(fine_ref, mid_ref, coarse_ref, fine_out, mid_out, coarse_out, pad):
+def inverses_body(moves_ref, fine_ref, mid_ref, coarse_ref, fine_out, mid_out, coarse_out, pad):
     coarse = invert(shifted_block(coarse_ref, pad, COARSE), 1)
     mid = invert(shifted_block(mid_ref, pad, MID), 2)
     fine = invert(shifted_block(fine_ref, pad, FINE), 8)
-    fine_out[...] = 0.35 * fine
-    mid_out[...] = 0.35 * repeated(mid)
-    coarse_out[...] = 0.35 * repeated(coarse)
+    levels = ((fine, fine_out), (repeated(mid), mid_out), (repeated(coarse), coarse_out))
+    for level, (inverse, out) in enumerate(levels):
+        inverse = 0.35 * inverse
+        out[0] = two_way_table(inverse)
+        for dimension in range(3):
+            moved = jnp.dot(
+                moves_ref[3 * level + dimension].astype(f32),
+                inverse,
+                precision=HIGHEST,
+                preferred_element_type=f32,
+            )
+            out[1 + dimension] = two_way_table(moved)
 
 
 def inverses(block_fine, block_mid, block_coarse):
-    square = jax.ShapeDtypeStruct((LANES, LANES), f32)
+    square = jax.ShapeDtypeStruct((4, 2 * LANES, 2 * LANES), bf16)
+    moves = exchanges(FINE, False) + exchanges(MID, True) + exchanges(COARSE, True)
+    moves = np.stack(moves).astype(jnp.bfloat16)
     return pl.pallas_call(
         inverses_body,
         out_shape=(square, square, square),
@@ -299,7 +312,7 @@
             flops=2_000_000_000, bytes_accessed=20_000_000, transcendentals=0
         ),
         name="inverses",
-    )(block_fine, block_mid, block_coarse)
+    )(moves, block_fine, block_mid, block_coarse)
 
 
 def two_way(values):
@@ -317,47 +330,76 @@
     )
 
 
-def times(values, table):
-    result = jnp.dot(two_way(values), table, preferred_element_type=f32)
+def times(values, *tables):
+    values = jnp.concatenate([two_way(value) for value in values], axis=1)
+    result = jnp.dot(values, jnp.concatenate(tables, axis=0), preferred_element_type=f32)
     return result[:, 0:LANES] + result[:, LANES : 2 * LANES]
+
+
+def exchanges(points, in_lanes):
+    nodes = points**3
+    tables = []
+    for dimension, stride in enumerate((points * points, points, 1)):
+        table = np.zeros((LANES, LANES), np.float32)
+        for place in range(EX if in_lanes else 1):
+            for node in range(nodes):
+                index = (node // stride) % points
+                for end, step in ((0, -1), (points - 1, 1)):
+                    if index != end:
+                        continue
+                    source = place * 32 + node - step * (points - 1) * stride
+                    if dimension == 0 and in_lanes:
+                        if not 0 <= place + step < EX:
+                            continue
+                        source += step * 32
+                    table[source, place * 32 + node] = 1.0
+        tables.append(table)
+    return tables
 
 
 class Faces:
     def __init__(self, points, in_lanes):
-        nodes = points**3
         lane, row = iota((EY, LANES), 1), iota((EY, LANES), 0)
         local = lane % 32 if in_lanes else lane
-        place = lane // 32
-        self.turns = []
+        self.masks = []
         for dimension, stride in enumerate((points * points, points, 1)):
             index = (local // stride) % points
-            first = (index == 0) & (local < nodes)
-            last = (index == points - 1) & (local < nodes)
-            reach = (points - 1) * stride
-            if dimension == 0 and in_lanes:
-                first, last = first & (place > 0), last & (place < EX - 1)
-                reach = reach - 32
+            first, last = index == 0, index == points - 1
             if dimension == 1:
-                first, last = first & (row > 0), last & (row < EY - 1)
-            self.turns.append((first[None], last[None], (-reach) % LANES, reach % LANES))
-
-    def gather(self, pairs):
-        total = None
-        for (before, after), (first, last, down, up) in zip(pairs, self.turns):
-            part = 0.0
-            if after is not None:
-                slabs = after.shape[0] // EY
-                turned = pltpu.roll(after, up, 1).reshape(slabs, EY, LANES)
-                part = jnp.where(last, turned, part)
-            if before is not None:
-                slabs = before.shape[0] // EY
-                turned = pltpu.roll(before, down, 1).reshape(slabs, EY, LANES)
-                part = jnp.where(first, turned, part)
-            total = part if total is None else total + part
-        return total.reshape(-1, LANES)
-
-
-CHUNK = 8
+                self.masks.append((last & (row > 0), first & (row < EY - 1)))
+            else:
+                self.masks.append((last, first))
+
+    def moved(self, dimension, faces):
+        reach = (FINE - 1) * FINE ** (2 - dimension)
+        lane = iota((1, LANES), 1)
+        index = (lane // FINE ** (2 - dimension)) % FINE
+        node = lane < FINE**3
+        order = jnp.where((index == 0) & node, lane + reach, LANES - 1)
+        order = jnp.where((index == FINE - 1) & node, lane - reach, order)
+        turned = jnp.take_along_axis(
+            faces, jnp.broadcast_to(order, faces.shape), axis=1, mode="promise_in_bounds"
+        )
+        return jnp.where(order < LANES - 1, turned, 0.0)
+
+    def select(self, dimension, before, after):
+        from_before, from_after = self.masks[dimension]
+        if before is None:
+            before, after = 0.0, flat_slabs(after)
+        elif after is None:
+            before, after = flat_slabs(before), 0.0
+        else:
+            before, after = flat_slabs(before), flat_slabs(after)
+        if dimension == 1:
+            after = jnp.where(from_after[None], after, 0.0)
+        return flat(jnp.where(from_before[None], before, after))
+
+
+def flat_slabs(values):
+    return values.reshape(-1, EY, LANES)
+
+
+CHUNK = 16
 
 
 def cuts(start, stop):
@@ -392,18 +434,26 @@
     ping,
     pong,
     left,
+    left_x,
+    left_y,
+    left_z,
     mid_start,
     mid_ping,
     mid_pong,
     mid_left,
+    mid_left_x,
+    mid_left_y,
+    mid_left_z,
     mask,
 ):
+    lefts = (left_x, left_y, left_z)
+    mid_lefts = (mid_left_x, mid_left_y, mid_left_z)
     fine_faces = Faces(FINE, False)
     mid_faces = Faces(MID, True)
     coarse_faces = Faces(COARSE, True)
-    fine_table = two_way_table(fine_ref[...])
-    mid_table = two_way_table(mid_ref[...])
-    coarse_table = two_way_table(coarse_ref[...])
+    fine_table, *fine_tables = [fine_ref[i] for i in range(4)]
+    mid_table, *mid_tables = [mid_ref[i] for i in range(4)]
+    coarse_table, *coarse_tables = [coarse_ref[i] for i in range(4)]
 
     slab = iota((WINDOW, EY, LANES), 0)
     mask[...] = jnp.where((slab >= bounds_ref[0]) & (slab < bounds_ref[1]), 1.0, 0.0)
@@ -419,15 +469,14 @@
         ref[rows, :, :] = values.reshape(-1, EY, LANES)
 
     def fine_gather(ref, x, a, b):
-        return fine_faces.gather(
-            (
-                (
-                    get(ref, at(x - 1, a, b)) if x > 0 else None,
-                    get(ref, at(x + 1, a, b)) if x < EX - 1 else None,
-                ),
-                beside(ref, at(x, a, b)),
-                (get(ref, at(x, a - 1, b - 1)), get(ref, at(x, a + 1, b + 1))),
-            )
+        return (
+            fine_faces.select(
+                0,
+                get(ref, at(x - 1, a, b)) if x > 0 else None,
+                get(ref, at(x + 1, a, b)) if x < EX - 1 else None,
+            ),
+            fine_faces.select(1, *beside(ref, at(x, a, b))),
+            fine_faces.select(2, get(ref, at(x, a - 1, b - 1)), get(ref, at(x, a + 1, b + 1))),
         )
 
     def fine_sweep(source, target, a, b, keep):
@@ -436,8 +485,12 @@
                 rows = at(x, c, d)
                 faces = fine_gather(source, x, c, d)
                 if keep is not None:
-                    put(left, rows, get(left, rows) + keep * faces)
-                moved = 0.3 * get(source, rows) + get(start, rows) + times(faces, fine_table)
+                    for ref, face in zip(lefts, faces):
+                        if keep[0]:
+                            put(ref, rows, keep[1] * face)
+                        else:
+                            put(ref, rows, get(ref, rows) + keep[1] * face)
+                moved = 0.3 * get(source, rows) + get(start, rows) + times(faces, *fine_tables)
                 put(target, rows, moved * get(mask, at(0, c, d)))
 
     for x in range(EX):
@@ -450,63 +503,70 @@
                 values.append(jnp.where(even_is_mine, other, mine))
             values = jnp.concatenate(values, axis=0)
             rows = at(x, c, d)
-            put(left, rows, 0.027 * values)
-            put(start, rows, 2.0 * times(values, fine_table))
-
-    fine_sweep(start, ping, 1, WINDOW - 1, -0.105)
-    fine_sweep(ping, pong, 2, WINDOW - 2, -0.35)
+            put(left, rows, values)
+            put(start, rows, 2.0 * times((values,), fine_table))
+
+    fine_sweep(start, ping, 1, WINDOW - 1, (True, -0.21))
+    fine_sweep(ping, pong, 2, WINDOW - 2, (False, -0.7))
 
     def mid_gather(faces, ref, a, b):
         here = get(ref, at(0, a, b))
-        return faces.gather(
-            (
-                (here, here),
-                beside(ref, at(0, a, b)),
-                (get(ref, at(0, a - 1, b - 1)), get(ref, at(0, a + 1, b + 1))),
-            )
+        return (
+            here,
+            faces.select(1, *beside(ref, at(0, a, b))),
+            faces.select(2, get(ref, at(0, a - 1, b - 1)), get(ref, at(0, a + 1, b + 1))),
         )
 
     for c, d in cuts(3, WINDOW - 3):
-        total = None
+        values = []
         for x in range(EX):
-            rest = get(left, at(x, c, d)) + 0.5 * fine_gather(pong, x, c, d)
-            part = times(rest, down_ref[x])
-            total = part if total is None else total + part
+            rest = 0.027 * get(left, at(x, c, d))
+            for dimension, face in enumerate(fine_gather(pong, x, c, d)):
+                face = 0.5 * (get(lefts[dimension], at(x, c, d)) + face)
+                rest = rest + fine_faces.moved(dimension, face)
+            values.append(rest)
+        tables = [down_ref[x] for x in range(EX)]
         rows = at(0, c, d)
-        total = total * get(mask, rows)
-        put(mid_left, rows, 0.027 * total)
-        put(mid_start, rows, 2.0 * times(total, mid_table))
-
-    def mid_sweep(faces, table, base, source, target, margin, keep=None):
+        total = times(values, *tables) * get(mask, rows)
+        put(mid_left, rows, total)
+        put(mid_start, rows, 2.0 * times((total,), mid_table))
+
+    def mid_sweep(faces, tables, base, source, target, margin, keep=None):
         for c, d in cuts(margin, WINDOW - margin):
             rows = at(0, c, d)
             values = mid_gather(faces, source, c, d)
             if keep is not None:
-                put(mid_left, rows, get(mid_left, rows) + keep * values)
-            moved = 0.3 * get(source, rows) + get(base, rows) + times(values, table)
+                for ref, face in zip(mid_lefts, values):
+                    if keep[0]:
+                        put(ref, rows, keep[1] * face)
+                    else:
+                        put(ref, rows, get(ref, rows) + keep[1] * face)
+            moved = 0.3 * get(source, rows) + get(base, rows) + times(values, *tables)
             put(target, rows, moved * get(mask, rows))
 
-    mid_sweep(mid_faces, mid_table, mid_start, mid_start, mid_ping, 4, -0.105)
-    mid_sweep(mid_faces, mid_table, mid_start, mid_ping, mid_pong, 5, -0.35)
+    mid_sweep(mid_faces, mid_tables, mid_start, mid_start, mid_ping, 4, (True, -0.21))
+    mid_sweep(mid_faces, mid_tables, mid_start, mid_ping, mid_pong, 5, (False, -0.7))
 
     base = ping.at[0:WINDOW]
     even = ping.at[WINDOW : 2 * WINDOW]
     odd = ping.at[2 * WINDOW : 3 * WINDOW]
     for c, d in cuts(6, WINDOW - 6):
         rows = at(0, c, d)
-        rest = get(mid_left, rows) + 0.5 * mid_gather(mid_faces, mid_pong, c, d)
-        low = times(rest * get(mask, rows), low_ref[...])
-        put(base, rows, 2.0 * times(low, coarse_table))
-    mid_sweep(coarse_faces, coarse_table, base, base, even, 7)
-    mid_sweep(coarse_faces, coarse_table, base, even, odd, 8)
-    mid_sweep(coarse_faces, coarse_table, base, odd, even, 9)
+        values = [get(mid_left, rows)]
+        for ref, face in zip(mid_lefts, mid_gather(mid_faces, mid_pong, c, d)):
+            values.append(get(ref, rows) + face)
+        low = times(values, *[low_ref[i] for i in range(4)]) * get(mask, rows)
+        put(base, rows, 2.0 * times((low,), coarse_table))
+    mid_sweep(coarse_faces, coarse_tables, base, base, even, 7)
+    mid_sweep(coarse_faces, coarse_tables, base, even, odd, 8)
+    mid_sweep(coarse_faces, coarse_tables, base, odd, even, 9)
 
     for c, d in cuts(9, WINDOW - 9):
         rows = at(0, c, d)
-        put(mid_pong, rows, get(mid_pong, rows) + times(get(even, rows), high_ref[...]))
-    mid_sweep(mid_faces, mid_table, mid_start, mid_pong, mid_ping, 10)
-    mid_sweep(mid_faces, mid_table, mid_start, mid_ping, mid_pong, 11)
-    mid_sweep(mid_faces, mid_table, mid_start, mid_pong, mid_ping, 12)
+        put(mid_pong, rows, get(mid_pong, rows) + times((get(even, rows),), high_ref[...]))
+    mid_sweep(mid_faces, mid_tables, mid_start, mid_pong, mid_ping, 10)
+    mid_sweep(mid_faces, mid_tables, mid_start, mid_ping, mid_pong, 11)
+    mid_sweep(mid_faces, mid_tables, mid_start, mid_pong, mid_ping, 12)
 
     lifted = two_way(get(mid_ping, at(0, 12, WINDOW - 12)))
     for x in range(EX):
@@ -535,7 +595,7 @@
         out_shape=jax.ShapeDtypeStruct((EX * HALF * 2 * OWN, LANES), f32),
         in_specs=[pl.BlockSpec(memory_space=pltpu.SMEM)] + [vmem] * 9,
         out_specs=vmem,
-        scratch_shapes=[big, big, big, big, small, small, small, small, small],
+        scratch_shapes=[big] * 7 + [small] * 8,
         compiler_params=pltpu.CompilerParams(vmem_limit_bytes=32 * MIB),
         name="cycle",
     )(bounds, mine, other, fine, mid, coarse, down, up, low, high)
@@ -559,7 +619,7 @@
     chunks = window(cores, mine, other, parts)
     chunks, *matrices = lax.optimization_barrier((chunks, block_fine, block_mid, block_coarse))
     recv = lax.all_to_all(
-        chunks.reshape(parts, WINDOW, LANES), ("gx", "gy"), 0, 0, tiled=True
+        chunks.reshape(parts * WINDOW // 2, 2, LANES), ("gx", "gy"), 0, 0, tiled=True
     ).reshape(parts * WINDOW, LANES)
     recv, fine, mid, coarse = lax.optimization_barrier(
         (recv, *inverses(*matrices))

time: 84 us -> 84 us (level)
  waiting for transfers between devices: 16 us -> 10.7 us
  local copies, waits for them, and re-layouts: 2.55 us -> 6.22 us
  blocking collectives: 18.2 us -> 20.1 us
    all_to_all x1, waiting for transfers between devices: 10.1 us -> 4.67 us  [per_device(): lax.all_to_all(chunks.reshape(parts * WINDOW // 2, 2, LANES), ('gx', 'gy'...]
    unnamed x18 -> x28, local copies, waits for them, and re-layouts: 1.61 us -> 6.22 us
    all_to_all x1, blocking collectives: 18.2 us -> 20.1 us  [per_device(): lax.all_to_all(result.reshape(parts, 2 * OWN, LANES), ('gx', 'gy'), 0, 0,...]
    pallas_call x1, Pallas kernels: 9.25 us -> 7.82 us  [cycle(): pl.pallas_call(cycle_body, out_shape=jax.ShapeDtypeStruct((EX * HALF * 2...]
    reshape x2 -> x0, local copies, waits for them, and re-layouts: 0.93 us -> none  [the longest x1 0.89 us: per_device(): chunks.reshape(parts, WINDOW, LANES)]
  transfers between devices with their start and end apart: 4 -> 4, of which waited for: 4 -> 4; matrix products, arithmetic and copies ran while one was open for 0% -> 0% of each run, Pallas kernels for 15% -> 16%
where the time goes in v3:
time: 84 us; the launch traced here: 83.5 us
  Pallas kernels  23.4 us (28%)
  starting transfers between devices  22.8 us (27%)
  blocking collectives  20.1 us (24%)
  waiting for transfers between devices  10.7 us (13%)
  local copies, waits for them, and re-layouts  6.22 us (7%)
    all_to_all x1, blocking collectives, per_device(): lax.all_to_all(result.reshape(parts, 2 * OWN, LANES), ('gx', 'gy'), 0, 0,...  20.1 us
    all_to_all x1, starting transfers between devices, per_device(): lax.all_to_all(chunks.reshape(parts * WINDOW // 2, 2, LANES), ('gx', 'gy'...  16.1 us
    pallas_call x1, Pallas kernels, inverses(): pl.pallas_call(inverses_body, out_shape=(square, square, square), scratch...  13.2 us
    pallas_call x1, Pallas kernels, cycle(): pl.pallas_call(cycle_body, out_shape=jax.ShapeDtypeStruct((EX * HALF * 2...  7.82 us
    unnamed x28, local copies, waits for them, and re-layouts  6.22 us
    all_to_all x1, waiting for transfers between devices, per_device(): lax.all_to_all(chunks.reshape(parts * WINDOW // 2, 2, LANES), ('gx', 'gy'...  4.67 us
    ppermute x1, waiting for transfers between devices, per_device(): halo = lax.ppermute(edge, 'gz', ties + [(j, i) for i, j in ties])  3.05 us
    ppermute x1, starting transfers between devices, per_device(): halo = lax.ppermute(edge, 'gz', ties + [(j, i) for i, j in ties])  2.9 us
  transfers between devices with their start and end apart: 4, of which 4 were waited for; matrix products, arithmetic and copies ran while one was open for 0% of the time, Pallas kernels for 16%

profile of v3, /device:TPU:2, one launch (start us, length us, event | category | flops | bytes accessed | tf_op | source)
XLA Modules:
  0.0 83.5 jit_solution(4917037837809191257)
XLA Ops:
  0.0 0.0 copy-start.9
  0.0 0.7 copy-done.9
  0.7 0.0 copy-start.8
  0.7 0.9 %copy-done.8 = f32[5,10,320]{2,1,0:T(8,128)S(1)} copy-done((f32[5,10,320]{2,1,0:T(8,128)S(1)}, f32[5,10,320]{2,1,0:T(8,128)}, u32[]{:S(2)}) %copy-start.8) | copy-done | bytes 64024
  1.6 0.3 pack.1
  1.9 2.9 %collective-permute-start = (f32[2,16,128]{2,1,0:T(8,128)S(1)}, f32[2,16,128]{2,1,0:T(8,128)S(1)}, u32[]{:S(2)}, u32[]{:S(2)}) collective-permute-start(f32[2,16,128]{2,1,0:T(8,128)S(1)} %get-tuple-element.21), channel_id=1, source_target_pairs={{1,2},{3,4},{5,6},{7,8},{9,10},{11,12},{13,14},{2,1},{4,3},{6,5},{... | collective-permute-start | bytes 49160 | tf_op jit(solution)/shard_map/ppermute | solution.py:615
  4.8 3.1 %collective-permute-done.refs_2_ = f32[2,16,128]{2,1,0:T(8,128)S(1)} collective-permute-done((f32[2,16,128]{2,1,0:T(8,128)S(1)}, f32[2,16,128]{2,1,0:T(8,128)S(1)}, u32[]{:S(2)}, u32[]{:S(2)}) %collective-permute-start) | collective-permute-done | bytes 16416 | tf_op jit(solution)/shard_map/ppermute | solution.py:615
  7.9 1.9 %collective-permute-start.1 = (f32[80,128]{1,0:T(8,128)S(1)}, f32[80,128]{1,0:T(8,128)S(1)}, u32[]{:S(2)}, u32[]{:S(2)}) collective-permute-start(f32[80,128]{1,0:T(8,128)S(1)} %get-tuple-element.23), channel_id=1, source_target_pairs={{0,1},{1,0},{2,3},{3,2},{4,5},{5,4},{6,7},{7,6},{8,9},{9,8},{10,11... | collective-permute-start | bytes 122888 | tf_op jit(solution)/shard_map/ppermute | solution.py:618
  9.8 1.2 %collective-permute-done.1.refs_2_ = f32[80,128]{1,0:T(8,128)S(1)} collective-permute-done((f32[80,128]{1,0:T(8,128)S(1)}, f32[80,128]{1,0:T(8,128)S(1)}, u32[]{:S(2)}, u32[]{:S(2)}) %collective-permute-start.1) | collective-permute-done | bytes 40992 | tf_op jit(solution)/shard_map/ppermute | solution.py:618
  11.0 0.9 %window.1 = f32[1088,128]{1,0:T(8,128)} custom-call(s32[1]{0:T(128)} %bitcast.refs_0_, f32[80,128]{1,0:T(8,128)S(1)} %get-tuple-element.22.refs_1_, f32[80,128]{1,0:T(8,128)S(1)} %collective-permute-done.1.refs_2_), custom_call_target="tpu_custom_call" | custom-call | tf_op jit(solution)/shard_map/window/pallas_call | solution.py:179
  11.9 0.0 copy-start.10
  11.9 0.0 copy-start.11
  11.9 0.0 copy-start.12
  11.9 16.1 %all-to-all-start = ((f32[544,2,128]{2,1,0:T(2,128)}), f32[544,2,128]{2,1,0:T(2,128)S(1)}, u32[]{:S(2)}, u32[]{:S(2)}) async-start(f32[544,2,128]{2,1,0:T(2,128)} %bitcast.3), calls=%async_computation | async-start | bytes 1114112 | tf_op jit(solution)/shard_map/all_to_all | solution.py:621
  28.0 0.0 copy-done.10
  28.0 0.0 copy-done.11
  28.0 0.0 copy-done.12
  28.0 0.0 copy-start.13
  28.0 1.0 %copy-done.13 = bf16[9,128,128]{2,1,0:T(8,128)(2,1)S(1)} copy-done((bf16[9,128,128]{2,1,0:T(8,128)(2,1)S(1)}, bf16[9,128,128]{2,1,0:T(8,128)(2,1)}, u32[]{:S(2)}) %copy-start.13) | copy-done | bytes 294936
  29.0 0.0 copy-start
  29.0 0.0 copy-start.1
  29.0 0.0 copy-start.2
  29.0 0.0 copy-start.7
  29.0 13.2 %inverses.1 = (bf16[4,256,256]{2,1,0:T(8,128)(2,1)S(1)}, bf16[4,256,256]{2,1,0:T(8,128)(2,1)S(1)}, bf16[4,256,256]{2,1,0:T(8,128)(2,1)S(1)}) custom-call(bf16[9,128,128]{2,1,0:T(8,128)(2,1)S(1)} %copy-done.13, f32[125,125]{1,0:T(8,128)S(1)} %copy-done.10, f32[27,27]{1,0:T(8,128)S(1)} %copy-done.11, f32[8,8]{1,0:T(8,128)S(1)} %copy-done.12), custom_call_target="tpu_custom_call" | custom-call | flops 2000000000 | bytes 20000000 | tf_op jit(solution)/shard_map/inverses/pallas_call | solution.py:306
  42.2 0.0 copy-start.3
  42.2 0.8 copy-done.3
  43.0 0.0 copy-start.5
  43.0 0.8 copy-done.5
  43.8 4.7 %all-to-all-done = f32[544,2,128]{2,1,0:T(2,128)S(1)} async-done(((f32[544,2,128]{2,1,0:T(2,128)}), f32[544,2,128]{2,1,0:T(2,128)S(1)}, u32[]{:S(2)}, u32[]{:S(2)}) %all-to-all-start) | async-done | bytes 557088 | tf_op jit(solution)/shard_map/all_to_all | solution.py:621
  48.5 1.9 %collective-permute-start.2 = (f32[1088,128]{1,0:T(8,128)S(1)}, f32[1088,128]{1,0:T(8,128)S(1)}, u32[]{:S(2)}, u32[]{:S(2)}) collective-permute-start(f32[1088,128]{1,0:T(8,128)S(1)} %bitcast.7), channel_id=1, source_target_pairs={{0,1},{1,0},{2,3},{3,2},{4,5},{5,4},{6,7},{7,6},{8,9},{9,8},{10,11... | collective-permute-start | bytes 1671176 | tf_op jit(solution)/shard_map/ppermute | solution.py:627
  50.4 0.1 pad_add_fusion.bounds_ref
  50.5 1.8 %collective-permute-done.2.other_ref = f32[1088,128]{1,0:T(8,128)S(1)} collective-permute-done((f32[1088,128]{1,0:T(8,128)S(1)}, f32[1088,128]{1,0:T(8,128)S(1)}, u32[]{:S(2)}, u32[]{:S(2)}) %collective-permute-start.2) | collective-permute-done | bytes 557088 | tf_op jit(solution)/shard_map/ppermute | solution.py:627
  52.3 0.0 copy-done
  52.3 0.0 copy-done.1
  52.3 0.0 copy-done.2
  52.3 0.0 copy-done.7
  52.3 0.0 copy-start.4
  52.3 1.0 %copy-done.4 = bf16[4,256,256]{2,1,0:T(8,128)(2,1)S(1)} copy-done((bf16[4,256,256]{2,1,0:T(8,128)(2,1)S(1)}, bf16[4,256,256]{2,1,0:T(8,128)(2,1)}, u32[]{:S(2)}) %copy-start.4) | copy-done | bytes 524312
  53.4 0.0 copy-start.6
  53.4 1.0 %copy-done.6 = bf16[4,256,256]{2,1,0:T(8,128)(2,1)S(1)} copy-done((bf16[4,256,256]{2,1,0:T(8,128)(2,1)S(1)}, bf16[4,256,256]{2,1,0:T(8,128)(2,1)}, u32[]{:S(2)}) %copy-start.6) | copy-done | bytes 524312
  54.4 7.8 %cycle.1 = f32[256,128]{1,0:T(8,128)S(1)} custom-call(s32[3]{0:T(128)S(1)} %pad_add_fusion.bounds_ref, f32[1088,128]{1,0:T(8,128)S(1)} %bitcast.8, f32[1088,128]{1,0:T(8,128)S(1)} %collective-permute-done.2.other_ref, bf16[4,256,256]{2,1,0:T(8,128)(2,1)S(1)} %get-tuple-element.32.fine_ref, bf16[4,256,256]{2,1,0:T(8,128)(2,1)S(1)} %copy-done.4, ...), custom_call_target="tpu_custom_call" | custom-call | tf_op jit(solution)/shard_map/cycle/pallas_call | solution.py:593
  62.2 20.1 %all_to_all.10 = f32[32,8,128]{2,1,0:T(8,128)S(1)} all-to-all(f32[32,8,128]{2,1,0:T(8,128)S(1)} %bitcast.9), channel_id=1, replica_groups=mesh['gx'=4,'gy'=8,'gz'=16] {'gx','gy'}, dimensions={0} | all-to-all | bytes 262144 | tf_op jit(solution)/shard_map/all_to_all | solution.py:637
  82.4 1.1 %unpack.1 = f32[5,10,320]{2,1,0:T(8,128)} custom-call(s32[1]{0:T(128)} %bitcast.refs_0_, f32[256,128]{1,0:T(8,128)S(1)} %bitcast.10, f32[1,2,64]{2,1,0:T(2,128)S(1)} %copy-done.9), custom_call_target="tpu_custom_call" | custom-call | tf_op jit(solution)/shard_map/unpack/pallas_call | solution.py:227
  (1 shorter events, 0.0 us)
Async XLA Ops:
  0.0 0.7 copy-start.9
  0.7 0.9 %copy-start.8 = (f32[5,10,320]{2,1,0:T(8,128)S(1)}, f32[5,10,320]{2,1,0:T(8,128)}, u32[]{:S(2)}) copy-start(f32[5,10,320]{2,1,0:T(8,128)} %refs_1_.1) | copy-start | bytes 192004
  1.9 6.0 %collective-permute-start = (f32[2,16,128]{2,1,0:T(8,128)S(1)}, f32[2,16,128]{2,1,0:T(8,128)S(1)}, u32[]{:S(2)}, u32[]{:S(2)}) collective-permute-start(f32[2,16,128]{2,1,0:T(8,128)S(1)} %get-tuple-element.21), channel_id=1, source_target_pairs={{1,2},{3,4},{5,6},{7,8},{9,10},{11,12},{13,14},{2,1},{4,3},{6,5},{... | collective-permute-start | bytes 49160 | tf_op jit(solution)/shard_map/ppermute | solution.py:615
  7.9 3.1 %collective-permute-start.1 = (f32[80,128]{1,0:T(8,128)S(1)}, f32[80,128]{1,0:T(8,128)S(1)}, u32[]{:S(2)}, u32[]{:S(2)}) collective-permute-start(f32[80,128]{1,0:T(8,128)S(1)} %get-tuple-element.23), channel_id=1, source_target_pairs={{0,1},{1,0},{2,3},{3,2},{4,5},{5,4},{6,7},{7,6},{8,9},{9,8},{10,11... | collective-permute-start | bytes 122888 | tf_op jit(solution)/shard_map/ppermute | solution.py:618
  11.9 16.1 %copy-start.10 = (f32[125,125]{1,0:T(8,128)S(1)}, f32[125,125]{1,0:T(8,128)}, u32[]{:S(2)}) copy-start(f32[125,125]{1,0:T(8,128)} %fine_ref) | copy-start | bytes 187504
  11.9 16.1 %copy-start.11 = (f32[27,27]{1,0:T(8,128)S(1)}, f32[27,27]{1,0:T(8,128)}, u32[]{:S(2)}) copy-start(f32[27,27]{1,0:T(8,128)} %mid_ref) | copy-start | bytes 8752
  11.9 16.1 %copy-start.12 = (f32[8,8]{1,0:T(8,128)S(1)}, f32[8,8]{1,0:T(8,128)}, u32[]{:S(2)}) copy-start(f32[8,8]{1,0:T(8,128)} %coarse_ref) | copy-start | bytes 772
  11.9 36.6 %all-to-all-start = ((f32[544,2,128]{2,1,0:T(2,128)}), f32[544,2,128]{2,1,0:T(2,128)S(1)}, u32[]{:S(2)}, u32[]{:S(2)}) async-start(f32[544,2,128]{2,1,0:T(2,128)} %bitcast.3), calls=%async_computation | async-start | bytes 1114112 | tf_op jit(solution)/shard_map/all_to_all | solution.py:621
  28.0 1.0 %copy-start.13 = (bf16[9,128,128]{2,1,0:T(8,128)(2,1)S(1)}, bf16[9,128,128]{2,1,0:T(8,128)(2,1)}, u32[]{:S(2)}) copy-start(bf16[9,128,128]{2,1,0:T(8,128)(2,1)} %constant.51.clone.moves_ref) | copy-start | bytes 884740
  29.0 23.3 %copy-start = (bf16[4,256,256]{2,1,0:T(8,128)(2,1)S(1)}, bf16[4,256,256]{2,1,0:T(8,128)(2,1)}, u32[]{:S(2)}) copy-start(bf16[4,256,256]{2,1,0:T(8,128)(2,1)} %constant.54.clone.low_ref) | copy-start | bytes 1572868
  29.0 23.3 %copy-start.1 = (bf16[4,256,256]{2,1,0:T(8,128)(2,1)S(1)}, bf16[4,256,256]{2,1,0:T(8,128)(2,1)}, u32[]{:S(2)}) copy-start(bf16[4,256,256]{2,1,0:T(8,128)(2,1)} %constant.53.clone.up_ref) | copy-start | bytes 1572868
  29.0 23.3 %copy-start.2 = (bf16[4,256,256]{2,1,0:T(8,128)(2,1)S(1)}, bf16[4,256,256]{2,1,0:T(8,128)(2,1)}, u32[]{:S(2)}) copy-start(bf16[4,256,256]{2,1,0:T(8,128)(2,1)} %constant.52.clone.down_ref) | copy-start | bytes 1572868
  29.0 23.3 %copy-start.7 = (bf16[256,256]{1,0:T(8,128)(2,1)S(1)}, bf16[256,256]{1,0:T(8,128)(2,1)}, u32[]{:S(2)}) copy-start(bf16[256,256]{1,0:T(8,128)(2,1)} %constant.55.clone.high_ref) | copy-start | bytes 393220
  42.2 0.8 copy-start.3
  43.0 0.8 copy-start.5
  48.5 3.8 %collective-permute-start.2 = (f32[1088,128]{1,0:T(8,128)S(1)}, f32[1088,128]{1,0:T(8,128)S(1)}, u32[]{:S(2)}, u32[]{:S(2)}) collective-permute-start(f32[1088,128]{1,0:T(8,128)S(1)} %bitcast.7), channel_id=1, source_target_pairs={{0,1},{1,0},{2,3},{3,2},{4,5},{5,4},{6,7},{7,6},{8,9},{9,8},{10,11... | collective-permute-start | bytes 1671176 | tf_op jit(solution)/shard_map/ppermute | solution.py:627
  52.3 1.0 %copy-start.4 = (bf16[4,256,256]{2,1,0:T(8,128)(2,1)S(1)}, bf16[4,256,256]{2,1,0:T(8,128)(2,1)}, u32[]{:S(2)}) copy-start(bf16[4,256,256]{2,1,0:T(8,128)(2,1)} %copy-done.3) | copy-start | bytes 1572868
  53.4 1.0 %copy-start.6 = (bf16[4,256,256]{2,1,0:T(8,128)(2,1)S(1)}, bf16[4,256,256]{2,1,0:T(8,128)(2,1)}, u32[]{:S(2)}) copy-start(bf16[4,256,256]{2,1,0:T(8,128)(2,1)} %copy-done.5) | copy-start | bytes 1572868

commit v4 on v3

--- a/solution.py
+++ b/solution.py
@@ -52,7 +52,7 @@
     table = np.asarray(table, np.float32)
     hi = table.astype(jnp.bfloat16)
     lo = (table - hi.astype(np.float32)).astype(jnp.bfloat16)
-    return np.block([[hi, lo], [hi, np.zeros_like(lo)]])
+    return np.concatenate([hi, lo], axis=1)
 
 
 def transfer_tables():
@@ -250,17 +250,24 @@
 
 def invert(matrix, panels):
     lane, row = iota((LANES, LANES), 1), iota((LANES, LANES), 0)
-    lane16, row16 = iota((16, LANES), 1), iota((16, LANES), 0)
+    lane1, lane16, row16 = iota((1, LANES), 1), iota((16, LANES), 1), iota((16, LANES), 0)
     for panel in range(panels):
         top = panel * 16
         rows = matrix[top : top + 16, :]
-        for step in range(16):
+        for step in range(0, 16, 2):
             pivot = top + step
-            column = rows[:, pivot : pivot + 1]
-            scale = 1.0 / rows[step : step + 1, pivot : pivot + 1]
-            scaled = jnp.where(lane16[0:1] == pivot, scale, rows[step : step + 1, :] * scale)
-            others = jnp.where(lane16 == pivot, 0.0, rows) - column * scaled
-            rows = jnp.where(row16 == step, scaled, others)
+            left = jnp.broadcast_to(rows[:, pivot : pivot + 1], (16, LANES))
+            right = jnp.broadcast_to(rows[:, pivot + 1 : pivot + 2], (16, LANES))
+            a, b = left[step : step + 1], right[step : step + 1]
+            c, d = left[step + 1 : step + 2], right[step + 1 : step + 2]
+            scale = 1.0 / (a * d - b * c)
+            here = (lane1 == pivot) | (lane1 == pivot + 1)
+            one = jnp.where(here, jnp.where(lane1 == pivot, 1.0, 0.0), rows[step : step + 1])
+            two = jnp.where(here, jnp.where(lane1 == pivot, 0.0, 1.0), rows[step + 1 : step + 2])
+            one, two = (d * one - b * two) * scale, (a * two - c * one) * scale
+            others = jnp.where((lane16 == pivot) | (lane16 == pivot + 1), 0.0, rows)
+            others = others - left * one - right * two
+            rows = jnp.where(row16 == step, one, jnp.where(row16 == step + 1, two, others))
         stacked = jnp.concatenate([rows] * 8, axis=0)
         inside = (lane >= top) & (lane < top + 16)
         update = jnp.dot(
@@ -281,38 +288,47 @@
     return jnp.where(row // 32 == lane // 32, wide, 0.0)
 
 
-def inverses_body(moves_ref, fine_ref, mid_ref, coarse_ref, fine_out, mid_out, coarse_out, pad):
+def moves(points, in_lanes):
+    lane, row = iota((1, LANES), 1), iota((LANES, LANES), 0)
+    local, place = (lane % 32, lane // 32) if in_lanes else (lane, 0)
+    tables = []
+    for dimension, stride in enumerate((points * points, points, 1)):
+        index = (local // stride) % points
+        first = (index == 0) & (local < points**3)
+        last = (index == points - 1) & (local < points**3)
+        reach = (points - 1) * stride
+        if dimension == 0 and in_lanes:
+            first, last = first & (place > 0), last & (place < EX - 1)
+            reach = reach - 32
+        source = jnp.where(first, lane + reach, jnp.where(last, lane - reach, -1))
+        tables.append(jnp.where(row == source, 1.0, 0.0))
+    return tables
+
+
+def inverses_body(fine_ref, mid_ref, coarse_ref, out_ref, pad):
     coarse = invert(shifted_block(coarse_ref, pad, COARSE), 1)
     mid = invert(shifted_block(mid_ref, pad, MID), 2)
     fine = invert(shifted_block(fine_ref, pad, FINE), 8)
-    levels = ((fine, fine_out), (repeated(mid), mid_out), (repeated(coarse), coarse_out))
-    for level, (inverse, out) in enumerate(levels):
+    levels = ((fine, FINE), (repeated(mid), MID), (repeated(coarse), COARSE))
+    for level, (inverse, points) in enumerate(levels):
         inverse = 0.35 * inverse
-        out[0] = two_way_table(inverse)
-        for dimension in range(3):
-            moved = jnp.dot(
-                moves_ref[3 * level + dimension].astype(f32),
-                inverse,
-                precision=HIGHEST,
-                preferred_element_type=f32,
-            )
-            out[1 + dimension] = two_way_table(moved)
+        out_ref[4 * level] = two_way(inverse)
+        for dimension, move in enumerate(moves(points, points < FINE)):
+            moved = jnp.dot(move, inverse, precision=HIGHEST, preferred_element_type=f32)
+            out_ref[4 * level + 1 + dimension] = two_way(moved)
 
 
 def inverses(block_fine, block_mid, block_coarse):
-    square = jax.ShapeDtypeStruct((4, 2 * LANES, 2 * LANES), bf16)
-    moves = exchanges(FINE, False) + exchanges(MID, True) + exchanges(COARSE, True)
-    moves = np.stack(moves).astype(jnp.bfloat16)
     return pl.pallas_call(
         inverses_body,
-        out_shape=(square, square, square),
+        out_shape=jax.ShapeDtypeStruct((12, LANES, 2 * LANES), bf16),
         scratch_shapes=[pltpu.VMEM((LANES, LANES), f32)],
         compiler_params=pltpu.CompilerParams(vmem_limit_bytes=8 * MIB),
         cost_estimate=pl.CostEstimate(
             flops=2_000_000_000, bytes_accessed=20_000_000, transcendentals=0
         ),
         name="inverses",
-    )(moves, block_fine, block_mid, block_coarse)
+    )(block_fine, block_mid, block_coarse)
 
 
 def two_way(values):
@@ -321,18 +337,13 @@
     return jnp.concatenate([hi, lo], axis=1)
 
 
-def two_way_table(table):
-    hi = table.astype(bf16)
-    lo = (table - hi.astype(f32)).astype(bf16)
-    return jnp.concatenate(
-        [jnp.concatenate([hi, lo], axis=1), jnp.concatenate([hi, jnp.zeros_like(lo)], axis=1)],
-        axis=0,
-    )
-
-
 def times(values, *tables):
     values = jnp.concatenate([two_way(value) for value in values], axis=1)
-    result = jnp.dot(values, jnp.concatenate(tables, axis=0), preferred_element_type=f32)
+    stack = []
+    for table in tables:
+        high = table[:, 0:LANES]
+        stack += [table, jnp.concatenate([high, jnp.zeros_like(high)], axis=1)]
+    result = jnp.dot(values, jnp.concatenate(stack, axis=0), preferred_element_type=f32)
     return result[:, 0:LANES] + result[:, LANES : 2 * LANES]
 
 
@@ -422,9 +433,7 @@
     bounds_ref,
     mine_ref,
     other_ref,
-    fine_ref,
-    mid_ref,
-    coarse_ref,
+    tables_ref,
     down_ref,
     up_ref,
     low_ref,
@@ -451,9 +460,9 @@
     fine_faces = Faces(FINE, False)
     mid_faces = Faces(MID, True)
     coarse_faces = Faces(COARSE, True)
-    fine_table, *fine_tables = [fine_ref[i] for i in range(4)]
-    mid_table, *mid_tables = [mid_ref[i] for i in range(4)]
-    coarse_table, *coarse_tables = [coarse_ref[i] for i in range(4)]
+    fine_table, *fine_tables = [tables_ref[i] for i in range(4)]
+    mid_table, *mid_tables = [tables_ref[i] for i in range(4, 8)]
+    coarse_table, *coarse_tables = [tables_ref[i] for i in range(8, 12)]
 
     slab = iota((WINDOW, EY, LANES), 0)
     mask[...] = jnp.where((slab >= bounds_ref[0]) & (slab < bounds_ref[1]), 1.0, 0.0)
@@ -568,12 +577,10 @@
     mid_sweep(mid_faces, mid_tables, mid_start, mid_ping, mid_pong, 11)
     mid_sweep(mid_faces, mid_tables, mid_start, mid_pong, mid_ping, 12)
 
-    lifted = two_way(get(mid_ping, at(0, 12, WINDOW - 12)))
+    lifted = get(mid_ping, at(0, 12, WINDOW - 12))
     for x in range(EX):
         rows = at(x, 12, WINDOW - 12)
-        added = jnp.dot(lifted, up_ref[x], preferred_element_type=f32)
-        added = added[:, 0:LANES] + added[:, LANES : 2 * LANES]
-        put(pong, rows, get(pong, rows) + added)
+        put(pong, rows, get(pong, rows) + times((lifted,), up_ref[x]))
     fine_sweep(pong, ping, 13, WINDOW - 13, None)
     fine_sweep(ping, pong, 14, WINDOW - 14, None)
     fine_sweep(pong, ping, RADIUS, WINDOW - RADIUS, None)
@@ -586,19 +593,19 @@
                 out_ref[pl.ds(first, HALF, stride=2 * OWN), :] = values
 
 
-def cycle(bounds, mine, other, fine, mid, coarse, down, up, low, high):
+def cycle(bounds, mine, other, tables, down, up, low, high):
     big = pltpu.VMEM((EX * WINDOW, EY, LANES), f32)
     small = pltpu.VMEM((WINDOW, EY, LANES), f32)
     vmem = pl.BlockSpec(memory_space=pltpu.VMEM)
     return pl.pallas_call(
         cycle_body,
         out_shape=jax.ShapeDtypeStruct((EX * HALF * 2 * OWN, LANES), f32),
-        in_specs=[pl.BlockSpec(memory_space=pltpu.SMEM)] + [vmem] * 9,
+        in_specs=[pl.BlockSpec(memory_space=pltpu.SMEM)] + [vmem] * 7,
         out_specs=vmem,
         scratch_shapes=[big] * 7 + [small] * 8,
-        compiler_params=pltpu.CompilerParams(vmem_limit_bytes=32 * MIB),
+        compiler_params=pltpu.CompilerParams(vmem_limit_bytes=20 * MIB),
         name="cycle",
-    )(bounds, mine, other, fine, mid, coarse, down, up, low, high)
+    )(bounds, mine, other, tables, down, up, low, high)
 
 
 def per_device(fine_source_field, scaling, block_fine, block_mid, block_coarse):
@@ -621,9 +628,7 @@
     recv = lax.all_to_all(
         chunks.reshape(parts * WINDOW // 2, 2, LANES), ("gx", "gy"), 0, 0, tiled=True
     ).reshape(parts * WINDOW, LANES)
-    recv, fine, mid, coarse = lax.optimization_barrier(
-        (recv, *inverses(*matrices))
-    )
+    recv, tables = lax.optimization_barrier((recv, inverses(*matrices)))
     other = lax.ppermute(recv, "gz", pairs)
 
     part = lax.axis_index("gx") * lax.axis_size("gy") + lax.axis_index("gy")
@@ -632,7 +637,7 @@
         [jnp.maximum(0, -first), jnp.minimum(WINDOW, groups * count_z - first), core]
     )
     result = cycle(
-        bounds.astype(jnp.int32), recv, other, fine, mid, coarse, down, up, low, high
+        bounds.astype(jnp.int32), recv, other, tables, down, up, low, high
     )
     back = lax.all_to_all(
         result.reshape(parts, 2 * OWN, LANES), ("gx", "gy"), 0, 0, tiled=True

time: 84 us -> 80.1 us (0.954)
  waiting for transfers between devices: 10.7 us -> 17.7 us
  local copies, waits for them, and re-layouts: 6.22 us -> 1.62 us
  Pallas kernels: 23.4 us -> 18.9 us
  blocking collectives: 20.1 us -> 18.5 us
    all_to_all x1, waiting for transfers between devices: 4.67 us -> 11.6 us  [per_device(): lax.all_to_all(chunks.reshape(parts * WINDOW // 2, 2, LANES), ('gx', 'gy'...]
    unnamed x28 -> x18, local copies, waits for them, and re-layouts: 6.22 us -> 1.62 us
    pallas_call x1, Pallas kernels: 13.2 us -> 8.8 us  [inverses(): pl.pallas_call(inverses_body, out_shape=jax.ShapeDtypeStruct((12, LANES,...]
    all_to_all x1, blocking collectives: 20.1 us -> 18.5 us  [per_device(): lax.all_to_all(result.reshape(parts, 2 * OWN, LANES), ('gx', 'gy'), 0, 0,...]
  transfers between devices with their start and end apart: 4 -> 4, of which waited for: 4 -> 4; matrix products, arithmetic and copies ran while one was open for 0% -> 0% of each run, Pallas kernels for 16% -> 11%
where the time goes in v4:
time: 80.1 us; the launch traced here: 79.7 us
  starting transfers between devices  22.8 us (28%)
  Pallas kernels  18.9 us (24%)
  blocking collectives  18.5 us (23%)
  waiting for transfers between devices  17.7 us (22%)
  local copies, waits for them, and re-layouts  1.62 us (2%)
    all_to_all x1, blocking collectives, per_device(): lax.all_to_all(result.reshape(parts, 2 * OWN, LANES), ('gx', 'gy'), 0, 0,...  18.5 us
    all_to_all x1, starting transfers between devices, per_device(): lax.all_to_all(chunks.reshape(parts * WINDOW // 2, 2, LANES), ('gx', 'gy'...  16.1 us
    all_to_all x1, waiting for transfers between devices, per_device(): lax.all_to_all(chunks.reshape(parts * WINDOW // 2, 2, LANES), ('gx', 'gy'...  11.6 us
    pallas_call x1, Pallas kernels, inverses(): pl.pallas_call(inverses_body, out_shape=jax.ShapeDtypeStruct((12, LANES,...  8.8 us
    pallas_call x1, Pallas kernels, cycle(): pl.pallas_call(cycle_body, out_shape=jax.ShapeDtypeStruct((EX * HALF * 2...  7.8 us
    ppermute x1, waiting for transfers between devices, per_device(): halo = lax.ppermute(edge, 'gz', ties + [(j, i) for i, j in ties])  3.05 us
    ppermute x1, starting transfers between devices, per_device(): halo = lax.ppermute(edge, 'gz', ties + [(j, i) for i, j in ties])  2.9 us
    ppermute x1, starting transfers between devices, per_device(): other = lax.ppermute(give, 'gz', pairs)  1.92 us
  transfers between devices with their start and end apart: 4, of which 4 were waited for; matrix products, arithmetic and copies ran while one was open for 0% of the time, Pallas kernels for 11%

profile of v4, /device:TPU:2, one launch (start us, length us, event | category | flops | bytes accessed | tf_op | source)
XLA Modules:
  0.0 79.7 jit_solution(1177002478968610871)
XLA Ops:
  0.0 0.0 copy-start.5
  0.0 0.7 copy-done.5
  0.7 0.0 copy-start.3
  0.7 0.9 %copy-done.3 = f32[5,10,320]{2,1,0:T(8,128)S(1)} copy-done((f32[5,10,320]{2,1,0:T(8,128)S(1)}, f32[5,10,320]{2,1,0:T(8,128)}, u32[]{:S(2)}) %copy-start.3) | copy-done | bytes 64024
  1.6 0.3 pack.1
  1.9 2.9 %collective-permute-start = (f32[2,16,128]{2,1,0:T(8,128)S(1)}, f32[2,16,128]{2,1,0:T(8,128)S(1)}, u32[]{:S(2)}, u32[]{:S(2)}) collective-permute-start(f32[2,16,128]{2,1,0:T(8,128)S(1)} %get-tuple-element.16), channel_id=1, source_target_pairs={{1,2},{3,4},{5,6},{7,8},{9,10},{11,12},{13,14},{2,1},{4,3},{6,5},{... | collective-permute-start | bytes 49160 | tf_op jit(solution)/shard_map/ppermute | solution.py:622
  4.8 3.1 %collective-permute-done.refs_2_ = f32[2,16,128]{2,1,0:T(8,128)S(1)} collective-permute-done((f32[2,16,128]{2,1,0:T(8,128)S(1)}, f32[2,16,128]{2,1,0:T(8,128)S(1)}, u32[]{:S(2)}, u32[]{:S(2)}) %collective-permute-start) | collective-permute-done | bytes 16416 | tf_op jit(solution)/shard_map/ppermute | solution.py:622
  7.9 1.9 %collective-permute-start.1 = (f32[80,128]{1,0:T(8,128)S(1)}, f32[80,128]{1,0:T(8,128)S(1)}, u32[]{:S(2)}, u32[]{:S(2)}) collective-permute-start(f32[80,128]{1,0:T(8,128)S(1)} %get-tuple-element.18), channel_id=1, source_target_pairs={{0,1},{1,0},{2,3},{3,2},{4,5},{5,4},{6,7},{7,6},{8,9},{9,8},{10,11... | collective-permute-start | bytes 122888 | tf_op jit(solution)/shard_map/ppermute | solution.py:625
  9.8 1.2 %collective-permute-done.1.refs_2_ = f32[80,128]{1,0:T(8,128)S(1)} collective-permute-done((f32[80,128]{1,0:T(8,128)S(1)}, f32[80,128]{1,0:T(8,128)S(1)}, u32[]{:S(2)}, u32[]{:S(2)}) %collective-permute-start.1) | collective-permute-done | bytes 40992 | tf_op jit(solution)/shard_map/ppermute | solution.py:625
  11.0 0.8 %window.1 = f32[1088,128]{1,0:T(8,128)} custom-call(s32[1]{0:T(128)} %bitcast.refs_0_, f32[80,128]{1,0:T(8,128)S(1)} %get-tuple-element.17.refs_1_, f32[80,128]{1,0:T(8,128)S(1)} %collective-permute-done.1.refs_2_), custom_call_target="tpu_custom_call" | custom-call | tf_op jit(solution)/shard_map/window/pallas_call | solution.py:179
  11.8 0.0 copy-start.6
  11.8 0.0 copy-start.7
  11.9 0.0 copy-start.8
  11.9 16.1 %all-to-all-start = ((f32[544,2,128]{2,1,0:T(2,128)}), f32[544,2,128]{2,1,0:T(2,128)S(1)}, u32[]{:S(2)}, u32[]{:S(2)}) async-start(f32[544,2,128]{2,1,0:T(2,128)} %bitcast.3), calls=%async_computation | async-start | bytes 1114112 | tf_op jit(solution)/shard_map/all_to_all | solution.py:628
  28.0 0.0 copy-done.6
  28.0 0.0 copy-done.7
  28.0 0.0 copy-done.8
  28.0 0.0 copy-start
  28.0 0.0 copy-start.1
  28.0 0.0 copy-start.2
  28.0 0.0 copy-start.4
  28.0 8.8 %inverses.1.tables_ref = bf16[12,128,256]{2,1,0:T(8,128)(2,1)S(1)} custom-call(f32[125,125]{1,0:T(8,128)S(1)} %copy-done.6, f32[27,27]{1,0:T(8,128)S(1)} %copy-done.7, f32[8,8]{1,0:T(8,128)S(1)} %copy-done.8), custom_call_target="tpu_custom_call" | custom-call | flops 2000000000 | bytes 20000000 | tf_op jit(solution)/shard_map/inverses/pallas_call | solution.py:322
  36.8 11.6 %all-to-all-done = f32[544,2,128]{2,1,0:T(2,128)S(1)} async-done(((f32[544,2,128]{2,1,0:T(2,128)}), f32[544,2,128]{2,1,0:T(2,128)S(1)}, u32[]{:S(2)}, u32[]{:S(2)}) %all-to-all-start) | async-done | bytes 557088 | tf_op jit(solution)/shard_map/all_to_all | solution.py:628
  48.5 1.9 %collective-permute-start.2 = (f32[1088,128]{1,0:T(8,128)S(1)}, f32[1088,128]{1,0:T(8,128)S(1)}, u32[]{:S(2)}, u32[]{:S(2)}) collective-permute-start(f32[1088,128]{1,0:T(8,128)S(1)} %bitcast.7), channel_id=1, source_target_pairs={{0,1},{1,0},{2,3},{3,2},{4,5},{5,4},{6,7},{7,6},{8,9},{9,8},{10,11... | collective-permute-start | bytes 1671176 | tf_op jit(solution)/shard_map/ppermute | solution.py:632
  50.4 0.1 pad_add_fusion.bounds_ref
  50.5 1.8 %collective-permute-done.2.other_ref = f32[1088,128]{1,0:T(8,128)S(1)} collective-permute-done((f32[1088,128]{1,0:T(8,128)S(1)}, f32[1088,128]{1,0:T(8,128)S(1)}, u32[]{:S(2)}, u32[]{:S(2)}) %collective-permute-start.2) | collective-permute-done | bytes 557088 | tf_op jit(solution)/shard_map/ppermute | solution.py:632
  52.3 0.0 copy-done
  52.3 0.0 copy-done.1
  52.3 0.0 copy-done.2
  52.3 0.0 copy-done.4
  52.3 7.8 %cycle.1 = f32[256,128]{1,0:T(8,128)S(1)} custom-call(s32[3]{0:T(128)S(1)} %pad_add_fusion.bounds_ref, f32[1088,128]{1,0:T(8,128)S(1)} %bitcast.8, f32[1088,128]{1,0:T(8,128)S(1)} %collective-permute-done.2.other_ref, bf16[12,128,256]{2,1,0:T(8,128)(2,1)S(1)} %inverses.1.tables_ref, bf16[4,128,256]{2,1,0:T(8,128)(2,1)S(1)} %copy-done.2, ...), custom_call_target="tpu_custom_call" | custom-call | tf_op jit(solution)/shard_map/cycle/pallas_call | solution.py:600
  60.1 18.5 %all_to_all.10 = f32[32,8,128]{2,1,0:T(8,128)S(1)} all-to-all(f32[32,8,128]{2,1,0:T(8,128)S(1)} %bitcast.9), channel_id=1, replica_groups=mesh['gx'=4,'gy'=8,'gz'=16] {'gx','gy'}, dimensions={0} | all-to-all | bytes 262144 | tf_op jit(solution)/shard_map/all_to_all | solution.py:642
  78.6 1.1 %unpack.1 = f32[5,10,320]{2,1,0:T(8,128)} custom-call(s32[1]{0:T(128)} %bitcast.refs_0_, f32[256,128]{1,0:T(8,128)S(1)} %bitcast.10, f32[1,2,64]{2,1,0:T(2,128)S(1)} %copy-done.5), custom_call_target="tpu_custom_call" | custom-call | tf_op jit(solution)/shard_map/unpack/pallas_call | solution.py:227
  (1 shorter events, 0.0 us)
Async XLA Ops:
  0.0 0.7 copy-start.5
  0.7 0.9 %copy-start.3 = (f32[5,10,320]{2,1,0:T(8,128)S(1)}, f32[5,10,320]{2,1,0:T(8,128)}, u32[]{:S(2)}) copy-start(f32[5,10,320]{2,1,0:T(8,128)} %refs_1_.1) | copy-start | bytes 192004
  1.9 6.0 %collective-permute-start = (f32[2,16,128]{2,1,0:T(8,128)S(1)}, f32[2,16,128]{2,1,0:T(8,128)S(1)}, u32[]{:S(2)}, u32[]{:S(2)}) collective-permute-start(f32[2,16,128]{2,1,0:T(8,128)S(1)} %get-tuple-element.16), channel_id=1, source_target_pairs={{1,2},{3,4},{5,6},{7,8},{9,10},{11,12},{13,14},{2,1},{4,3},{6,5},{... | collective-permute-start | bytes 49160 | tf_op jit(solution)/shard_map/ppermute | solution.py:622
  7.9 3.1 %collective-permute-start.1 = (f32[80,128]{1,0:T(8,128)S(1)}, f32[80,128]{1,0:T(8,128)S(1)}, u32[]{:S(2)}, u32[]{:S(2)}) collective-permute-start(f32[80,128]{1,0:T(8,128)S(1)} %get-tuple-element.18), channel_id=1, source_target_pairs={{0,1},{1,0},{2,3},{3,2},{4,5},{5,4},{6,7},{7,6},{8,9},{9,8},{10,11... | collective-permute-start | bytes 122888 | tf_op jit(solution)/shard_map/ppermute | solution.py:625
  11.8 16.1 %copy-start.6 = (f32[125,125]{1,0:T(8,128)S(1)}, f32[125,125]{1,0:T(8,128)}, u32[]{:S(2)}) copy-start(f32[125,125]{1,0:T(8,128)} %fine_ref) | copy-start | bytes 187504
  11.8 16.1 %copy-start.7 = (f32[27,27]{1,0:T(8,128)S(1)}, f32[27,27]{1,0:T(8,128)}, u32[]{:S(2)}) copy-start(f32[27,27]{1,0:T(8,128)} %mid_ref) | copy-start | bytes 8752
  11.9 16.1 %copy-start.8 = (f32[8,8]{1,0:T(8,128)S(1)}, f32[8,8]{1,0:T(8,128)}, u32[]{:S(2)}) copy-start(f32[8,8]{1,0:T(8,128)} %coarse_ref) | copy-start | bytes 772
  11.9 36.6 %all-to-all-start = ((f32[544,2,128]{2,1,0:T(2,128)}), f32[544,2,128]{2,1,0:T(2,128)S(1)}, u32[]{:S(2)}, u32[]{:S(2)}) async-start(f32[544,2,128]{2,1,0:T(2,128)} %bitcast.3), calls=%async_computation | async-start | bytes 1114112 | tf_op jit(solution)/shard_map/all_to_all | solution.py:628
  28.0 24.3 %copy-start = (bf16[4,128,256]{2,1,0:T(8,128)(2,1)S(1)}, bf16[4,128,256]{2,1,0:T(8,128)(2,1)}, u32[]{:S(2)}) copy-start(bf16[4,128,256]{2,1,0:T(8,128)(2,1)} %constant.51.clone.low_ref) | copy-start | bytes 786436
  28.0 24.3 %copy-start.1 = (bf16[4,128,256]{2,1,0:T(8,128)(2,1)S(1)}, bf16[4,128,256]{2,1,0:T(8,128)(2,1)}, u32[]{:S(2)}) copy-start(bf16[4,128,256]{2,1,0:T(8,128)(2,1)} %constant.50.clone.up_ref) | copy-start | bytes 786436
  28.0 24.3 %copy-start.2 = (bf16[4,128,256]{2,1,0:T(8,128)(2,1)S(1)}, bf16[4,128,256]{2,1,0:T(8,128)(2,1)}, u32[]{:S(2)}) copy-start(bf16[4,128,256]{2,1,0:T(8,128)(2,1)} %constant.49.clone.down_ref) | copy-start | bytes 786436
  28.0 24.3 %copy-start.4 = (bf16[128,256]{1,0:T(8,128)(2,1)S(1)}, bf16[128,256]{1,0:T(8,128)(2,1)}, u32[]{:S(2)}) copy-start(bf16[128,256]{1,0:T(8,128)(2,1)} %constant.52.clone.high_ref) | copy-start | bytes 196612
  48.5 3.8 %collective-permute-start.2 = (f32[1088,128]{1,0:T(8,128)S(1)}, f32[1088,128]{1,0:T(8,128)S(1)}, u32[]{:S(2)}, u32[]{:S(2)}) collective-permute-start(f32[1088,128]{1,0:T(8,128)S(1)} %bitcast.7), channel_id=1, source_target_pairs={{0,1},{1,0},{2,3},{3,2},{4,5},{5,4},{6,7},{7,6},{8,9},{9,8},{10,11... | collective-permute-start | bytes 1671176 | tf_op jit(solution)/shard_map/ppermute | solution.py:632

commit v5 on v4

--- a/solution.py
+++ b/solution.py
@@ -16,6 +16,7 @@
 HALO = 16
 OWN = 4
 WINDOW = OWN + 2 * RADIUS
+SPLIT = WINDOW // 2
 EX = 4
 EY = 16
 HALF = EY // 2
@@ -134,44 +135,24 @@
     )(core, field, scaling)
 
 
-def join_body(core_ref, own_ref, halo_ref, mine_ref, give_ref, *, count_z):
-    core = core_ref[0]
-    own_at = pl.multiple_of((1 - core) * HALO, HALO)
-    halo_at = pl.multiple_of(core * count_z, HALO)
-    for ref, y in ((mine_ref, core), (give_ref, 1 - core)):
-        ref[pl.ds(own_at, count_z), :] = own_ref[y]
-        ref[pl.ds(halo_at, HALO), :] = halo_ref[y]
-
-
-def join(core, own, halo):
-    count_z = own.shape[1]
-
-    def body(*refs):
-        join_body(*refs, count_z=count_z)
-
-    vmem = pl.BlockSpec(memory_space=pltpu.VMEM)
-    line = jax.ShapeDtypeStruct((count_z + HALO, LANES), f32)
-    return pl.pallas_call(
-        body,
-        out_shape=(line, line),
-        in_specs=[pl.BlockSpec(memory_space=pltpu.SMEM), vmem, vmem],
-        out_specs=(vmem, vmem),
-        compiler_params=pltpu.CompilerParams(vmem_limit_bytes=8 * MIB),
-        name="join",
-    )(core, own, halo)
-
-
-def window_body(core_ref, mine_ref, other_ref, out_ref, line, *, parts):
-    length = mine_ref.shape[0]
-    core = core_ref[0]
-    line[pl.ds(pl.multiple_of(core * length, HALO), length), :] = mine_ref[...]
-    line[pl.ds(pl.multiple_of((1 - core) * length, HALO), length), :] = other_ref[...]
-    for part in range(parts):
-        start = HALO - RADIUS + OWN * part
-        out_ref[part * WINDOW : (part + 1) * WINDOW, :] = line[start : start + WINDOW, :]
-
-
-def window(core, mine, other, parts):
+def window_body(core_ref, own_ref, sibling_ref, halo_ref, out_ref, line, *, parts):
+    count_z = own_ref.shape[1]
+    for core in range(2):
+        places = (HALO, HALO + count_z, 0) if core == 0 else (count_z, 0, 2 * count_z)
+
+        @pl.when(core_ref[0] == core)
+        def _(core=core, places=places):
+            for ref, place in zip((own_ref, sibling_ref, halo_ref), places):
+                line[:, place : place + ref.shape[1], :] = ref[...]
+            first = HALO - RADIUS if core == 0 else SPLIT - RADIUS
+            for part in range(parts):
+                for y in range(2):
+                    start = first + OWN * part
+                    row = part * WINDOW + y * SPLIT
+                    out_ref[row : row + SPLIT, :] = line[y, start : start + SPLIT, :]
+
+
+def window(core, own, sibling, halo, parts):
     def body(*refs):
         window_body(*refs, parts=parts)
 
@@ -179,12 +160,12 @@
     return pl.pallas_call(
         body,
         out_shape=jax.ShapeDtypeStruct((parts * WINDOW, LANES), f32),
-        in_specs=[pl.BlockSpec(memory_space=pltpu.SMEM), vmem, vmem],
+        in_specs=[pl.BlockSpec(memory_space=pltpu.SMEM), vmem, vmem, vmem],
         out_specs=vmem,
-        scratch_shapes=[pltpu.VMEM((2 * mine.shape[0], LANES), f32)],
+        scratch_shapes=[pltpu.VMEM((2, 2 * own.shape[1] + HALO, LANES), f32)],
         compiler_params=pltpu.CompilerParams(vmem_limit_bytes=8 * MIB),
         name="window",
-    )(core, mine, other)
+    )(core, own, sibling, halo)
 
 
 def unpack_body(core_ref, back_ref, scale_ref, out_ref, turned, *, count_z):
@@ -413,8 +394,8 @@
 CHUNK = 16
 
 
-def cuts(start, stop):
-    count = -(-(stop - start) // CHUNK)
+def cuts(start, stop, chunk=CHUNK):
+    count = -(-(stop - start) // chunk)
     edges = [start + (stop - start) * piece // count for piece in range(count + 1)]
     return list(zip(edges[:-1], edges[1:]))
 
@@ -466,7 +447,7 @@
 
     slab = iota((WINDOW, EY, LANES), 0)
     mask[...] = jnp.where((slab >= bounds_ref[0]) & (slab < bounds_ref[1]), 1.0, 0.0)
-    even_is_mine = bounds_ref[2] == 0
+    upper_is_mine = bounds_ref[2] == 1
 
     def at(x, a, b):
         return slice(x * WINDOW + a, x * WINDOW + b)
@@ -506,10 +487,13 @@
         for c, d in cuts(0, WINDOW):
             values = []
             for z in range(c, d):
-                place = pl.ds(x * HALF * WINDOW + z, HALF, stride=WINDOW)
-                mine, other = mine_ref[place, :], other_ref[place, :]
-                values.append(jnp.where(even_is_mine, mine, other))
-                values.append(jnp.where(even_is_mine, other, mine))
+                for y in range(2):
+                    first = x * HALF * WINDOW + y * SPLIT + z % SPLIT
+                    place = pl.ds(first, HALF, stride=WINDOW)
+                    mine, other = mine_ref[place, :], other_ref[place, :]
+                    if z < SPLIT:
+                        mine, other = other, mine
+                    values.append(jnp.where(upper_is_mine, mine, other))
             values = jnp.concatenate(values, axis=0)
             rows = at(x, c, d)
             put(left, rows, values)
@@ -541,7 +525,7 @@
         put(mid_start, rows, 2.0 * times((total,), mid_table))
 
     def mid_sweep(faces, tables, base, source, target, margin, keep=None):
-        for c, d in cuts(margin, WINDOW - margin):
+        for c, d in cuts(margin, WINDOW - margin, CHUNK // 2):
             rows = at(0, c, d)
             values = mid_gather(faces, source, c, d)
             if keep is not None:
@@ -619,11 +603,10 @@
 
     own, edge = pack(cores, fine_source_field, scaling)
     ties = [(i, i + 1) for i in range(1, groups - 1, 2)]
+    pairs = [(i, i ^ 1) for i in range(groups)]
     halo = lax.ppermute(edge, "gz", ties + [(j, i) for i, j in ties])
-    pairs = [(i, i ^ 1) for i in range(groups)]
-    mine, give = join(cores, own, halo)
-    other = lax.ppermute(give, "gz", pairs)
-    chunks = window(cores, mine, other, parts)
+    sibling = lax.ppermute(own, "gz", pairs)
+    chunks = window(cores, own, sibling, halo, parts)
     chunks, *matrices = lax.optimization_barrier((chunks, block_fine, block_mid, block_coarse))
     recv = lax.all_to_all(
         chunks.reshape(parts * WINDOW // 2, 2, LANES), ("gx", "gy"), 0, 0, tiled=True

time: 80.1 us -> 77.9 us (0.973)
  the two profiles are of different devices: /device:TPU:2 before, /device:TPU:4 now
where the time goes in v5:
time: 77.9 us; the launch traced here: 77.6 us
  starting transfers between devices  23.5 us (30%)
  blocking collectives  18.9 us (24%)
  Pallas kernels  18.8 us (24%)
  waiting for transfers between devices  14.5 us (19%)
  local copies, waits for them, and re-layouts  1.62 us (2%)
    all_to_all x1, blocking collectives, per_device(): lax.all_to_all(result.reshape(parts, 2 * OWN, LANES), ('gx', 'gy'), 0, 0,...  18.9 us
    all_to_all x1, starting transfers between devices, per_device(): lax.all_to_all(chunks.reshape(parts * WINDOW // 2, 2, LANES), ('gx', 'gy'...  16.1 us
    all_to_all x1, waiting for transfers between devices, per_device(): lax.all_to_all(chunks.reshape(parts * WINDOW // 2, 2, LANES), ('gx', 'gy'...  10.3 us
    pallas_call x1, Pallas kernels, inverses(): pl.pallas_call(inverses_body, out_shape=jax.ShapeDtypeStruct((12, LANES,...  8.8 us
    pallas_call x1, Pallas kernels, cycle(): pl.pallas_call(cycle_body, out_shape=jax.ShapeDtypeStruct((EX * HALF * 2...  7.69 us
    ppermute x1, starting transfers between devices, per_device(): halo = lax.ppermute(edge, 'gz', ties + [(j, i) for i, j in ties])  3.56 us
    ppermute x1, waiting for transfers between devices, per_device(): halo = lax.ppermute(edge, 'gz', ties + [(j, i) for i, j in ties])  2.39 us
    ppermute x1, starting transfers between devices, per_device(): sibling = lax.ppermute(own, 'gz', pairs)  1.92 us
  transfers between devices with their start and end apart: 4, of which 3 were waited for; matrix products, arithmetic and copies ran while one was open for 0% of the time, Pallas kernels for 11%

profile of v5, /device:TPU:4, one launch (start us, length us, event | category | flops | bytes accessed | tf_op | source)
XLA Modules:
  0.0 77.6 jit_solution(7022625851020020285)
XLA Ops:
  0.0 0.0 copy-start.5
  0.0 0.7 copy-done.5
  0.7 0.0 copy-start.3
  0.7 0.9 %copy-done.3 = f32[5,10,320]{2,1,0:T(8,128)S(1)} copy-done((f32[5,10,320]{2,1,0:T(8,128)S(1)}, f32[5,10,320]{2,1,0:T(8,128)}, u32[]{:S(2)}) %copy-start.3) | copy-done | bytes 64024
  1.6 0.3 pack.1
  1.9 1.9 %collective-permute-start = (f32[2,64,128]{2,1,0:T(8,128)S(1)}, f32[2,64,128]{2,1,0:T(8,128)S(1)}, u32[]{:S(2)}, u32[]{:S(2)}) collective-permute-start(f32[2,64,128]{2,1,0:T(8,128)S(1)} %get-tuple-element.13.refs_1_), channel_id=1, source_target_pairs={{0,1},{1,0},{2,3},{3,2},{4,5},{5,4},{6,7},{7,6},{8,9},{9,8},{10,11... | collective-permute-start | bytes 196616 | tf_op jit(solution)/shard_map/ppermute | solution.py:608
  3.9 3.6 %collective-permute-start.1 = (f32[2,16,128]{2,1,0:T(8,128)S(1)}, f32[2,16,128]{2,1,0:T(8,128)S(1)}, u32[]{:S(2)}, u32[]{:S(2)}) collective-permute-start(f32[2,16,128]{2,1,0:T(8,128)S(1)} %get-tuple-element.14), channel_id=1, source_target_pairs={{1,2},{3,4},{5,6},{7,8},{9,10},{11,12},{13,14},{2,1},{4,3},{6,5},{... | collective-permute-start | bytes 49160 | tf_op jit(solution)/shard_map/ppermute | solution.py:607
  7.4 2.4 %collective-permute-done.1.refs_3_ = f32[2,16,128]{2,1,0:T(8,128)S(1)} collective-permute-done((f32[2,16,128]{2,1,0:T(8,128)S(1)}, f32[2,16,128]{2,1,0:T(8,128)S(1)}, u32[]{:S(2)}, u32[]{:S(2)}) %collective-permute-start.1) | collective-permute-done | bytes 16416 | tf_op jit(solution)/shard_map/ppermute | solution.py:607
  9.8 0.0 collective-permute-done.refs_2_
  9.8 0.9 %window.1 = f32[1088,128]{1,0:T(8,128)} custom-call(s32[1]{0:T(128)} %bitcast.refs_0_, f32[2,64,128]{2,1,0:T(8,128)S(1)} %get-tuple-element.13.refs_1_, f32[2,64,128]{2,1,0:T(8,128)S(1)} %collective-permute-done.refs_2_, f32[2,16,128]{2,1,0:T(8,128)S(1)} %collective-permute-done.1.refs_3_), custom_call_target="tpu_custom_call" | custom-call | tf_op jit(solution)/shard_map/window/pallas_call | solution.py:160
  10.7 0.0 copy-start.6
  10.7 0.0 copy-start.7
  10.7 0.0 copy-start.8
  10.7 16.1 %all-to-all-start = ((f32[544,2,128]{2,1,0:T(2,128)}), f32[544,2,128]{2,1,0:T(2,128)S(1)}, u32[]{:S(2)}, u32[]{:S(2)}) async-start(f32[544,2,128]{2,1,0:T(2,128)} %bitcast.3), calls=%async_computation | async-start | bytes 1114112 | tf_op jit(solution)/shard_map/all_to_all | solution.py:611
  26.8 0.0 copy-done.6
  26.8 0.0 copy-done.7
  26.8 0.0 copy-done.8
  26.8 0.0 copy-start
  26.8 0.0 copy-start.1
  26.9 0.0 copy-start.2
  26.9 0.0 copy-start.4
  26.9 8.8 %inverses.1.tables_ref = bf16[12,128,256]{2,1,0:T(8,128)(2,1)S(1)} custom-call(f32[125,125]{1,0:T(8,128)S(1)} %copy-done.6, f32[27,27]{1,0:T(8,128)S(1)} %copy-done.7, f32[8,8]{1,0:T(8,128)S(1)} %copy-done.8), custom_call_target="tpu_custom_call" | custom-call | flops 2000000000 | bytes 20000000 | tf_op jit(solution)/shard_map/inverses/pallas_call | solution.py:303
  35.7 10.3 %all-to-all-done = f32[544,2,128]{2,1,0:T(2,128)S(1)} async-done(((f32[544,2,128]{2,1,0:T(2,128)}), f32[544,2,128]{2,1,0:T(2,128)S(1)}, u32[]{:S(2)}, u32[]{:S(2)}) %all-to-all-start) | async-done | bytes 557088 | tf_op jit(solution)/shard_map/all_to_all | solution.py:611
  46.0 1.9 %collective-permute-start.2 = (f32[1088,128]{1,0:T(8,128)S(1)}, f32[1088,128]{1,0:T(8,128)S(1)}, u32[]{:S(2)}, u32[]{:S(2)}) collective-permute-start(f32[1088,128]{1,0:T(8,128)S(1)} %bitcast.7), channel_id=1, source_target_pairs={{0,1},{1,0},{2,3},{3,2},{4,5},{5,4},{6,7},{7,6},{8,9},{9,8},{10,11... | collective-permute-start | bytes 1671176 | tf_op jit(solution)/shard_map/ppermute | solution.py:615
  47.9 0.1 pad_add_fusion.bounds_ref
  48.0 1.8 %collective-permute-done.2.other_ref = f32[1088,128]{1,0:T(8,128)S(1)} collective-permute-done((f32[1088,128]{1,0:T(8,128)S(1)}, f32[1088,128]{1,0:T(8,128)S(1)}, u32[]{:S(2)}, u32[]{:S(2)}) %collective-permute-start.2) | collective-permute-done | bytes 557088 | tf_op jit(solution)/shard_map/ppermute | solution.py:615
  49.8 0.0 copy-done
  49.8 0.0 copy-done.1
  49.8 0.0 copy-done.2
  49.8 0.0 copy-done.4
  49.8 7.7 %cycle.1 = f32[256,128]{1,0:T(8,128)S(1)} custom-call(s32[3]{0:T(128)S(1)} %pad_add_fusion.bounds_ref, f32[1088,128]{1,0:T(8,128)S(1)} %bitcast.8, f32[1088,128]{1,0:T(8,128)S(1)} %collective-permute-done.2.other_ref, bf16[12,128,256]{2,1,0:T(8,128)(2,1)S(1)} %inverses.1.tables_ref, bf16[4,128,256]{2,1,0:T(8,128)(2,1)S(1)} %copy-done.2, ...), custom_call_target="tpu_custom_call" | custom-call | tf_op jit(solution)/shard_map/cycle/pallas_call | solution.py:584
  57.5 18.9 %all_to_all.10 = f32[32,8,128]{2,1,0:T(8,128)S(1)} all-to-all(f32[32,8,128]{2,1,0:T(8,128)S(1)} %bitcast.9), channel_id=1, replica_groups=mesh['gx'=4,'gy'=8,'gz'=16] {'gx','gy'}, dimensions={0} | all-to-all | bytes 262144 | tf_op jit(solution)/shard_map/all_to_all | solution.py:625
  76.4 1.1 %unpack.1 = f32[5,10,320]{2,1,0:T(8,128)} custom-call(s32[1]{0:T(128)} %bitcast.refs_0_, f32[256,128]{1,0:T(8,128)S(1)} %bitcast.10, f32[1,2,64]{2,1,0:T(2,128)S(1)} %copy-done.5), custom_call_target="tpu_custom_call" | custom-call | tf_op jit(solution)/shard_map/unpack/pallas_call | solution.py:208
Async XLA Ops:
  0.0 0.7 copy-start.5
  0.7 0.9 %copy-start.3 = (f32[5,10,320]{2,1,0:T(8,128)S(1)}, f32[5,10,320]{2,1,0:T(8,128)}, u32[]{:S(2)}) copy-start(f32[5,10,320]{2,1,0:T(8,128)} %refs_1_.1) | copy-start | bytes 192004
  1.9 7.9 %collective-permute-start = (f32[2,64,128]{2,1,0:T(8,128)S(1)}, f32[2,64,128]{2,1,0:T(8,128)S(1)}, u32[]{:S(2)}, u32[]{:S(2)}) collective-permute-start(f32[2,64,128]{2,1,0:T(8,128)S(1)} %get-tuple-element.13.refs_1_), channel_id=1, source_target_pairs={{0,1},{1,0},{2,3},{3,2},{4,5},{5,4},{6,7},{7,6},{8,9},{9,8},{10,11... | collective-permute-start | bytes 196616 | tf_op jit(solution)/shard_map/ppermute | solution.py:608
  3.9 6.0 %collective-permute-start.1 = (f32[2,16,128]{2,1,0:T(8,128)S(1)}, f32[2,16,128]{2,1,0:T(8,128)S(1)}, u32[]{:S(2)}, u32[]{:S(2)}) collective-permute-start(f32[2,16,128]{2,1,0:T(8,128)S(1)} %get-tuple-element.14), channel_id=1, source_target_pairs={{1,2},{3,4},{5,6},{7,8},{9,10},{11,12},{13,14},{2,1},{4,3},{6,5},{... | collective-permute-start | bytes 49160 | tf_op jit(solution)/shard_map/ppermute | solution.py:607
  10.7 16.1 %copy-start.6 = (f32[125,125]{1,0:T(8,128)S(1)}, f32[125,125]{1,0:T(8,128)}, u32[]{:S(2)}) copy-start(f32[125,125]{1,0:T(8,128)} %fine_ref) | copy-start | bytes 187504
  10.7 16.1 %copy-start.7 = (f32[27,27]{1,0:T(8,128)S(1)}, f32[27,27]{1,0:T(8,128)}, u32[]{:S(2)}) copy-start(f32[27,27]{1,0:T(8,128)} %mid_ref) | copy-start | bytes 8752
  10.7 16.1 %copy-start.8 = (f32[8,8]{1,0:T(8,128)S(1)}, f32[8,8]{1,0:T(8,128)}, u32[]{:S(2)}) copy-start(f32[8,8]{1,0:T(8,128)} %coarse_ref) | copy-start | bytes 772
  10.7 35.3 %all-to-all-start = ((f32[544,2,128]{2,1,0:T(2,128)}), f32[544,2,128]{2,1,0:T(2,128)S(1)}, u32[]{:S(2)}, u32[]{:S(2)}) async-start(f32[544,2,128]{2,1,0:T(2,128)} %bitcast.3), calls=%async_computation | async-start | bytes 1114112 | tf_op jit(solution)/shard_map/all_to_all | solution.py:611
  26.8 23.0 %copy-start = (bf16[4,128,256]{2,1,0:T(8,128)(2,1)S(1)}, bf16[4,128,256]{2,1,0:T(8,128)(2,1)}, u32[]{:S(2)}) copy-start(bf16[4,128,256]{2,1,0:T(8,128)(2,1)} %constant.51.clone.low_ref) | copy-start | bytes 786436
  26.8 23.0 %copy-start.1 = (bf16[4,128,256]{2,1,0:T(8,128)(2,1)S(1)}, bf16[4,128,256]{2,1,0:T(8,128)(2,1)}, u32[]{:S(2)}) copy-start(bf16[4,128,256]{2,1,0:T(8,128)(2,1)} %constant.50.clone.up_ref) | copy-start | bytes 786436
  26.9 23.0 %copy-start.2 = (bf16[4,128,256]{2,1,0:T(8,128)(2,1)S(1)}, bf16[4,128,256]{2,1,0:T(8,128)(2,1)}, u32[]{:S(2)}) copy-start(bf16[4,128,256]{2,1,0:T(8,128)(2,1)} %constant.49.clone.down_ref) | copy-start | bytes 786436
  26.9 23.0 %copy-start.4 = (bf16[128,256]{1,0:T(8,128)(2,1)S(1)}, bf16[128,256]{1,0:T(8,128)(2,1)}, u32[]{:S(2)}) copy-start(bf16[128,256]{1,0:T(8,128)(2,1)} %constant.52.clone.high_ref) | copy-start | bytes 196612
  46.0 3.8 %collective-permute-start.2 = (f32[1088,128]{1,0:T(8,128)S(1)}, f32[1088,128]{1,0:T(8,128)S(1)}, u32[]{:S(2)}, u32[]{:S(2)}) collective-permute-start(f32[1088,128]{1,0:T(8,128)S(1)} %bitcast.7), channel_id=1, source_target_pairs={{0,1},{1,0},{2,3},{3,2},{4,5},{5,4},{6,7},{7,6},{8,9},{9,8},{10,11... | collective-permute-start | bytes 1671176 | tf_op jit(solution)/shard_map/ppermute | solution.py:615

commit v6 on v5

--- a/solution.py
+++ b/solution.py
@@ -65,12 +65,13 @@
         table[:125, place * 32 : place * 32 + 27] = fine_mid
         down.append(halves(table))
         up.append(halves(table.T))
-    middle = np.zeros((LANES, LANES))
+    middle = np.zeros((LANES, LANES), np.float32)
     for place in range(EX):
-        middle[place * 32 : place * 32 + 27, place * 32 : place * 32 + 8] = mid_coarse
-    low = [halves(0.027 * middle)]
-    low += [halves(0.5 * np.dot(move, middle)) for move in exchanges(MID, True)]
-    return np.stack(down), np.stack(up), np.stack(low), halves(middle.T)
+        middle[place * 32 : place * 32 + 27, place * 8 : place * 8 + 8] = mid_coarse
+    low = [0.027 * middle]
+    low += [0.5 * np.dot(move, middle) for move in exchanges(MID, True)]
+    high = [np.roll(middle.T, 32 * copy, axis=0) for copy in range(3)]
+    return np.stack(down), np.stack(up), np.stack(low), np.stack(high)
 
 
 def iota(shape, dimension):
@@ -260,56 +261,74 @@
     return matrix
 
 
-def repeated(matrix):
+def exact(left, right):
+    return jnp.dot(left, right, precision=HIGHEST, preferred_element_type=f32)
+
+
+def repeated(matrix, width):
     lane, row = iota((LANES, LANES), 1), iota((LANES, LANES), 0)
-    pick = jnp.where((row % 32 == lane) & (lane < 32), 1.0, 0.0)
-    put = jnp.where((lane % 32 == row) & (row < 32), 1.0, 0.0)
-    tall = jnp.dot(pick, matrix, precision=HIGHEST, preferred_element_type=f32)
-    wide = jnp.dot(tall, put, precision=HIGHEST, preferred_element_type=f32)
-    return jnp.where(row // 32 == lane // 32, wide, 0.0)
-
-
-def moves(points, in_lanes):
+    used = (lane < EX * width) & (row < EX * width)
+    pick = jnp.where((row % width == lane) & (lane < width), 1.0, 0.0)
+    put = jnp.where((lane % width == row) & (row < width), 1.0, 0.0)
+    wide = exact(exact(pick, matrix), put)
+    return jnp.where(used & (row // width == lane // width), wide, 0.0)
+
+
+def moves(points, width):
     lane, row = iota((1, LANES), 1), iota((LANES, LANES), 0)
-    local, place = (lane % 32, lane // 32) if in_lanes else (lane, 0)
+    local, place = lane % width, lane // width
     tables = []
     for dimension, stride in enumerate((points * points, points, 1)):
         index = (local // stride) % points
         first = (index == 0) & (local < points**3)
         last = (index == points - 1) & (local < points**3)
         reach = (points - 1) * stride
-        if dimension == 0 and in_lanes:
+        if dimension == 0 and width < LANES:
             first, last = first & (place > 0), last & (place < EX - 1)
-            reach = reach - 32
-        source = jnp.where(first, lane + reach, jnp.where(last, lane - reach, -1))
-        tables.append(jnp.where(row == source, 1.0, 0.0))
+            reach = reach - width
+        source = jnp.where(first, lane + reach, jnp.where(last, lane - reach, -LANES))
+        tables.append((row, source))
     return tables
 
 
-def inverses_body(fine_ref, mid_ref, coarse_ref, out_ref, pad):
+def inverses_body(fine_ref, mid_ref, coarse_ref, low_ref, high_ref, out_ref, pad):
+    lane, row = iota((LANES, LANES), 1), iota((LANES, LANES), 0)
     coarse = invert(shifted_block(coarse_ref, pad, COARSE), 1)
     mid = invert(shifted_block(mid_ref, pad, MID), 2)
     fine = invert(shifted_block(fine_ref, pad, FINE), 8)
-    levels = ((fine, FINE), (repeated(mid), MID), (repeated(coarse), COARSE))
-    for level, (inverse, points) in enumerate(levels):
+    levels = ((fine, FINE, LANES), (repeated(mid, 32), MID, 32))
+    for level, (inverse, points, width) in enumerate(levels):
         inverse = 0.35 * inverse
         out_ref[4 * level] = two_way(inverse)
-        for dimension, move in enumerate(moves(points, points < FINE)):
-            moved = jnp.dot(move, inverse, precision=HIGHEST, preferred_element_type=f32)
-            out_ref[4 * level + 1 + dimension] = two_way(moved)
-
-
-def inverses(block_fine, block_mid, block_coarse):
+        moved = []
+        for dimension, (own, source) in enumerate(moves(points, width)):
+            moved.append(exact(jnp.where(own == source, 1.0, 0.0), inverse))
+            out_ref[4 * level + 1 + dimension] = two_way(moved[dimension])
+    lifted = 0.3 * high_ref[0]
+    for dimension in range(3):
+        lifted = lifted + exact(high_ref[dimension], moved[dimension])
+    out_ref[8] = two_way(lifted)
+    copies = jnp.where((lane % 32 == row) & (lane < 96), 1.0, 0.0)
+    inverse = exact(0.35 * repeated(coarse, 8), copies)
+    gather = jnp.zeros((LANES, LANES), f32)
+    for dimension, (own, source) in enumerate(moves(COARSE, 8)):
+        gather = gather + jnp.where((own == source + 32 * dimension) & (lane < 32), 1.0, 0.0)
+    out_ref[9] = two_way(exact(gather, inverse))
+    for part in range(4):
+        out_ref[10 + part] = two_way(exact(low_ref[part], 2.0 * inverse))
+
+
+def inverses(block_fine, block_mid, block_coarse, low, high):
     return pl.pallas_call(
         inverses_body,
-        out_shape=jax.ShapeDtypeStruct((12, LANES, 2 * LANES), bf16),
+        out_shape=jax.ShapeDtypeStruct((14, LANES, 2 * LANES), bf16),
         scratch_shapes=[pltpu.VMEM((LANES, LANES), f32)],
         compiler_params=pltpu.CompilerParams(vmem_limit_bytes=8 * MIB),
         cost_estimate=pl.CostEstimate(
             flops=2_000_000_000, bytes_accessed=20_000_000, transcendentals=0
         ),
         name="inverses",
-    )(block_fine, block_mid, block_coarse)
+    )(block_fine, block_mid, block_coarse, low, high)
 
 
 def two_way(values):
@@ -387,6 +406,26 @@
         return flat(jnp.where(from_before[None], before, after))
 
 
+def coarse_rows():
+    lane, row = iota((EY, LANES), 1), iota((EY, LANES), 0)
+    copy, j, k = lane // 32, (lane // 2) % 2, lane % 2
+    masks = (
+        copy == 0,
+        (copy == 1) & (j == 1) & (row > 0),
+        (copy == 1) & (j == 0) & (row < EY - 1),
+        (copy == 2) & (k == 1),
+        (copy == 2) & (k == 0),
+    )
+
+    def build(*parts):
+        result = 0.0
+        for mask, part in zip(masks, parts):
+            result = jnp.where(mask[None], flat_slabs(part), result)
+        return flat(result)
+
+    return build
+
+
 def flat_slabs(values):
     return values.reshape(-1, EY, LANES)
 
@@ -417,8 +456,6 @@
     tables_ref,
     down_ref,
     up_ref,
-    low_ref,
-    high_ref,
     out_ref,
     start,
     ping,
@@ -440,10 +477,10 @@
     mid_lefts = (mid_left_x, mid_left_y, mid_left_z)
     fine_faces = Faces(FINE, False)
     mid_faces = Faces(MID, True)
-    coarse_faces = Faces(COARSE, True)
+    coarse_row = coarse_rows()
     fine_table, *fine_tables = [tables_ref[i] for i in range(4)]
     mid_table, *mid_tables = [tables_ref[i] for i in range(4, 8)]
-    coarse_table, *coarse_tables = [tables_ref[i] for i in range(8, 12)]
+    lift_table, coarse_table, *low_tables = [tables_ref[i] for i in range(8, 14)]
 
     slab = iota((WINDOW, EY, LANES), 0)
     mask[...] = jnp.where((slab >= bounds_ref[0]) & (slab < bounds_ref[1]), 1.0, 0.0)
@@ -545,19 +582,39 @@
     odd = ping.at[2 * WINDOW : 3 * WINDOW]
     for c, d in cuts(6, WINDOW - 6):
         rows = at(0, c, d)
+        faces = mid_gather(mid_faces, mid_pong, c, d)
         values = [get(mid_left, rows)]
-        for ref, face in zip(mid_lefts, mid_gather(mid_faces, mid_pong, c, d)):
+        for ref, face in zip(mid_lefts, faces):
             values.append(get(ref, rows) + face)
-        low = times(values, *[low_ref[i] for i in range(4)]) * get(mask, rows)
-        put(base, rows, 2.0 * times((low,), coarse_table))
-    mid_sweep(coarse_faces, coarse_tables, base, base, even, 7)
-    mid_sweep(coarse_faces, coarse_tables, base, even, odd, 8)
-    mid_sweep(coarse_faces, coarse_tables, base, odd, even, 9)
-
-    for c, d in cuts(9, WINDOW - 9):
+        put(base, rows, times(values, *low_tables) * get(mask, rows))
+
+    for c, d in cuts(10, WINDOW - 10, CHUNK // 2):
         rows = at(0, c, d)
-        put(mid_pong, rows, get(mid_pong, rows) + times((get(even, rows),), high_ref[...]))
-    mid_sweep(mid_faces, mid_tables, mid_start, mid_pong, mid_ping, 10)
+        moved = times(mid_gather(mid_faces, mid_pong, c, d), *mid_tables)
+        put(mid_left, rows, 0.3 * get(mid_pong, rows) + get(mid_start, rows) + moved)
+
+    def coarse_gather(ref, a, b):
+        rows = at(0, a, b)
+        near = beside(ref, rows)
+        return coarse_row(
+            get(ref, rows), *near, get(ref, at(0, a - 1, b - 1)), get(ref, at(0, a + 1, b + 1))
+        )
+
+    def coarse_sweep(source, target, margin):
+        for c, d in cuts(margin, WINDOW - margin, CHUNK // 2):
+            rows = at(0, c, d)
+            moved = times((coarse_gather(source, c, d),), coarse_table)
+            moved = 0.3 * get(source, rows) + get(base, rows) + moved
+            put(target, rows, moved * get(mask, rows))
+
+    coarse_sweep(base, even, 7)
+    coarse_sweep(even, odd, 8)
+    coarse_sweep(odd, even, 9)
+
+    for c, d in cuts(10, WINDOW - 10, CHUNK // 2):
+        rows = at(0, c, d)
+        moved = get(mid_left, rows) + times((coarse_gather(even, c, d),), lift_table)
+        put(mid_ping, rows, moved * get(mask, rows))
     mid_sweep(mid_faces, mid_tables, mid_start, mid_ping, mid_pong, 11)
     mid_sweep(mid_faces, mid_tables, mid_start, mid_pong, mid_ping, 12)
 
@@ -577,19 +634,19 @@
                 out_ref[pl.ds(first, HALF, stride=2 * OWN), :] = values
 
 
-def cycle(bounds, mine, other, tables, down, up, low, high):
+def cycle(bounds, mine, other, tables, down, up):
     big = pltpu.VMEM((EX * WINDOW, EY, LANES), f32)
     small = pltpu.VMEM((WINDOW, EY, LANES), f32)
     vmem = pl.BlockSpec(memory_space=pltpu.VMEM)
     return pl.pallas_call(
         cycle_body,
         out_shape=jax.ShapeDtypeStruct((EX * HALF * 2 * OWN, LANES), f32),
-        in_specs=[pl.BlockSpec(memory_space=pltpu.SMEM)] + [vmem] * 7,
+        in_specs=[pl.BlockSpec(memory_space=pltpu.SMEM)] + [vmem] * 5,
         out_specs=vmem,
         scratch_shapes=[big] * 7 + [small] * 8,
         compiler_params=pltpu.CompilerParams(vmem_limit_bytes=20 * MIB),
         name="cycle",
-    )(bounds, mine, other, tables, down, up, low, high)
+    )(bounds, mine, other, tables, down, up)
 
 
 def per_device(fine_source_field, scaling, block_fine, block_mid, block_coarse):
@@ -611,7 +668,7 @@
     recv = lax.all_to_all(
         chunks.reshape(parts * WINDOW // 2, 2, LANES), ("gx", "gy"), 0, 0, tiled=True
     ).reshape(parts * WINDOW, LANES)
-    recv, tables = lax.optimization_barrier((recv, inverses(*matrices)))
+    recv, tables = lax.optimization_barrier((recv, inverses(*matrices, low, high)))
     other = lax.ppermute(recv, "gz", pairs)
 
     part = lax.axis_index("gx") * lax.axis_size("gy") + lax.axis_index("gy")
@@ -620,7 +677,7 @@
         [jnp.maximum(0, -first), jnp.minimum(WINDOW, groups * count_z - first), core]
     )
     result = cycle(
-        bounds.astype(jnp.int32), recv, other, tables, down, up, low, high
+        bounds.astype(jnp.int32), recv, other, tables, down, up
     )
     back = lax.all_to_all(
         result.reshape(parts, 2 * OWN, LANES), ("gx", "gy"), 0, 0, tiled=True

time: 77.9 us -> 77.1 us (0.990)
    pallas_call x1, Pallas kernels: 7.69 us -> 6.91 us  [cycle(): pl.pallas_call(cycle_body, out_shape=jax.ShapeDtypeStruct((EX * HALF * 2...]
  transfers between devices with their start and end apart: 4 -> 4, of which waited for: 3 -> 3; matrix products, arithmetic and copies ran while one was open for 0% -> 0% of each run, Pallas kernels for 11% -> 12%
where the time goes in v6:
time: 77.1 us; the launch traced here: 76.8 us
  starting transfers between devices  23.5 us (30%)
  blocking collectives  18.9 us (25%)
  Pallas kernels  18.8 us (24%)
  waiting for transfers between devices  13.8 us (18%)
  local copies, waits for them, and re-layouts  1.61 us (2%)
    all_to_all x1, blocking collectives, per_device(): lax.all_to_all(result.reshape(parts, 2 * OWN, LANES), ('gx', 'gy'), 0, 0,...  18.9 us
    all_to_all x1, starting transfers between devices, per_device(): lax.all_to_all(chunks.reshape(parts * WINDOW // 2, 2, LANES), ('gx', 'gy'...  16.1 us
    pallas_call x1, Pallas kernels, inverses(): pl.pallas_call(inverses_body, out_shape=jax.ShapeDtypeStruct((14, LANES,...  9.56 us
    all_to_all x1, waiting for transfers between devices, per_device(): lax.all_to_all(chunks.reshape(parts * WINDOW // 2, 2, LANES), ('gx', 'gy'...  9.54 us
    pallas_call x1, Pallas kernels, cycle(): pl.pallas_call(cycle_body, out_shape=jax.ShapeDtypeStruct((EX * HALF * 2...  6.91 us
    ppermute x1, starting transfers between devices, per_device(): halo = lax.ppermute(edge, 'gz', ties + [(j, i) for i, j in ties])  3.56 us
    ppermute x1, waiting for transfers between devices, per_device(): halo = lax.ppermute(edge, 'gz', ties + [(j, i) for i, j in ties])  2.39 us
    ppermute x1, starting transfers between devices, per_device(): sibling = lax.ppermute(own, 'gz', pairs)  1.92 us
  transfers between devices with their start and end apart: 4, of which 3 were waited for; matrix products, arithmetic and copies ran while one was open for 0% of the time, Pallas kernels for 12%

profile of v6, /device:TPU:4, one launch (start us, length us, event | category | flops | bytes accessed | tf_op | source)
XLA Modules:
  0.0 76.8 jit_solution(9246690453575844336)
XLA Ops:
  0.0 0.0 copy-start.3
  0.0 0.7 copy-done.3
  0.7 0.0 copy-start.2
  0.7 0.9 %copy-done.2 = f32[5,10,320]{2,1,0:T(8,128)S(1)} copy-done((f32[5,10,320]{2,1,0:T(8,128)S(1)}, f32[5,10,320]{2,1,0:T(8,128)}, u32[]{:S(2)}) %copy-start.2) | copy-done | bytes 64024
  1.6 0.3 pack.1
  1.9 1.9 %collective-permute-start = (f32[2,64,128]{2,1,0:T(8,128)S(1)}, f32[2,64,128]{2,1,0:T(8,128)S(1)}, u32[]{:S(2)}, u32[]{:S(2)}) collective-permute-start(f32[2,64,128]{2,1,0:T(8,128)S(1)} %get-tuple-element.13.refs_1_), channel_id=1, source_target_pairs={{0,1},{1,0},{2,3},{3,2},{4,5},{5,4},{6,7},{7,6},{8,9},{9,8},{10,11... | collective-permute-start | bytes 196616 | tf_op jit(solution)/shard_map/ppermute | solution.py:665
  3.9 3.6 %collective-permute-start.1 = (f32[2,16,128]{2,1,0:T(8,128)S(1)}, f32[2,16,128]{2,1,0:T(8,128)S(1)}, u32[]{:S(2)}, u32[]{:S(2)}) collective-permute-start(f32[2,16,128]{2,1,0:T(8,128)S(1)} %get-tuple-element.14), channel_id=1, source_target_pairs={{1,2},{3,4},{5,6},{7,8},{9,10},{11,12},{13,14},{2,1},{4,3},{6,5},{... | collective-permute-start | bytes 49160 | tf_op jit(solution)/shard_map/ppermute | solution.py:664
  7.4 2.4 %collective-permute-done.1.refs_3_ = f32[2,16,128]{2,1,0:T(8,128)S(1)} collective-permute-done((f32[2,16,128]{2,1,0:T(8,128)S(1)}, f32[2,16,128]{2,1,0:T(8,128)S(1)}, u32[]{:S(2)}, u32[]{:S(2)}) %collective-permute-start.1) | collective-permute-done | bytes 16416 | tf_op jit(solution)/shard_map/ppermute | solution.py:664
  9.8 0.0 collective-permute-done.refs_2_
  9.8 0.9 %window.1 = f32[1088,128]{1,0:T(8,128)} custom-call(s32[1]{0:T(128)} %bitcast.refs_0_, f32[2,64,128]{2,1,0:T(8,128)S(1)} %get-tuple-element.13.refs_1_, f32[2,64,128]{2,1,0:T(8,128)S(1)} %collective-permute-done.refs_2_, f32[2,16,128]{2,1,0:T(8,128)S(1)} %collective-permute-done.1.refs_3_), custom_call_target="tpu_custom_call" | custom-call | tf_op jit(solution)/shard_map/window/pallas_call | solution.py:161
  10.7 0.0 copy-start.4
  10.7 0.0 copy-start.5
  10.7 0.0 copy-start.6
  10.7 0.0 copy-start.7
  10.7 0.0 copy-start.8
  10.7 16.1 %all-to-all-start = ((f32[544,2,128]{2,1,0:T(2,128)}), f32[544,2,128]{2,1,0:T(2,128)S(1)}, u32[]{:S(2)}, u32[]{:S(2)}) async-start(f32[544,2,128]{2,1,0:T(2,128)} %bitcast.3), calls=%async_computation | async-start | bytes 1114112 | tf_op jit(solution)/shard_map/all_to_all | solution.py:668
  26.8 0.0 copy-done.4
  26.8 0.0 copy-done.5
  26.8 0.0 copy-done.6
  26.9 0.0 copy-done.7
  26.9 0.0 copy-done.8
  26.9 0.0 copy-start
  26.9 0.0 copy-start.1
  26.9 9.6 %inverses.1.tables_ref = bf16[14,128,256]{2,1,0:T(8,128)(2,1)S(1)} custom-call(f32[125,125]{1,0:T(8,128)S(1)} %copy-done.4, f32[27,27]{1,0:T(8,128)S(1)} %copy-done.5, f32[8,8]{1,0:T(8,128)S(1)} %copy-done.6, f32[4,128,128]{2,1,0:T(8,128)S(1)} %copy-done.7, f32[3,128,128]{2,1,0:T(8,128)S(1)} %copy-done.8), custom_call_target="tpu_custom_call" | custom-call | flops 2000000000 | bytes 20000000 | tf_op jit(solution)/shard_map/inverses/pallas_call | solution.py:322
  36.5 9.5 %all-to-all-done = f32[544,2,128]{2,1,0:T(2,128)S(1)} async-done(((f32[544,2,128]{2,1,0:T(2,128)}), f32[544,2,128]{2,1,0:T(2,128)S(1)}, u32[]{:S(2)}, u32[]{:S(2)}) %all-to-all-start) | async-done | bytes 557088 | tf_op jit(solution)/shard_map/all_to_all | solution.py:668
  46.0 1.9 %collective-permute-start.2 = (f32[1088,128]{1,0:T(8,128)S(1)}, f32[1088,128]{1,0:T(8,128)S(1)}, u32[]{:S(2)}, u32[]{:S(2)}) collective-permute-start(f32[1088,128]{1,0:T(8,128)S(1)} %bitcast.7), channel_id=1, source_target_pairs={{0,1},{1,0},{2,3},{3,2},{4,5},{5,4},{6,7},{7,6},{8,9},{9,8},{10,11... | collective-permute-start | bytes 1671176 | tf_op jit(solution)/shard_map/ppermute | solution.py:672
  47.9 0.1 pad_add_fusion.bounds_ref
  48.0 1.8 %collective-permute-done.2.other_ref = f32[1088,128]{1,0:T(8,128)S(1)} collective-permute-done((f32[1088,128]{1,0:T(8,128)S(1)}, f32[1088,128]{1,0:T(8,128)S(1)}, u32[]{:S(2)}, u32[]{:S(2)}) %collective-permute-start.2) | collective-permute-done | bytes 557088 | tf_op jit(solution)/shard_map/ppermute | solution.py:672
  49.9 0.0 copy-done
  49.9 0.0 copy-done.1
  49.9 6.9 %cycle.1 = f32[256,128]{1,0:T(8,128)S(1)} custom-call(s32[3]{0:T(128)S(1)} %pad_add_fusion.bounds_ref, f32[1088,128]{1,0:T(8,128)S(1)} %bitcast.8, f32[1088,128]{1,0:T(8,128)S(1)} %collective-permute-done.2.other_ref, bf16[14,128,256]{2,1,0:T(8,128)(2,1)S(1)} %inverses.1.tables_ref, bf16[4,128,256]{2,1,0:T(8,128)(2,1)S(1)} %copy-done.1, ...), custom_call_target="tpu_custom_call" | custom-call | tf_op jit(solution)/shard_map/cycle/pallas_call | solution.py:641
  56.8 18.9 %all_to_all.10 = f32[32,8,128]{2,1,0:T(8,128)S(1)} all-to-all(f32[32,8,128]{2,1,0:T(8,128)S(1)} %bitcast.9), channel_id=1, replica_groups=mesh['gx'=4,'gy'=8,'gz'=16] {'gx','gy'}, dimensions={0} | all-to-all | bytes 262144 | tf_op jit(solution)/shard_map/all_to_all | solution.py:682
  75.7 1.1 %unpack.1 = f32[5,10,320]{2,1,0:T(8,128)} custom-call(s32[1]{0:T(128)} %bitcast.refs_0_, f32[256,128]{1,0:T(8,128)S(1)} %bitcast.10, f32[1,2,64]{2,1,0:T(2,128)S(1)} %copy-done.3), custom_call_target="tpu_custom_call" | custom-call | tf_op jit(solution)/shard_map/unpack/pallas_call | solution.py:209
Async XLA Ops:
  0.0 0.7 copy-start.3
  0.7 0.9 %copy-start.2 = (f32[5,10,320]{2,1,0:T(8,128)S(1)}, f32[5,10,320]{2,1,0:T(8,128)}, u32[]{:S(2)}) copy-start(f32[5,10,320]{2,1,0:T(8,128)} %refs_1_.1) | copy-start | bytes 192004
  1.9 7.9 %collective-permute-start = (f32[2,64,128]{2,1,0:T(8,128)S(1)}, f32[2,64,128]{2,1,0:T(8,128)S(1)}, u32[]{:S(2)}, u32[]{:S(2)}) collective-permute-start(f32[2,64,128]{2,1,0:T(8,128)S(1)} %get-tuple-element.13.refs_1_), channel_id=1, source_target_pairs={{0,1},{1,0},{2,3},{3,2},{4,5},{5,4},{6,7},{7,6},{8,9},{9,8},{10,11... | collective-permute-start | bytes 196616 | tf_op jit(solution)/shard_map/ppermute | solution.py:665
  3.9 6.0 %collective-permute-start.1 = (f32[2,16,128]{2,1,0:T(8,128)S(1)}, f32[2,16,128]{2,1,0:T(8,128)S(1)}, u32[]{:S(2)}, u32[]{:S(2)}) collective-permute-start(f32[2,16,128]{2,1,0:T(8,128)S(1)} %get-tuple-element.14), channel_id=1, source_target_pairs={{1,2},{3,4},{5,6},{7,8},{9,10},{11,12},{13,14},{2,1},{4,3},{6,5},{... | collective-permute-start | bytes 49160 | tf_op jit(solution)/shard_map/ppermute | solution.py:664
  10.7 16.1 %copy-start.4 = (f32[125,125]{1,0:T(8,128)S(1)}, f32[125,125]{1,0:T(8,128)}, u32[]{:S(2)}) copy-start(f32[125,125]{1,0:T(8,128)} %fine_ref) | copy-start | bytes 187504
  10.7 16.2 %copy-start.5 = (f32[27,27]{1,0:T(8,128)S(1)}, f32[27,27]{1,0:T(8,128)}, u32[]{:S(2)}) copy-start(f32[27,27]{1,0:T(8,128)} %mid_ref) | copy-start | bytes 8752
  10.7 16.2 %copy-start.6 = (f32[8,8]{1,0:T(8,128)S(1)}, f32[8,8]{1,0:T(8,128)}, u32[]{:S(2)}) copy-start(f32[8,8]{1,0:T(8,128)} %coarse_ref) | copy-start | bytes 772
  10.7 16.2 %copy-start.7 = (f32[4,128,128]{2,1,0:T(8,128)S(1)}, f32[4,128,128]{2,1,0:T(8,128)}, u32[]{:S(2)}) copy-start(f32[4,128,128]{2,1,0:T(8,128)} %constant.49.clone.low_ref) | copy-start | bytes 786436
  10.7 16.2 %copy-start.8 = (f32[3,128,128]{2,1,0:T(8,128)S(1)}, f32[3,128,128]{2,1,0:T(8,128)}, u32[]{:S(2)}) copy-start(f32[3,128,128]{2,1,0:T(8,128)} %constant.50.clone.high_ref) | copy-start | bytes 589828
  10.7 35.3 %all-to-all-start = ((f32[544,2,128]{2,1,0:T(2,128)}), f32[544,2,128]{2,1,0:T(2,128)S(1)}, u32[]{:S(2)}, u32[]{:S(2)}) async-start(f32[544,2,128]{2,1,0:T(2,128)} %bitcast.3), calls=%async_computation | async-start | bytes 1114112 | tf_op jit(solution)/shard_map/all_to_all | solution.py:668
  26.9 23.0 %copy-start = (bf16[4,128,256]{2,1,0:T(8,128)(2,1)S(1)}, bf16[4,128,256]{2,1,0:T(8,128)(2,1)}, u32[]{:S(2)}) copy-start(bf16[4,128,256]{2,1,0:T(8,128)(2,1)} %constant.52.clone.up_ref) | copy-start | bytes 786436
  26.9 23.0 %copy-start.1 = (bf16[4,128,256]{2,1,0:T(8,128)(2,1)S(1)}, bf16[4,128,256]{2,1,0:T(8,128)(2,1)}, u32[]{:S(2)}) copy-start(bf16[4,128,256]{2,1,0:T(8,128)(2,1)} %constant.51.clone.down_ref) | copy-start | bytes 786436
  46.0 3.8 %collective-permute-start.2 = (f32[1088,128]{1,0:T(8,128)S(1)}, f32[1088,128]{1,0:T(8,128)S(1)}, u32[]{:S(2)}, u32[]{:S(2)}) collective-permute-start(f32[1088,128]{1,0:T(8,128)S(1)} %bitcast.7), channel_id=1, source_target_pairs={{0,1},{1,0},{2,3},{3,2},{4,5},{5,4},{6,7},{7,6},{8,9},{9,8},{10,11... | collective-permute-start | bytes 1671176 | tf_op jit(solution)/shard_map/ppermute | solution.py:672

commit v7 on v6

--- a/solution.py
+++ b/solution.py
@@ -136,24 +136,37 @@
     )(core, field, scaling)
 
 
-def window_body(core_ref, own_ref, sibling_ref, halo_ref, out_ref, line, *, parts):
+def starts(core, parts):
+    first = HALO - RADIUS if core == 0 else HALO + SPLIT - RADIUS
+    return [first + OWN * part for part in parts]
+
+
+def lay(line, core, count_z, own_ref, sibling_ref):
+    own_at, sibling_at = (HALO, HALO + count_z) if core == 0 else (HALO + count_z, HALO)
+    line[:, own_at : own_at + count_z, :] = own_ref[...]
+    line[:, sibling_at : sibling_at + count_z, :] = sibling_ref[...]
+
+
+def cut(line, core, parts, out_ref):
+    for row, start in enumerate(starts(core, parts)):
+        for y in range(2):
+            place = row * WINDOW + y * SPLIT
+            out_ref[place : place + SPLIT, :] = line[y, start : start + SPLIT, :]
+
+
+def window_body(core_ref, own_ref, sibling_ref, out_ref, line, *, parts):
     count_z = own_ref.shape[1]
+    line[:, 0:HALO, :] = jnp.zeros((2, HALO, LANES), f32)
+    line[:, HALO + 2 * count_z :, :] = jnp.zeros((2, HALO, LANES), f32)
     for core in range(2):
-        places = (HALO, HALO + count_z, 0) if core == 0 else (count_z, 0, 2 * count_z)
 
         @pl.when(core_ref[0] == core)
-        def _(core=core, places=places):
-            for ref, place in zip((own_ref, sibling_ref, halo_ref), places):
-                line[:, place : place + ref.shape[1], :] = ref[...]
-            first = HALO - RADIUS if core == 0 else SPLIT - RADIUS
-            for part in range(parts):
-                for y in range(2):
-                    start = first + OWN * part
-                    row = part * WINDOW + y * SPLIT
-                    out_ref[row : row + SPLIT, :] = line[y, start : start + SPLIT, :]
-
-
-def window(core, own, sibling, halo, parts):
+        def _(core=core):
+            lay(line, core, count_z, own_ref, sibling_ref)
+            cut(line, core, range(parts), out_ref)
+
+
+def window(core, own, sibling, parts):
     def body(*refs):
         window_body(*refs, parts=parts)
 
@@ -161,12 +174,54 @@
     return pl.pallas_call(
         body,
         out_shape=jax.ShapeDtypeStruct((parts * WINDOW, LANES), f32),
-        in_specs=[pl.BlockSpec(memory_space=pltpu.SMEM), vmem, vmem, vmem],
+        in_specs=[pl.BlockSpec(memory_space=pltpu.SMEM), vmem, vmem],
         out_specs=vmem,
-        scratch_shapes=[pltpu.VMEM((2, 2 * own.shape[1] + HALO, LANES), f32)],
+        scratch_shapes=[pltpu.VMEM((2, 2 * own.shape[1] + 2 * HALO, LANES), f32)],
         compiler_params=pltpu.CompilerParams(vmem_limit_bytes=8 * MIB),
         name="window",
-    )(core, own, sibling, halo)
+    )(core, own, sibling)
+
+
+ENDS = 4
+
+
+def ends_body(core_ref, own_ref, sibling_ref, halo_ref, _, out_ref, line, block, sem, *, parts):
+    count_z = own_ref.shape[1]
+    for core in range(2):
+
+        @pl.when(core_ref[0] == core)
+        def _(core=core):
+            lay(line, core, count_z, own_ref, sibling_ref)
+            halo_at = 0 if core == 0 else HALO + 2 * count_z
+            line[:, halo_at : halo_at + HALO, :] = halo_ref[...]
+            first = 0 if core == 0 else parts - ENDS
+            cut(line, core, range(first, first + ENDS), block)
+            place = out_ref.at[first * WINDOW : (first + ENDS) * WINDOW, :]
+            copy = pltpu.make_async_copy(block, place, sem)
+            copy.start()
+            copy.wait()
+
+
+def ends(core, own, sibling, halo, chunks, parts):
+    def body(*refs):
+        ends_body(*refs, parts=parts)
+
+    vmem = pl.BlockSpec(memory_space=pltpu.VMEM)
+    anywhere = pl.BlockSpec(memory_space=pl.ANY)
+    return pl.pallas_call(
+        body,
+        out_shape=jax.ShapeDtypeStruct(chunks.shape, f32),
+        in_specs=[pl.BlockSpec(memory_space=pltpu.SMEM), vmem, vmem, vmem, anywhere],
+        out_specs=anywhere,
+        scratch_shapes=[
+            pltpu.VMEM((2, 2 * own.shape[1] + 2 * HALO, LANES), f32),
+            pltpu.VMEM((ENDS * WINDOW, LANES), f32),
+            pltpu.SemaphoreType.DMA,
+        ],
+        input_output_aliases={4: 0},
+        compiler_params=pltpu.CompilerParams(vmem_limit_bytes=8 * MIB),
+        name="ends",
+    )(core, own, sibling, halo, chunks)
 
 
 def unpack_body(core_ref, back_ref, scale_ref, out_ref, turned, *, count_z):
@@ -663,7 +718,8 @@
     pairs = [(i, i ^ 1) for i in range(groups)]
     halo = lax.ppermute(edge, "gz", ties + [(j, i) for i, j in ties])
     sibling = lax.ppermute(own, "gz", pairs)
-    chunks = window(cores, own, sibling, halo, parts)
+    chunks = window(cores, own, sibling, parts)
+    chunks = ends(cores, own, sibling, halo, chunks, parts)
     chunks, *matrices = lax.optimization_barrier((chunks, block_fine, block_mid, block_coarse))
     recv = lax.all_to_all(
         chunks.reshape(parts * WINDOW // 2, 2, LANES), ("gx", "gy"), 0, 0, tiled=True

time: 77.1 us -> 76.9 us (level)
  waiting for transfers between devices: 13.8 us -> 12.9 us
    ppermute x1, waiting for transfers between devices: 2.39 us -> 1.5 us  [per_device(): halo = lax.ppermute(edge, 'gz', ties + [(j, i) for i, j in ties])]
  transfers between devices with their start and end apart: 4 -> 4, of which waited for: 3 -> 3; matrix products, arithmetic and copies ran while one was open for 0% -> 0% of each run, Pallas kernels for 12% -> 14%
where the time goes in v7:
time: 76.9 us; the launch traced here: 76.6 us
  starting transfers between devices  23.5 us (31%)
  Pallas kernels  19.5 us (25%)
  blocking collectives  18.9 us (25%)
  waiting for transfers between devices  12.9 us (17%)
  local copies, waits for them, and re-layouts  1.63 us (2%)
    all_to_all x1, blocking collectives, per_device(): lax.all_to_all(result.reshape(parts, 2 * OWN, LANES), ('gx', 'gy'), 0, 0,...  18.9 us
    all_to_all x1, starting transfers between devices, per_device(): lax.all_to_all(chunks.reshape(parts * WINDOW // 2, 2, LANES), ('gx', 'gy'...  16.1 us
    all_to_all x1, waiting for transfers between devices, per_device(): lax.all_to_all(chunks.reshape(parts * WINDOW // 2, 2, LANES), ('gx', 'gy'...  9.57 us
    pallas_call x1, Pallas kernels, inverses(): pl.pallas_call(inverses_body, out_shape=jax.ShapeDtypeStruct((14, LANES,...  9.56 us
    pallas_call x1, Pallas kernels, cycle(): pl.pallas_call(cycle_body, out_shape=jax.ShapeDtypeStruct((EX * HALF * 2...  6.92 us
    ppermute x1, starting transfers between devices, per_device(): halo = lax.ppermute(edge, 'gz', ties + [(j, i) for i, j in ties])  3.56 us
    ppermute x1, starting transfers between devices, per_device(): sibling = lax.ppermute(own, 'gz', pairs)  1.92 us
    ppermute x1, starting transfers between devices, per_device(): other = lax.ppermute(recv, 'gz', pairs)  1.91 us
  transfers between devices with their start and end apart: 4, of which 3 were waited for; matrix products, arithmetic and copies ran while one was open for 0% of the time, Pallas kernels for 14%

profile of v7, /device:TPU:4, one launch (start us, length us, event | category | flops | bytes accessed | tf_op | source)
XLA Modules:
  0.0 76.6 jit_solution(12957902748085513774)
XLA Ops:
  0.0 0.0 copy-start.3
  0.0 0.7 copy-done.3
  0.7 0.0 copy-start.2
  0.7 0.9 %copy-done.2 = f32[5,10,320]{2,1,0:T(8,128)S(1)} copy-done((f32[5,10,320]{2,1,0:T(8,128)S(1)}, f32[5,10,320]{2,1,0:T(8,128)}, u32[]{:S(2)}) %copy-start.2) | copy-done | bytes 64024
  1.6 0.3 pack.1
  1.9 1.9 %collective-permute-start = (f32[2,64,128]{2,1,0:T(8,128)S(1)}, f32[2,64,128]{2,1,0:T(8,128)S(1)}, u32[]{:S(2)}, u32[]{:S(2)}) collective-permute-start(f32[2,64,128]{2,1,0:T(8,128)S(1)} %get-tuple-element.13.refs_1_), channel_id=1, source_target_pairs={{0,1},{1,0},{2,3},{3,2},{4,5},{5,4},{6,7},{7,6},{8,9},{9,8},{10,11... | collective-permute-start | bytes 196616 | tf_op jit(solution)/shard_map/ppermute | solution.py:720
  3.9 3.6 %collective-permute-start.1 = (f32[2,16,128]{2,1,0:T(8,128)S(1)}, f32[2,16,128]{2,1,0:T(8,128)S(1)}, u32[]{:S(2)}, u32[]{:S(2)}) collective-permute-start(f32[2,16,128]{2,1,0:T(8,128)S(1)} %get-tuple-element.14), channel_id=1, source_target_pairs={{1,2},{3,4},{5,6},{7,8},{9,10},{11,12},{13,14},{2,1},{4,3},{6,5},{... | collective-permute-start | bytes 49160 | tf_op jit(solution)/shard_map/ppermute | solution.py:719
  7.4 0.0 collective-permute-done.refs_2_
  7.4 0.9 %window.1.refs_4_ = f32[1088,128]{1,0:T(8,128)} custom-call(s32[1]{0:T(128)} %bitcast.refs_0_, f32[2,64,128]{2,1,0:T(8,128)S(1)} %get-tuple-element.13.refs_1_, f32[2,64,128]{2,1,0:T(8,128)S(1)} %collective-permute-done.refs_2_), custom_call_target="tpu_custom_call" | custom-call | tf_op jit(solution)/shard_map/window/pallas_call | solution.py:174
  8.3 1.5 %collective-permute-done.1.refs_3_ = f32[2,16,128]{2,1,0:T(8,128)S(1)} collective-permute-done((f32[2,16,128]{2,1,0:T(8,128)S(1)}, f32[2,16,128]{2,1,0:T(8,128)S(1)}, u32[]{:S(2)}, u32[]{:S(2)}) %collective-permute-start.1) | collective-permute-done | bytes 16416 | tf_op jit(solution)/shard_map/ppermute | solution.py:719
  9.8 0.6 ends.1
  10.5 0.0 copy-start.4
  10.5 0.0 copy-start.5
  10.5 0.0 copy-start.6
  10.5 0.0 copy-start.7
  10.5 0.0 copy-start.8
  10.5 16.1 %all-to-all-start = ((f32[544,2,128]{2,1,0:T(2,128)}), f32[544,2,128]{2,1,0:T(2,128)S(1)}, u32[]{:S(2)}, u32[]{:S(2)}) async-start(f32[544,2,128]{2,1,0:T(2,128)} %bitcast.3), calls=%async_computation | async-start | bytes 1114112 | tf_op jit(solution)/shard_map/all_to_all | solution.py:724
  26.6 0.0 copy-done.4
  26.6 0.0 copy-done.5
  26.7 0.0 copy-done.6
  26.7 0.0 copy-done.7
  26.7 0.0 copy-done.8
  26.7 0.0 copy-start
  26.7 0.0 copy-start.1
  26.7 9.6 %inverses.1.tables_ref = bf16[14,128,256]{2,1,0:T(8,128)(2,1)S(1)} custom-call(f32[125,125]{1,0:T(8,128)S(1)} %copy-done.4, f32[27,27]{1,0:T(8,128)S(1)} %copy-done.5, f32[8,8]{1,0:T(8,128)S(1)} %copy-done.6, f32[4,128,128]{2,1,0:T(8,128)S(1)} %copy-done.7, f32[3,128,128]{2,1,0:T(8,128)S(1)} %copy-done.8), custom_call_target="tpu_custom_call" | custom-call | flops 2000000000 | bytes 20000000 | tf_op jit(solution)/shard_map/inverses/pallas_call | solution.py:377
  36.3 9.6 %all-to-all-done = f32[544,2,128]{2,1,0:T(2,128)S(1)} async-done(((f32[544,2,128]{2,1,0:T(2,128)}), f32[544,2,128]{2,1,0:T(2,128)S(1)}, u32[]{:S(2)}, u32[]{:S(2)}) %all-to-all-start) | async-done | bytes 557088 | tf_op jit(solution)/shard_map/all_to_all | solution.py:724
  45.8 1.9 %collective-permute-start.2 = (f32[1088,128]{1,0:T(8,128)S(1)}, f32[1088,128]{1,0:T(8,128)S(1)}, u32[]{:S(2)}, u32[]{:S(2)}) collective-permute-start(f32[1088,128]{1,0:T(8,128)S(1)} %bitcast.7), channel_id=1, source_target_pairs={{0,1},{1,0},{2,3},{3,2},{4,5},{5,4},{6,7},{7,6},{8,9},{9,8},{10,11... | collective-permute-start | bytes 1671176 | tf_op jit(solution)/shard_map/ppermute | solution.py:728
  47.8 0.1 pad_add_fusion.bounds_ref
  47.9 1.8 %collective-permute-done.2.other_ref = f32[1088,128]{1,0:T(8,128)S(1)} collective-permute-done((f32[1088,128]{1,0:T(8,128)S(1)}, f32[1088,128]{1,0:T(8,128)S(1)}, u32[]{:S(2)}, u32[]{:S(2)}) %collective-permute-start.2) | collective-permute-done | bytes 557088 | tf_op jit(solution)/shard_map/ppermute | solution.py:728
  49.7 0.0 copy-done
  49.7 0.0 copy-done.1
  49.7 6.9 %cycle.1 = f32[256,128]{1,0:T(8,128)S(1)} custom-call(s32[3]{0:T(128)S(1)} %pad_add_fusion.bounds_ref, f32[1088,128]{1,0:T(8,128)S(1)} %bitcast.8, f32[1088,128]{1,0:T(8,128)S(1)} %collective-permute-done.2.other_ref, bf16[14,128,256]{2,1,0:T(8,128)(2,1)S(1)} %inverses.1.tables_ref, bf16[4,128,256]{2,1,0:T(8,128)(2,1)S(1)} %copy-done.1, ...), custom_call_target="tpu_custom_call" | custom-call | tf_op jit(solution)/shard_map/cycle/pallas_call | solution.py:696
  56.6 18.9 %all_to_all.10 = f32[32,8,128]{2,1,0:T(8,128)S(1)} all-to-all(f32[32,8,128]{2,1,0:T(8,128)S(1)} %bitcast.9), channel_id=1, replica_groups=mesh['gx'=4,'gy'=8,'gz'=16] {'gx','gy'}, dimensions={0} | all-to-all | bytes 262144 | tf_op jit(solution)/shard_map/all_to_all | solution.py:738
  75.5 1.1 %unpack.1 = f32[5,10,320]{2,1,0:T(8,128)} custom-call(s32[1]{0:T(128)} %bitcast.refs_0_, f32[256,128]{1,0:T(8,128)S(1)} %bitcast.10, f32[1,2,64]{2,1,0:T(2,128)S(1)} %copy-done.3), custom_call_target="tpu_custom_call" | custom-call | tf_op jit(solution)/shard_map/unpack/pallas_call | solution.py:264
Async XLA Ops:
  0.0 0.7 copy-start.3
  0.7 0.9 %copy-start.2 = (f32[5,10,320]{2,1,0:T(8,128)S(1)}, f32[5,10,320]{2,1,0:T(8,128)}, u32[]{:S(2)}) copy-start(f32[5,10,320]{2,1,0:T(8,128)} %refs_1_.1) | copy-start | bytes 192004
  1.9 5.5 %collective-permute-start = (f32[2,64,128]{2,1,0:T(8,128)S(1)}, f32[2,64,128]{2,1,0:T(8,128)S(1)}, u32[]{:S(2)}, u32[]{:S(2)}) collective-permute-start(f32[2,64,128]{2,1,0:T(8,128)S(1)} %get-tuple-element.13.refs_1_), channel_id=1, source_target_pairs={{0,1},{1,0},{2,3},{3,2},{4,5},{5,4},{6,7},{7,6},{8,9},{9,8},{10,11... | collective-permute-start | bytes 196616 | tf_op jit(solution)/shard_map/ppermute | solution.py:720
  3.9 6.0 %collective-permute-start.1 = (f32[2,16,128]{2,1,0:T(8,128)S(1)}, f32[2,16,128]{2,1,0:T(8,128)S(1)}, u32[]{:S(2)}, u32[]{:S(2)}) collective-permute-start(f32[2,16,128]{2,1,0:T(8,128)S(1)} %get-tuple-element.14), channel_id=1, source_target_pairs={{1,2},{3,4},{5,6},{7,8},{9,10},{11,12},{13,14},{2,1},{4,3},{6,5},{... | collective-permute-start | bytes 49160 | tf_op jit(solution)/shard_map/ppermute | solution.py:719
  10.5 16.2 %copy-start.4 = (f32[125,125]{1,0:T(8,128)S(1)}, f32[125,125]{1,0:T(8,128)}, u32[]{:S(2)}) copy-start(f32[125,125]{1,0:T(8,128)} %fine_ref) | copy-start | bytes 187504
  10.5 16.2 %copy-start.5 = (f32[27,27]{1,0:T(8,128)S(1)}, f32[27,27]{1,0:T(8,128)}, u32[]{:S(2)}) copy-start(f32[27,27]{1,0:T(8,128)} %mid_ref) | copy-start | bytes 8752
  10.5 16.2 %copy-start.6 = (f32[8,8]{1,0:T(8,128)S(1)}, f32[8,8]{1,0:T(8,128)}, u32[]{:S(2)}) copy-start(f32[8,8]{1,0:T(8,128)} %coarse_ref) | copy-start | bytes 772
  10.5 16.2 %copy-start.7 = (f32[4,128,128]{2,1,0:T(8,128)S(1)}, f32[4,128,128]{2,1,0:T(8,128)}, u32[]{:S(2)}) copy-start(f32[4,128,128]{2,1,0:T(8,128)} %constant.49.clone.low_ref) | copy-start | bytes 786436
  10.5 16.2 %copy-start.8 = (f32[3,128,128]{2,1,0:T(8,128)S(1)}, f32[3,128,128]{2,1,0:T(8,128)}, u32[]{:S(2)}) copy-start(f32[3,128,128]{2,1,0:T(8,128)} %constant.50.clone.high_ref) | copy-start | bytes 589828
  10.5 35.3 %all-to-all-start = ((f32[544,2,128]{2,1,0:T(2,128)}), f32[544,2,128]{2,1,0:T(2,128)S(1)}, u32[]{:S(2)}, u32[]{:S(2)}) async-start(f32[544,2,128]{2,1,0:T(2,128)} %bitcast.3), calls=%async_computation | async-start | bytes 1114112 | tf_op jit(solution)/shard_map/all_to_all | solution.py:724
  26.7 23.0 %copy-start = (bf16[4,128,256]{2,1,0:T(8,128)(2,1)S(1)}, bf16[4,128,256]{2,1,0:T(8,128)(2,1)}, u32[]{:S(2)}) copy-start(bf16[4,128,256]{2,1,0:T(8,128)(2,1)} %constant.52.clone.up_ref) | copy-start | bytes 786436
  26.7 23.0 %copy-start.1 = (bf16[4,128,256]{2,1,0:T(8,128)(2,1)S(1)}, bf16[4,128,256]{2,1,0:T(8,128)(2,1)}, u32[]{:S(2)}) copy-start(bf16[4,128,256]{2,1,0:T(8,128)(2,1)} %constant.51.clone.down_ref) | copy-start | bytes 786436
  45.8 3.8 %collective-permute-start.2 = (f32[1088,128]{1,0:T(8,128)S(1)}, f32[1088,128]{1,0:T(8,128)S(1)}, u32[]{:S(2)}, u32[]{:S(2)}) collective-permute-start(f32[1088,128]{1,0:T(8,128)S(1)} %bitcast.7), channel_id=1, source_target_pairs={{0,1},{1,0},{2,3},{3,2},{4,5},{5,4},{6,7},{7,6},{8,9},{9,8},{10,11... | collective-permute-start | bytes 1671176 | tf_op jit(solution)/shard_map/ppermute | solution.py:728

commit v8 on v6

--- a/solution.py
+++ b/solution.py
@@ -131,13 +131,19 @@
         in_specs=[pl.BlockSpec(memory_space=pltpu.SMEM), vmem, vmem],
         out_specs=(vmem, vmem),
         scratch_shapes=[pltpu.VMEM((LANES, width), f32), pltpu.VMEM((width, LANES), f32)],
-        compiler_params=pltpu.CompilerParams(vmem_limit_bytes=8 * MIB),
+        compiler_params=pltpu.CompilerParams(vmem_limit_bytes=60 * MIB),
         name="pack",
     )(core, field, scaling)
 
 
-def window_body(core_ref, own_ref, sibling_ref, halo_ref, out_ref, line, *, parts):
+PIECES = 4
+
+
+def window_body(
+    core_ref, own_ref, sibling_ref, halo_ref, out_ref, line, block, sems, *, parts
+):
     count_z = own_ref.shape[1]
+    rows = parts // PIECES * WINDOW
     for core in range(2):
         places = (HALO, HALO + count_z, 0) if core == 0 else (count_z, 0, 2 * count_z)
 
@@ -146,11 +152,23 @@
             for ref, place in zip((own_ref, sibling_ref, halo_ref), places):
                 line[:, place : place + ref.shape[1], :] = ref[...]
             first = HALO - RADIUS if core == 0 else SPLIT - RADIUS
+            copies = []
             for part in range(parts):
                 for y in range(2):
                     start = first + OWN * part
                     row = part * WINDOW + y * SPLIT
-                    out_ref[row : row + SPLIT, :] = line[y, start : start + SPLIT, :]
+                    block[row : row + SPLIT, :] = line[y, start : start + SPLIT, :]
+                if (part + 1) % (parts // PIECES) == 0:
+                    piece = part // (parts // PIECES)
+                    place = slice(piece * rows, (piece + 1) * rows)
+                    copies.append(
+                        pltpu.make_async_copy(
+                            block.at[place, :], out_ref.at[place, :], sems.at[piece]
+                        )
+                    )
+                    copies[-1].start()
+            for copy in copies:
+                copy.wait()
 
 
 def window(core, own, sibling, halo, parts):
@@ -162,8 +180,12 @@
         body,
         out_shape=jax.ShapeDtypeStruct((parts * WINDOW, LANES), f32),
         in_specs=[pl.BlockSpec(memory_space=pltpu.SMEM), vmem, vmem, vmem],
-        out_specs=vmem,
-        scratch_shapes=[pltpu.VMEM((2, 2 * own.shape[1] + HALO, LANES), f32)],
+        out_specs=pl.BlockSpec(memory_space=pl.ANY),
+        scratch_shapes=[
+            pltpu.VMEM((2, 2 * own.shape[1] + HALO, LANES), f32),
+            pltpu.VMEM((parts * WINDOW, LANES), f32),
+            pltpu.SemaphoreType.DMA((PIECES,)),
+        ],
         compiler_params=pltpu.CompilerParams(vmem_limit_bytes=8 * MIB),
         name="window",
     )(core, own, sibling, halo)

time: 77.1 us -> 78.9 us (1.023)
  Pallas kernels: 18.8 us -> 20.4 us
    pallas_call x1, Pallas kernels: 0.33 us -> 1.9 us  [pack(): pl.pallas_call(body, out_shape=(jax.ShapeDtypeStruct((2, count_z, LANES),...]
where the time goes in v8:
time: 78.9 us; the launch traced here: 78.5 us
  starting transfers between devices  23.5 us (30%)
  Pallas kernels  20.4 us (26%)
  blocking collectives  18.9 us (24%)
  waiting for transfers between devices  14 us (18%)
  local copies, waits for them, and re-layouts  1.57 us (2%)
    all_to_all x1, blocking collectives, per_device(): lax.all_to_all(result.reshape(parts, 2 * OWN, LANES), ('gx', 'gy'), 0, 0,...  18.9 us
    all_to_all x1, starting transfers between devices, per_device(): lax.all_to_all(chunks.reshape(parts * WINDOW // 2, 2, LANES), ('gx', 'gy'...  16.1 us
    pallas_call x1, Pallas kernels, inverses(): pl.pallas_call(inverses_body, out_shape=jax.ShapeDtypeStruct((14, LANES,...  9.56 us
    all_to_all x1, waiting for transfers between devices, per_device(): lax.all_to_all(chunks.reshape(parts * WINDOW // 2, 2, LANES), ('gx', 'gy'...  9.53 us
    pallas_call x1, Pallas kernels, cycle(): pl.pallas_call(cycle_body, out_shape=jax.ShapeDtypeStruct((EX * HALF * 2...  6.92 us
    ppermute x1, starting transfers between devices, per_device(): halo = lax.ppermute(edge, 'gz', ties + [(j, i) for i, j in ties])  3.55 us
    ppermute x1, waiting for transfers between devices, per_device(): halo = lax.ppermute(edge, 'gz', ties + [(j, i) for i, j in ties])  2.6 us
    ppermute x1, starting transfers between devices, per_device(): other = lax.ppermute(recv, 'gz', pairs)  1.91 us
  transfers between devices with their start and end apart: 4, of which 3 were waited for; matrix products, arithmetic and copies ran while one was open for 0% of the time, Pallas kernels for 12%

profile of v8, /device:TPU:4, one launch (start us, length us, event | category | flops | bytes accessed | tf_op | source)
XLA Modules:
  0.0 78.5 jit_solution(4565436860119350763)
XLA Ops:
  0.0 1.9 %pack.1 = (f32[2,64,128]{2,1,0:T(8,128)}, f32[2,16,128]{2,1,0:T(8,128)}) custom-call(s32[1]{0:T(128)} %bitcast.refs_0_, f32[5,10,320]{2,1,0:T(8,128)} %refs_1_.1, f32[1,2,64]{2,1,0:T(2,128)} %refs_2_.3), custom_call_target="tpu_custom_call" | custom-call | tf_op jit(solution)/shard_map/pack/pallas_call | solution.py:125
  1.9 1.9 %collective-permute-start = (f32[2,64,128]{2,1,0:T(8,128)}, f32[2,64,128]{2,1,0:T(8,128)S(1)}, u32[]{:S(2)}, u32[]{:S(2)}) collective-permute-start(f32[2,64,128]{2,1,0:T(8,128)} %get-tuple-element.13.refs_1_), channel_id=1, source_target_pairs={{0,1},{1,0},{2,3},{3,2},{4,5},{5,4},{6,7},{7,6},{8,9},{9,8},{10,11... | collective-permute-start | bytes 196616 | tf_op jit(solution)/shard_map/ppermute | solution.py:687
  3.8 3.6 %collective-permute-start.1 = (f32[2,16,128]{2,1,0:T(8,128)}, f32[2,16,128]{2,1,0:T(8,128)S(1)}, u32[]{:S(2)}, u32[]{:S(2)}) collective-permute-start(f32[2,16,128]{2,1,0:T(8,128)} %get-tuple-element.14), channel_id=1, source_target_pairs={{1,2},{3,4},{5,6},{7,8},{9,10},{11,12},{13,14},{2,1},{4,3},{6,5},{... | collective-permute-start | bytes 49160 | tf_op jit(solution)/shard_map/ppermute | solution.py:686
  7.4 2.6 %collective-permute-done.1.refs_3_ = f32[2,16,128]{2,1,0:T(8,128)S(1)} collective-permute-done((f32[2,16,128]{2,1,0:T(8,128)}, f32[2,16,128]{2,1,0:T(8,128)S(1)}, u32[]{:S(2)}, u32[]{:S(2)}) %collective-permute-start.1) | collective-permute-done | bytes 16416 | tf_op jit(solution)/shard_map/ppermute | solution.py:686
  10.0 0.0 collective-permute-done.refs_2_
  10.0 0.0 copy-start.2
  10.0 0.8 %copy-done.2 = f32[2,64,128]{2,1,0:T(8,128)S(1)} copy-done((f32[2,64,128]{2,1,0:T(8,128)S(1)}, f32[2,64,128]{2,1,0:T(8,128)}, u32[]{:S(2)}) %copy-start.2) | copy-done | bytes 65560
  10.8 0.9 %window.1 = f32[1088,128]{1,0:T(8,128)} custom-call(s32[1]{0:T(128)} %bitcast.refs_0_, f32[2,64,128]{2,1,0:T(8,128)S(1)} %copy-done.2, f32[2,64,128]{2,1,0:T(8,128)S(1)} %collective-permute-done.refs_2_, f32[2,16,128]{2,1,0:T(8,128)S(1)} %collective-permute-done.1.refs_3_), custom_call_target="tpu_custom_call" | custom-call | tf_op jit(solution)/shard_map/window/pallas_call | solution.py:179
  11.7 0.0 copy-start.4
  11.7 0.0 copy-start.5
  11.7 0.0 copy-start.6
  11.7 0.0 copy-start.7
  11.7 0.0 copy-start.8
  11.8 16.1 %all-to-all-start = ((f32[544,2,128]{2,1,0:T(2,128)}), f32[544,2,128]{2,1,0:T(2,128)S(1)}, u32[]{:S(2)}, u32[]{:S(2)}) async-start(f32[544,2,128]{2,1,0:T(2,128)} %bitcast.3), calls=%async_computation | async-start | bytes 1114112 | tf_op jit(solution)/shard_map/all_to_all | solution.py:690
  27.9 0.0 copy-done.4
  27.9 0.0 copy-done.5
  27.9 0.0 copy-done.6
  27.9 0.0 copy-done.7
  27.9 0.0 copy-done.8
  27.9 0.0 copy-start
  27.9 0.0 copy-start.1
  27.9 9.6 %inverses.1.tables_ref = bf16[14,128,256]{2,1,0:T(8,128)(2,1)S(1)} custom-call(f32[125,125]{1,0:T(8,128)S(1)} %copy-done.4, f32[27,27]{1,0:T(8,128)S(1)} %copy-done.5, f32[8,8]{1,0:T(8,128)S(1)} %copy-done.6, f32[4,128,128]{2,1,0:T(8,128)S(1)} %copy-done.7, f32[3,128,128]{2,1,0:T(8,128)S(1)} %copy-done.8), custom_call_target="tpu_custom_call" | custom-call | flops 2000000000 | bytes 20000000 | tf_op jit(solution)/shard_map/inverses/pallas_call | solution.py:344
  37.5 9.5 %all-to-all-done = f32[544,2,128]{2,1,0:T(2,128)S(1)} async-done(((f32[544,2,128]{2,1,0:T(2,128)}), f32[544,2,128]{2,1,0:T(2,128)S(1)}, u32[]{:S(2)}, u32[]{:S(2)}) %all-to-all-start) | async-done | bytes 557088 | tf_op jit(solution)/shard_map/all_to_all | solution.py:690
  47.1 1.9 %collective-permute-start.2 = (f32[1088,128]{1,0:T(8,128)S(1)}, f32[1088,128]{1,0:T(8,128)S(1)}, u32[]{:S(2)}, u32[]{:S(2)}) collective-permute-start(f32[1088,128]{1,0:T(8,128)S(1)} %bitcast.7), channel_id=1, source_target_pairs={{0,1},{1,0},{2,3},{3,2},{4,5},{5,4},{6,7},{7,6},{8,9},{9,8},{10,11... | collective-permute-start | bytes 1671176 | tf_op jit(solution)/shard_map/ppermute | solution.py:694
  49.0 0.1 pad_add_fusion.bounds_ref
  49.1 1.8 %collective-permute-done.2.other_ref = f32[1088,128]{1,0:T(8,128)S(1)} collective-permute-done((f32[1088,128]{1,0:T(8,128)S(1)}, f32[1088,128]{1,0:T(8,128)S(1)}, u32[]{:S(2)}, u32[]{:S(2)}) %collective-permute-start.2) | collective-permute-done | bytes 557088 | tf_op jit(solution)/shard_map/ppermute | solution.py:694
  50.9 0.0 copy-done
  50.9 0.0 copy-done.1
  50.9 6.9 %cycle.1 = f32[256,128]{1,0:T(8,128)S(1)} custom-call(s32[3]{0:T(128)S(1)} %pad_add_fusion.bounds_ref, f32[1088,128]{1,0:T(8,128)S(1)} %bitcast.8, f32[1088,128]{1,0:T(8,128)S(1)} %collective-permute-done.2.other_ref, bf16[14,128,256]{2,1,0:T(8,128)(2,1)S(1)} %inverses.1.tables_ref, bf16[4,128,256]{2,1,0:T(8,128)(2,1)S(1)} %copy-done.1, ...), custom_call_target="tpu_custom_call" | custom-call | tf_op jit(solution)/shard_map/cycle/pallas_call | solution.py:663
  57.8 18.9 %all_to_all.10 = f32[32,8,128]{2,1,0:T(8,128)S(1)} all-to-all(f32[32,8,128]{2,1,0:T(8,128)S(1)} %bitcast.9), channel_id=1, replica_groups=mesh['gx'=4,'gy'=8,'gz'=16] {'gx','gy'}, dimensions={0} | all-to-all | bytes 262144 | tf_op jit(solution)/shard_map/all_to_all | solution.py:704
  76.7 0.0 copy-start.3
  76.7 0.7 copy-done.3
  77.4 1.1 %unpack.1 = f32[5,10,320]{2,1,0:T(8,128)} custom-call(s32[1]{0:T(128)} %bitcast.refs_0_, f32[256,128]{1,0:T(8,128)S(1)} %bitcast.10, f32[1,2,64]{2,1,0:T(2,128)S(1)} %copy-done.3), custom_call_target="tpu_custom_call" | custom-call | tf_op jit(solution)/shard_map/unpack/pallas_call | solution.py:231
Async XLA Ops:
  1.9 8.1 %collective-permute-start = (f32[2,64,128]{2,1,0:T(8,128)}, f32[2,64,128]{2,1,0:T(8,128)S(1)}, u32[]{:S(2)}, u32[]{:S(2)}) collective-permute-start(f32[2,64,128]{2,1,0:T(8,128)} %get-tuple-element.13.refs_1_), channel_id=1, source_target_pairs={{0,1},{1,0},{2,3},{3,2},{4,5},{5,4},{6,7},{7,6},{8,9},{9,8},{10,11... | collective-permute-start | bytes 196616 | tf_op jit(solution)/shard_map/ppermute | solution.py:687
  3.8 6.2 %collective-permute-start.1 = (f32[2,16,128]{2,1,0:T(8,128)}, f32[2,16,128]{2,1,0:T(8,128)S(1)}, u32[]{:S(2)}, u32[]{:S(2)}) collective-permute-start(f32[2,16,128]{2,1,0:T(8,128)} %get-tuple-element.14), channel_id=1, source_target_pairs={{1,2},{3,4},{5,6},{7,8},{9,10},{11,12},{13,14},{2,1},{4,3},{6,5},{... | collective-permute-start | bytes 49160 | tf_op jit(solution)/shard_map/ppermute | solution.py:686
  10.0 0.8 %copy-start.2 = (f32[2,64,128]{2,1,0:T(8,128)S(1)}, f32[2,64,128]{2,1,0:T(8,128)}, u32[]{:S(2)}) copy-start(f32[2,64,128]{2,1,0:T(8,128)} %get-tuple-element.13.refs_1_) | copy-start | bytes 196612
  11.7 16.2 %copy-start.4 = (f32[125,125]{1,0:T(8,128)S(1)}, f32[125,125]{1,0:T(8,128)}, u32[]{:S(2)}) copy-start(f32[125,125]{1,0:T(8,128)} %fine_ref) | copy-start | bytes 187504
  11.7 16.2 %copy-start.5 = (f32[27,27]{1,0:T(8,128)S(1)}, f32[27,27]{1,0:T(8,128)}, u32[]{:S(2)}) copy-start(f32[27,27]{1,0:T(8,128)} %mid_ref) | copy-start | bytes 8752
  11.7 16.2 %copy-start.6 = (f32[8,8]{1,0:T(8,128)S(1)}, f32[8,8]{1,0:T(8,128)}, u32[]{:S(2)}) copy-start(f32[8,8]{1,0:T(8,128)} %coarse_ref) | copy-start | bytes 772
  11.7 16.2 %copy-start.7 = (f32[4,128,128]{2,1,0:T(8,128)S(1)}, f32[4,128,128]{2,1,0:T(8,128)}, u32[]{:S(2)}) copy-start(f32[4,128,128]{2,1,0:T(8,128)} %constant.49.clone.low_ref) | copy-start | bytes 786436
  11.7 16.2 %copy-start.8 = (f32[3,128,128]{2,1,0:T(8,128)S(1)}, f32[3,128,128]{2,1,0:T(8,128)}, u32[]{:S(2)}) copy-start(f32[3,128,128]{2,1,0:T(8,128)} %constant.50.clone.high_ref) | copy-start | bytes 589828
  11.8 35.3 %all-to-all-start = ((f32[544,2,128]{2,1,0:T(2,128)}), f32[544,2,128]{2,1,0:T(2,128)S(1)}, u32[]{:S(2)}, u32[]{:S(2)}) async-start(f32[544,2,128]{2,1,0:T(2,128)} %bitcast.3), calls=%async_computation | async-start | bytes 1114112 | tf_op jit(solution)/shard_map/all_to_all | solution.py:690
  27.9 23.0 %copy-start = (bf16[4,128,256]{2,1,0:T(8,128)(2,1)S(1)}, bf16[4,128,256]{2,1,0:T(8,128)(2,1)}, u32[]{:S(2)}) copy-start(bf16[4,128,256]{2,1,0:T(8,128)(2,1)} %constant.52.clone.up_ref) | copy-start | bytes 786436
  27.9 23.0 %copy-start.1 = (bf16[4,128,256]{2,1,0:T(8,128)(2,1)S(1)}, bf16[4,128,256]{2,1,0:T(8,128)(2,1)}, u32[]{:S(2)}) copy-start(bf16[4,128,256]{2,1,0:T(8,128)(2,1)} %constant.51.clone.down_ref) | copy-start | bytes 786436
  47.1 3.8 %collective-permute-start.2 = (f32[1088,128]{1,0:T(8,128)S(1)}, f32[1088,128]{1,0:T(8,128)S(1)}, u32[]{:S(2)}, u32[]{:S(2)}) collective-permute-start(f32[1088,128]{1,0:T(8,128)S(1)} %bitcast.7), channel_id=1, source_target_pairs={{0,1},{1,0},{2,3},{3,2},{4,5},{5,4},{6,7},{7,6},{8,9},{9,8},{10,11... | collective-permute-start | bytes 1671176 | tf_op jit(solution)/shard_map/ppermute | solution.py:694
  76.7 0.7 copy-start.3

commit v9 on v6

--- a/solution.py
+++ b/solution.py
@@ -134,6 +134,21 @@
         compiler_params=pltpu.CompilerParams(vmem_limit_bytes=8 * MIB),
         name="pack",
     )(core, field, scaling)
+
+
+def settle(halo):
+    def body(in_ref, out_ref):
+        out_ref[...] = in_ref[...]
+
+    return pl.pallas_call(
+        body,
+        out_shape=jax.ShapeDtypeStruct(halo.shape, f32),
+        cost_estimate=pl.CostEstimate(
+            flops=2_000_000_000, bytes_accessed=20_000_000, transcendentals=0
+        ),
+        compiler_params=pltpu.CompilerParams(vmem_limit_bytes=8 * MIB),
+        name="settle",
+    )(halo)
 
 
 def window_body(core_ref, own_ref, sibling_ref, halo_ref, out_ref, line, *, parts):
@@ -661,7 +676,7 @@
     own, edge = pack(cores, fine_source_field, scaling)
     ties = [(i, i + 1) for i in range(1, groups - 1, 2)]
     pairs = [(i, i ^ 1) for i in range(groups)]
-    halo = lax.ppermute(edge, "gz", ties + [(j, i) for i, j in ties])
+    halo = settle(lax.ppermute(edge, "gz", ties + [(j, i) for i, j in ties]))
     sibling = lax.ppermute(own, "gz", pairs)
     chunks = window(cores, own, sibling, halo, parts)
     chunks, *matrices = lax.optimization_barrier((chunks, block_fine, block_mid, block_coarse))

time: 77.1 us -> 76.4 us (level)
  the two profiles are of different devices: /device:TPU:4 before, /device:TPU:10 now
where the time goes in v9:
time: 76.4 us; the launch traced here: 76.1 us
  starting transfers between devices  23.3 us (30%)
  Pallas kernels  18.8 us (25%)
  blocking collectives  18.3 us (24%)
  waiting for transfers between devices  13.8 us (18%)
  local copies, waits for them, and re-layouts  1.61 us (2%)
    all_to_all x1, blocking collectives, per_device(): lax.all_to_all(result.reshape(parts, 2 * OWN, LANES), ('gx', 'gy'), 0, 0,...  18.3 us
    all_to_all x1, starting transfers between devices, per_device(): lax.all_to_all(chunks.reshape(parts * WINDOW // 2, 2, LANES), ('gx', 'gy'...  16.1 us
    all_to_all x1, waiting for transfers between devices, per_device(): lax.all_to_all(chunks.reshape(parts * WINDOW // 2, 2, LANES), ('gx', 'gy'...  11.1 us
    pallas_call x1, Pallas kernels, inverses(): pl.pallas_call(inverses_body, out_shape=jax.ShapeDtypeStruct((14, LANES,...  9.56 us
    pallas_call x1, Pallas kernels, cycle(): pl.pallas_call(cycle_body, out_shape=jax.ShapeDtypeStruct((EX * HALF * 2...  6.91 us
    ppermute x1, starting transfers between devices, per_device(): sibling = lax.ppermute(own, 'gz', pairs)  3.39 us
    ppermute x1, starting transfers between devices, per_device(): halo = settle(lax.ppermute(edge, 'gz', ties + [(j, i) for i, j in ties]))  1.92 us
    ppermute x1, starting transfers between devices, per_device(): other = lax.ppermute(recv, 'gz', pairs)  1.91 us
  transfers between devices with their start and end apart: 4, of which 3 were waited for; matrix products, arithmetic and copies ran while one was open for 0% of the time, Pallas kernels for 13%

profile of v9, /device:TPU:10, one launch (start us, length us, event | category | flops | bytes accessed | tf_op | source)
XLA Modules:
  0.0 76.1 jit_solution(7702398827093883675)
XLA Ops:
  0.0 0.0 copy-start.3
  0.0 0.7 copy-done.3
  0.7 0.0 copy-start.2
  0.7 0.9 %copy-done.2 = f32[5,10,320]{2,1,0:T(8,128)S(1)} copy-done((f32[5,10,320]{2,1,0:T(8,128)S(1)}, f32[5,10,320]{2,1,0:T(8,128)}, u32[]{:S(2)}) %copy-start.2) | copy-done | bytes 64024
  1.6 0.3 pack.1
  1.9 1.9 %collective-permute-start.1 = (f32[2,16,128]{2,1,0:T(8,128)S(1)}, f32[2,16,128]{2,1,0:T(8,128)S(1)}, u32[]{:S(2)}, u32[]{:S(2)}) collective-permute-start(f32[2,16,128]{2,1,0:T(8,128)S(1)} %get-tuple-element.14), channel_id=1, source_target_pairs={{1,2},{3,4},{5,6},{7,8},{9,10},{11,12},{13,14},{2,1},{4,3},{6,5},{... | collective-permute-start | bytes 49160 | tf_op jit(solution)/shard_map/ppermute | solution.py:679
  3.9 3.4 %collective-permute-start = (f32[2,64,128]{2,1,0:T(8,128)S(1)}, f32[2,64,128]{2,1,0:T(8,128)S(1)}, u32[]{:S(2)}, u32[]{:S(2)}) collective-permute-start(f32[2,64,128]{2,1,0:T(8,128)S(1)} %get-tuple-element.13.refs_1_), channel_id=1, source_target_pairs={{0,1},{1,0},{2,3},{3,2},{4,5},{5,4},{6,7},{7,6},{8,9},{9,8},{10,11... | collective-permute-start | bytes 196616 | tf_op jit(solution)/shard_map/ppermute | solution.py:680
  7.2 0.0 collective-permute-done.1.in_ref
  7.3 0.9 %collective-permute-done.refs_2_ = f32[2,64,128]{2,1,0:T(8,128)S(1)} collective-permute-done((f32[2,64,128]{2,1,0:T(8,128)S(1)}, f32[2,64,128]{2,1,0:T(8,128)S(1)}, u32[]{:S(2)}, u32[]{:S(2)}) %collective-permute-start) | collective-permute-done | bytes 65568 | tf_op jit(solution)/shard_map/ppermute | solution.py:680
  8.1 0.9 %window.1 = f32[1088,128]{1,0:T(8,128)} custom-call(s32[1]{0:T(128)} %bitcast.refs_0_, f32[2,64,128]{2,1,0:T(8,128)S(1)} %get-tuple-element.13.refs_1_, f32[2,64,128]{2,1,0:T(8,128)S(1)} %collective-permute-done.refs_2_, f32[2,16,128]{2,1,0:T(8,128)S(1)} %settle.1.refs_3_), custom_call_target="tpu_custom_call" | custom-call | tf_op jit(solution)/shard_map/window/pallas_call | solution.py:176
  9.0 0.0 copy-start.4
  9.0 0.0 copy-start.5
  9.0 0.0 copy-start.6
  9.0 0.0 copy-start.7
  9.0 0.0 copy-start.8
  9.0 16.1 %all-to-all-start = ((f32[544,2,128]{2,1,0:T(2,128)}), f32[544,2,128]{2,1,0:T(2,128)S(1)}, u32[]{:S(2)}, u32[]{:S(2)}) async-start(f32[544,2,128]{2,1,0:T(2,128)} %bitcast.3), calls=%async_computation | async-start | bytes 1114112 | tf_op jit(solution)/shard_map/all_to_all | solution.py:683
  25.1 0.0 copy-done.4
  25.2 0.0 copy-done.5
  25.2 0.0 copy-done.6
  25.2 0.0 copy-done.7
  25.2 0.0 copy-done.8
  25.2 0.0 copy-start
  25.2 0.0 copy-start.1
  25.2 9.6 %inverses.1.tables_ref = bf16[14,128,256]{2,1,0:T(8,128)(2,1)S(1)} custom-call(f32[125,125]{1,0:T(8,128)S(1)} %copy-done.4, f32[27,27]{1,0:T(8,128)S(1)} %copy-done.5, f32[8,8]{1,0:T(8,128)S(1)} %copy-done.6, f32[4,128,128]{2,1,0:T(8,128)S(1)} %copy-done.7, f32[3,128,128]{2,1,0:T(8,128)S(1)} %copy-done.8), custom_call_target="tpu_custom_call" | custom-call | flops 2000000000 | bytes 20000000 | tf_op jit(solution)/shard_map/inverses/pallas_call | solution.py:337
  34.8 11.1 %all-to-all-done = f32[544,2,128]{2,1,0:T(2,128)S(1)} async-done(((f32[544,2,128]{2,1,0:T(2,128)}), f32[544,2,128]{2,1,0:T(2,128)S(1)}, u32[]{:S(2)}, u32[]{:S(2)}) %all-to-all-start) | async-done | bytes 557088 | tf_op jit(solution)/shard_map/all_to_all | solution.py:683
  45.9 1.9 %collective-permute-start.2 = (f32[1088,128]{1,0:T(8,128)S(1)}, f32[1088,128]{1,0:T(8,128)S(1)}, u32[]{:S(2)}, u32[]{:S(2)}) collective-permute-start(f32[1088,128]{1,0:T(8,128)S(1)} %bitcast.7), channel_id=1, source_target_pairs={{0,1},{1,0},{2,3},{3,2},{4,5},{5,4},{6,7},{7,6},{8,9},{9,8},{10,11... | collective-permute-start | bytes 1671176 | tf_op jit(solution)/shard_map/ppermute | solution.py:687
  47.8 0.1 pad_add_fusion.bounds_ref
  47.9 1.8 %collective-permute-done.2.other_ref = f32[1088,128]{1,0:T(8,128)S(1)} collective-permute-done((f32[1088,128]{1,0:T(8,128)S(1)}, f32[1088,128]{1,0:T(8,128)S(1)}, u32[]{:S(2)}, u32[]{:S(2)}) %collective-permute-start.2) | collective-permute-done | bytes 557088 | tf_op jit(solution)/shard_map/ppermute | solution.py:687
  49.7 0.0 copy-done
  49.7 0.0 copy-done.1
  49.7 6.9 %cycle.1 = f32[256,128]{1,0:T(8,128)S(1)} custom-call(s32[3]{0:T(128)S(1)} %pad_add_fusion.bounds_ref, f32[1088,128]{1,0:T(8,128)S(1)} %bitcast.8, f32[1088,128]{1,0:T(8,128)S(1)} %collective-permute-done.2.other_ref, bf16[14,128,256]{2,1,0:T(8,128)(2,1)S(1)} %inverses.1.tables_ref, bf16[4,128,256]{2,1,0:T(8,128)(2,1)S(1)} %copy-done.1, ...), custom_call_target="tpu_custom_call" | custom-call | tf_op jit(solution)/shard_map/cycle/pallas_call | solution.py:656
  56.6 18.3 %all_to_all.10 = f32[32,8,128]{2,1,0:T(8,128)S(1)} all-to-all(f32[32,8,128]{2,1,0:T(8,128)S(1)} %bitcast.9), channel_id=1, replica_groups=mesh['gx'=4,'gy'=8,'gz'=16] {'gx','gy'}, dimensions={0} | all-to-all | bytes 262144 | tf_op jit(solution)/shard_map/all_to_all | solution.py:697
  75.0 1.1 %unpack.1 = f32[5,10,320]{2,1,0:T(8,128)} custom-call(s32[1]{0:T(128)} %bitcast.refs_0_, f32[256,128]{1,0:T(8,128)S(1)} %bitcast.10, f32[1,2,64]{2,1,0:T(2,128)S(1)} %copy-done.3), custom_call_target="tpu_custom_call" | custom-call | tf_op jit(solution)/shard_map/unpack/pallas_call | solution.py:224
  (1 shorter events, 0.0 us)
Async XLA Ops:
  0.0 0.7 copy-start.3
  0.7 0.9 %copy-start.2 = (f32[5,10,320]{2,1,0:T(8,128)S(1)}, f32[5,10,320]{2,1,0:T(8,128)}, u32[]{:S(2)}) copy-start(f32[5,10,320]{2,1,0:T(8,128)} %refs_1_.1) | copy-start | bytes 192004
  1.9 5.3 %collective-permute-start.1 = (f32[2,16,128]{2,1,0:T(8,128)S(1)}, f32[2,16,128]{2,1,0:T(8,128)S(1)}, u32[]{:S(2)}, u32[]{:S(2)}) collective-permute-start(f32[2,16,128]{2,1,0:T(8,128)S(1)} %get-tuple-element.14), channel_id=1, source_target_pairs={{1,2},{3,4},{5,6},{7,8},{9,10},{11,12},{13,14},{2,1},{4,3},{6,5},{... | collective-permute-start | bytes 49160 | tf_op jit(solution)/shard_map/ppermute | solution.py:679
  3.9 4.3 %collective-permute-start = (f32[2,64,128]{2,1,0:T(8,128)S(1)}, f32[2,64,128]{2,1,0:T(8,128)S(1)}, u32[]{:S(2)}, u32[]{:S(2)}) collective-permute-start(f32[2,64,128]{2,1,0:T(8,128)S(1)} %get-tuple-element.13.refs_1_), channel_id=1, source_target_pairs={{0,1},{1,0},{2,3},{3,2},{4,5},{5,4},{6,7},{7,6},{8,9},{9,8},{10,11... | collective-permute-start | bytes 196616 | tf_op jit(solution)/shard_map/ppermute | solution.py:680
  9.0 16.1 %copy-start.4 = (f32[125,125]{1,0:T(8,128)S(1)}, f32[125,125]{1,0:T(8,128)}, u32[]{:S(2)}) copy-start(f32[125,125]{1,0:T(8,128)} %fine_ref) | copy-start | bytes 187504
  9.0 16.1 %copy-start.5 = (f32[27,27]{1,0:T(8,128)S(1)}, f32[27,27]{1,0:T(8,128)}, u32[]{:S(2)}) copy-start(f32[27,27]{1,0:T(8,128)} %mid_ref) | copy-start | bytes 8752
  9.0 16.2 %copy-start.6 = (f32[8,8]{1,0:T(8,128)S(1)}, f32[8,8]{1,0:T(8,128)}, u32[]{:S(2)}) copy-start(f32[8,8]{1,0:T(8,128)} %coarse_ref) | copy-start | bytes 772
  9.0 16.2 %copy-start.7 = (f32[4,128,128]{2,1,0:T(8,128)S(1)}, f32[4,128,128]{2,1,0:T(8,128)}, u32[]{:S(2)}) copy-start(f32[4,128,128]{2,1,0:T(8,128)} %constant.49.clone.low_ref) | copy-start | bytes 786436
  9.0 16.2 %copy-start.8 = (f32[3,128,128]{2,1,0:T(8,128)S(1)}, f32[3,128,128]{2,1,0:T(8,128)}, u32[]{:S(2)}) copy-start(f32[3,128,128]{2,1,0:T(8,128)} %constant.50.clone.high_ref) | copy-start | bytes 589828
  9.0 36.9 %all-to-all-start = ((f32[544,2,128]{2,1,0:T(2,128)}), f32[544,2,128]{2,1,0:T(2,128)S(1)}, u32[]{:S(2)}, u32[]{:S(2)}) async-start(f32[544,2,128]{2,1,0:T(2,128)} %bitcast.3), calls=%async_computation | async-start | bytes 1114112 | tf_op jit(solution)/shard_map/all_to_all | solution.py:683
  25.2 24.5 %copy-start = (bf16[4,128,256]{2,1,0:T(8,128)(2,1)S(1)}, bf16[4,128,256]{2,1,0:T(8,128)(2,1)}, u32[]{:S(2)}) copy-start(bf16[4,128,256]{2,1,0:T(8,128)(2,1)} %constant.52.clone.up_ref) | copy-start | bytes 786436
  25.2 24.5 %copy-start.1 = (bf16[4,128,256]{2,1,0:T(8,128)(2,1)S(1)}, bf16[4,128,256]{2,1,0:T(8,128)(2,1)}, u32[]{:S(2)}) copy-start(bf16[4,128,256]{2,1,0:T(8,128)(2,1)} %constant.51.clone.down_ref) | copy-start | bytes 786436
  45.9 3.8 %collective-permute-start.2 = (f32[1088,128]{1,0:T(8,128)S(1)}, f32[1088,128]{1,0:T(8,128)S(1)}, u32[]{:S(2)}, u32[]{:S(2)}) collective-permute-start(f32[1088,128]{1,0:T(8,128)S(1)} %bitcast.7), channel_id=1, source_target_pairs={{0,1},{1,0},{2,3},{3,2},{4,5},{5,4},{6,7},{7,6},{8,9},{9,8},{10,11... | collective-permute-start | bytes 1671176 | tf_op jit(solution)/shard_map/ppermute | solution.py:687

commit v10 on v9

--- a/solution.py
+++ b/solution.py
@@ -684,7 +684,14 @@
         chunks.reshape(parts * WINDOW // 2, 2, LANES), ("gx", "gy"), 0, 0, tiled=True
     ).reshape(parts * WINDOW, LANES)
     recv, tables = lax.optimization_barrier((recv, inverses(*matrices, low, high)))
-    other = lax.ppermute(recv, "gz", pairs)
+    wide = lax.axis_size("gx")
+    ways = [
+        (x * groups + i, x * groups + (i ^ 1))
+        for x in range(wide)
+        for i in range(groups)
+        if i % 2 == (1 if 2 * x < wide else 0)
+    ]
+    other = lax.ppermute(recv, ("gx", "gz"), ways)
 
     part = lax.axis_index("gx") * lax.axis_size("gy") + lax.axis_index("gy")
     first = (group - core) * count_z + OWN * part - RADIUS

time: 76.4 us -> 75.5 us (0.988)
  the two profiles are of different devices: /device:TPU:10 before, /device:TPU:2 now
where the time goes in v10:
time: 75.5 us; the launch traced here: 75 us
  starting transfers between devices  22.5 us (30%)
  blocking collectives  20.6 us (27%)
  Pallas kernels  18.8 us (25%)
  waiting for transfers between devices  11.3 us (15%)
  local copies, waits for them, and re-layouts  1.61 us (2%)
    all_to_all x1, blocking collectives, per_device(): lax.all_to_all(result.reshape(parts, 2 * OWN, LANES), ('gx', 'gy'), 0, 0,...  20.6 us
    all_to_all x1, starting transfers between devices, per_device(): lax.all_to_all(chunks.reshape(parts * WINDOW // 2, 2, LANES), ('gx', 'gy'...  15.7 us
    pallas_call x1, Pallas kernels, inverses(): pl.pallas_call(inverses_body, out_shape=jax.ShapeDtypeStruct((14, LANES,...  9.56 us
    all_to_all x1, waiting for transfers between devices, per_device(): lax.all_to_all(chunks.reshape(parts * WINDOW // 2, 2, LANES), ('gx', 'gy'...  7.95 us
    pallas_call x1, Pallas kernels, cycle(): pl.pallas_call(cycle_body, out_shape=jax.ShapeDtypeStruct((EX * HALF * 2...  6.92 us
    ppermute x1, starting transfers between devices, per_device(): halo = settle(lax.ppermute(edge, 'gz', ties + [(j, i) for i, j in ties]))  2.9 us
    ppermute x1, starting transfers between devices, per_device(): sibling = lax.ppermute(own, 'gz', pairs)  2.61 us
    ppermute x1, waiting for transfers between devices, per_device(): other = lax.ppermute(recv, ('gx', 'gz'), ways)  2.46 us
  transfers between devices with their start and end apart: 4, of which 4 were waited for; matrix products, arithmetic and copies ran while one was open for 0% of the time, Pallas kernels for 13%

profile of v10, /device:TPU:2, one launch (start us, length us, event | category | flops | bytes accessed | tf_op | source)
XLA Modules:
  0.0 75.0 jit_solution(12225113688883505715)
XLA Ops:
  0.0 0.0 copy-start.3
  0.0 0.7 copy-done.3
  0.7 0.0 copy-start.2
  0.7 0.9 %copy-done.2 = f32[5,10,320]{2,1,0:T(8,128)S(1)} copy-done((f32[5,10,320]{2,1,0:T(8,128)S(1)}, f32[5,10,320]{2,1,0:T(8,128)}, u32[]{:S(2)}) %copy-start.2) | copy-done | bytes 64024
  1.6 0.3 pack.1
  1.9 2.9 %collective-permute-start.1 = (f32[2,16,128]{2,1,0:T(8,128)S(1)}, f32[2,16,128]{2,1,0:T(8,128)S(1)}, u32[]{:S(2)}, u32[]{:S(2)}) collective-permute-start(f32[2,16,128]{2,1,0:T(8,128)S(1)} %get-tuple-element.14), channel_id=1, source_target_pairs={{1,2},{3,4},{5,6},{7,8},{9,10},{11,12},{13,14},{2,1},{4,3},{6,5},{... | collective-permute-start | bytes 49160 | tf_op jit(solution)/shard_map/ppermute | solution.py:679
  4.8 2.6 %collective-permute-start = (f32[2,64,128]{2,1,0:T(8,128)S(1)}, f32[2,64,128]{2,1,0:T(8,128)S(1)}, u32[]{:S(2)}, u32[]{:S(2)}) collective-permute-start(f32[2,64,128]{2,1,0:T(8,128)S(1)} %get-tuple-element.13.refs_1_), channel_id=1, source_target_pairs={{0,1},{1,0},{2,3},{3,2},{4,5},{5,4},{6,7},{7,6},{8,9},{9,8},{10,11... | collective-permute-start | bytes 196616 | tf_op jit(solution)/shard_map/ppermute | solution.py:680
  7.4 0.4 collective-permute-done.1.in_ref
  7.9 0.4 collective-permute-done.refs_2_
  8.3 0.9 %window.1 = f32[1088,128]{1,0:T(8,128)} custom-call(s32[1]{0:T(128)} %bitcast.refs_0_, f32[2,64,128]{2,1,0:T(8,128)S(1)} %get-tuple-element.13.refs_1_, f32[2,64,128]{2,1,0:T(8,128)S(1)} %collective-permute-done.refs_2_, f32[2,16,128]{2,1,0:T(8,128)S(1)} %settle.1.refs_3_), custom_call_target="tpu_custom_call" | custom-call | tf_op jit(solution)/shard_map/window/pallas_call | solution.py:176
  9.2 0.0 copy-start.4
  9.2 0.0 copy-start.5
  9.2 0.0 copy-start.6
  9.2 0.0 copy-start.7
  9.2 0.0 copy-start.8
  9.2 15.7 %all-to-all-start = ((f32[544,2,128]{2,1,0:T(2,128)}), f32[544,2,128]{2,1,0:T(2,128)S(1)}, u32[]{:S(2)}, u32[]{:S(2)}) async-start(f32[544,2,128]{2,1,0:T(2,128)} %bitcast.3), calls=%async_computation | async-start | bytes 1114112 | tf_op jit(solution)/shard_map/all_to_all | solution.py:683
  24.9 0.0 copy-done.4
  24.9 0.0 copy-done.5
  24.9 0.0 copy-done.6
  24.9 0.0 copy-done.7
  24.9 0.0 copy-done.8
  25.0 0.0 copy-start
  25.0 0.0 copy-start.1
  25.0 9.6 %inverses.1.tables_ref = bf16[14,128,256]{2,1,0:T(8,128)(2,1)S(1)} custom-call(f32[125,125]{1,0:T(8,128)S(1)} %copy-done.4, f32[27,27]{1,0:T(8,128)S(1)} %copy-done.5, f32[8,8]{1,0:T(8,128)S(1)} %copy-done.6, f32[4,128,128]{2,1,0:T(8,128)S(1)} %copy-done.7, f32[3,128,128]{2,1,0:T(8,128)S(1)} %copy-done.8), custom_call_target="tpu_custom_call" | custom-call | flops 2000000000 | bytes 20000000 | tf_op jit(solution)/shard_map/inverses/pallas_call | solution.py:337
  34.5 7.9 %all-to-all-done = f32[544,2,128]{2,1,0:T(2,128)S(1)} async-done(((f32[544,2,128]{2,1,0:T(2,128)}), f32[544,2,128]{2,1,0:T(2,128)S(1)}, u32[]{:S(2)}, u32[]{:S(2)}) %all-to-all-start) | async-done | bytes 557088 | tf_op jit(solution)/shard_map/all_to_all | solution.py:683
  42.5 1.3 %collective-permute-start.2 = (f32[1088,128]{1,0:T(8,128)S(1)}, f32[1088,128]{1,0:T(8,128)S(1)}, u32[]{:S(2)}, u32[]{:S(2)}) collective-permute-start(f32[1088,128]{1,0:T(8,128)S(1)} %bitcast.7), channel_id=1, source_target_pairs={{1,0},{3,2},{5,4},{7,6},{9,8},{11,10},{13,12},{15,14},{129,128},{1... | collective-permute-start | bytes 1671176 | tf_op jit(solution)/shard_map/ppermute | solution.py:694
  43.8 0.1 pad_add_fusion.bounds_ref
  43.9 2.5 %collective-permute-done.2.other_ref = f32[1088,128]{1,0:T(8,128)S(1)} collective-permute-done((f32[1088,128]{1,0:T(8,128)S(1)}, f32[1088,128]{1,0:T(8,128)S(1)}, u32[]{:S(2)}, u32[]{:S(2)}) %collective-permute-start.2) | collective-permute-done | bytes 557088 | tf_op jit(solution)/shard_map/ppermute | solution.py:694
  46.3 0.0 copy-done
  46.3 0.0 copy-done.1
  46.3 6.9 %cycle.1 = f32[256,128]{1,0:T(8,128)S(1)} custom-call(s32[3]{0:T(128)S(1)} %pad_add_fusion.bounds_ref, f32[1088,128]{1,0:T(8,128)S(1)} %bitcast.8, f32[1088,128]{1,0:T(8,128)S(1)} %collective-permute-done.2.other_ref, bf16[14,128,256]{2,1,0:T(8,128)(2,1)S(1)} %inverses.1.tables_ref, bf16[4,128,256]{2,1,0:T(8,128)(2,1)S(1)} %copy-done.1, ...), custom_call_target="tpu_custom_call" | custom-call | tf_op jit(solution)/shard_map/cycle/pallas_call | solution.py:656
  53.3 20.6 %all_to_all.10 = f32[32,8,128]{2,1,0:T(8,128)S(1)} all-to-all(f32[32,8,128]{2,1,0:T(8,128)S(1)} %bitcast.9), channel_id=1, replica_groups=mesh['gx'=4,'gy'=8,'gz'=16] {'gx','gy'}, dimensions={0} | all-to-all | bytes 262144 | tf_op jit(solution)/shard_map/all_to_all | solution.py:704
  73.9 1.1 %unpack.1 = f32[5,10,320]{2,1,0:T(8,128)} custom-call(s32[1]{0:T(128)} %bitcast.refs_0_, f32[256,128]{1,0:T(8,128)S(1)} %bitcast.10, f32[1,2,64]{2,1,0:T(2,128)S(1)} %copy-done.3), custom_call_target="tpu_custom_call" | custom-call | tf_op jit(solution)/shard_map/unpack/pallas_call | solution.py:224
  (1 shorter events, 0.0 us)
Async XLA Ops:
  0.0 0.7 copy-start.3
  0.7 0.9 %copy-start.2 = (f32[5,10,320]{2,1,0:T(8,128)S(1)}, f32[5,10,320]{2,1,0:T(8,128)}, u32[]{:S(2)}) copy-start(f32[5,10,320]{2,1,0:T(8,128)} %refs_1_.1) | copy-start | bytes 192004
  1.9 6.0 %collective-permute-start.1 = (f32[2,16,128]{2,1,0:T(8,128)S(1)}, f32[2,16,128]{2,1,0:T(8,128)S(1)}, u32[]{:S(2)}, u32[]{:S(2)}) collective-permute-start(f32[2,16,128]{2,1,0:T(8,128)S(1)} %get-tuple-element.14), channel_id=1, source_target_pairs={{1,2},{3,4},{5,6},{7,8},{9,10},{11,12},{13,14},{2,1},{4,3},{6,5},{... | collective-permute-start | bytes 49160 | tf_op jit(solution)/shard_map/ppermute | solution.py:679
  4.8 3.5 %collective-permute-start = (f32[2,64,128]{2,1,0:T(8,128)S(1)}, f32[2,64,128]{2,1,0:T(8,128)S(1)}, u32[]{:S(2)}, u32[]{:S(2)}) collective-permute-start(f32[2,64,128]{2,1,0:T(8,128)S(1)} %get-tuple-element.13.refs_1_), channel_id=1, source_target_pairs={{0,1},{1,0},{2,3},{3,2},{4,5},{5,4},{6,7},{7,6},{8,9},{9,8},{10,11... | collective-permute-start | bytes 196616 | tf_op jit(solution)/shard_map/ppermute | solution.py:680
  9.2 15.7 %copy-start.4 = (f32[125,125]{1,0:T(8,128)S(1)}, f32[125,125]{1,0:T(8,128)}, u32[]{:S(2)}) copy-start(f32[125,125]{1,0:T(8,128)} %fine_ref) | copy-start | bytes 187504
  9.2 15.7 %copy-start.5 = (f32[27,27]{1,0:T(8,128)S(1)}, f32[27,27]{1,0:T(8,128)}, u32[]{:S(2)}) copy-start(f32[27,27]{1,0:T(8,128)} %mid_ref) | copy-start | bytes 8752
  9.2 15.7 %copy-start.6 = (f32[8,8]{1,0:T(8,128)S(1)}, f32[8,8]{1,0:T(8,128)}, u32[]{:S(2)}) copy-start(f32[8,8]{1,0:T(8,128)} %coarse_ref) | copy-start | bytes 772
  9.2 15.7 %copy-start.7 = (f32[4,128,128]{2,1,0:T(8,128)S(1)}, f32[4,128,128]{2,1,0:T(8,128)}, u32[]{:S(2)}) copy-start(f32[4,128,128]{2,1,0:T(8,128)} %constant.49.clone.low_ref) | copy-start | bytes 786436
  9.2 15.7 %copy-start.8 = (f32[3,128,128]{2,1,0:T(8,128)S(1)}, f32[3,128,128]{2,1,0:T(8,128)}, u32[]{:S(2)}) copy-start(f32[3,128,128]{2,1,0:T(8,128)} %constant.50.clone.high_ref) | copy-start | bytes 589828
  9.2 33.3 %all-to-all-start = ((f32[544,2,128]{2,1,0:T(2,128)}), f32[544,2,128]{2,1,0:T(2,128)S(1)}, u32[]{:S(2)}, u32[]{:S(2)}) async-start(f32[544,2,128]{2,1,0:T(2,128)} %bitcast.3), calls=%async_computation | async-start | bytes 1114112 | tf_op jit(solution)/shard_map/all_to_all | solution.py:683
  25.0 21.4 %copy-start = (bf16[4,128,256]{2,1,0:T(8,128)(2,1)S(1)}, bf16[4,128,256]{2,1,0:T(8,128)(2,1)}, u32[]{:S(2)}) copy-start(bf16[4,128,256]{2,1,0:T(8,128)(2,1)} %constant.52.clone.up_ref) | copy-start | bytes 786436
  25.0 21.4 %copy-start.1 = (bf16[4,128,256]{2,1,0:T(8,128)(2,1)S(1)}, bf16[4,128,256]{2,1,0:T(8,128)(2,1)}, u32[]{:S(2)}) copy-start(bf16[4,128,256]{2,1,0:T(8,128)(2,1)} %constant.51.clone.down_ref) | copy-start | bytes 786436
  42.5 3.8 %collective-permute-start.2 = (f32[1088,128]{1,0:T(8,128)S(1)}, f32[1088,128]{1,0:T(8,128)S(1)}, u32[]{:S(2)}, u32[]{:S(2)}) collective-permute-start(f32[1088,128]{1,0:T(8,128)S(1)} %bitcast.7), channel_id=1, source_target_pairs={{1,0},{3,2},{5,4},{7,6},{9,8},{11,10},{13,12},{15,14},{129,128},{1... | collective-permute-start | bytes 1671176 | tf_op jit(solution)/shard_map/ppermute | solution.py:694

commit v11 on v9

--- a/solution.py
+++ b/solution.py
@@ -540,8 +540,8 @@
             values = []
             for z in range(c, d):
                 for y in range(2):
-                    first = x * HALF * WINDOW + y * SPLIT + z % SPLIT
-                    place = pl.ds(first, HALF, stride=WINDOW)
+                    first = x * WINDOW + y * SPLIT + z % SPLIT
+                    place = pl.ds(first, HALF, stride=EX * WINDOW)
                     mine, other = mine_ref[place, :], other_ref[place, :]
                     if z < SPLIT:
                         mine, other = other, mine
@@ -645,8 +645,8 @@
         for z in range(OWN):
             for y in range(2):
                 values = ping[x * WINDOW + RADIUS + z, y * HALF : (y + 1) * HALF, :]
-                first = x * HALF * OWN * 2 + z * 2 + y
-                out_ref[pl.ds(first, HALF, stride=2 * OWN), :] = values
+                first = x * OWN * 2 + z * 2 + y
+                out_ref[pl.ds(first, HALF, stride=EX * 2 * OWN), :] = values
 
 
 def cycle(bounds, mine, other, tables, down, up):
@@ -681,12 +681,19 @@
     chunks = window(cores, own, sibling, halo, parts)
     chunks, *matrices = lax.optimization_barrier((chunks, block_fine, block_mid, block_coarse))
     recv = lax.all_to_all(
-        chunks.reshape(parts * WINDOW // 2, 2, LANES), ("gx", "gy"), 0, 0, tiled=True
+        chunks.reshape(parts * WINDOW // 2, 2, LANES), ("gy", "gx"), 0, 0, tiled=True
     ).reshape(parts * WINDOW, LANES)
     recv, tables = lax.optimization_barrier((recv, inverses(*matrices, low, high)))
-    other = lax.ppermute(recv, "gz", pairs)
-
-    part = lax.axis_index("gx") * lax.axis_size("gy") + lax.axis_index("gy")
+    tall = lax.axis_size("gy")
+    ways = [
+        (y * groups + i, y * groups + (i ^ 1))
+        for y in range(tall)
+        for i in range(groups)
+        if i % 2 == (1 if 2 * y < tall else 0)
+    ]
+    other = lax.ppermute(recv, ("gy", "gz"), ways)
+
+    part = lax.axis_index("gy") * lax.axis_size("gx") + lax.axis_index("gx")
     first = (group - core) * count_z + OWN * part - RADIUS
     bounds = jnp.stack(
         [jnp.maximum(0, -first), jnp.minimum(WINDOW, groups * count_z - first), core]
@@ -695,7 +702,7 @@
         bounds.astype(jnp.int32), recv, other, tables, down, up
     )
     back = lax.all_to_all(
-        result.reshape(parts, 2 * OWN, LANES), ("gx", "gy"), 0, 0, tiled=True
+        result.reshape(parts, 2 * OWN, LANES), ("gy", "gx"), 0, 0, tiled=True
     ).reshape(parts * 2 * OWN, LANES)
     return unpack(cores, back, scaling, fine_source_field.shape)
 

time: 76.4 us -> 76 us (level)
  the two profiles are of different devices: /device:TPU:10 before, /device:TPU:8 now
where the time goes in v11:
time: 76 us; the launch traced here: 75.7 us
  starting transfers between devices  22.7 us (30%)
  Pallas kernels  18.9 us (25%)
  blocking collectives  16.8 us (22%)
  waiting for transfers between devices  15.4 us (20%)
  local copies, waits for them, and re-layouts  1.61 us (2%)
    all_to_all x1, blocking collectives, per_device(): lax.all_to_all(result.reshape(parts, 2 * OWN, LANES), ('gy', 'gx'), 0, 0,...  16.8 us
    all_to_all x1, starting transfers between devices, per_device(): lax.all_to_all(chunks.reshape(parts * WINDOW // 2, 2, LANES), ('gy', 'gx'...  16.1 us
    all_to_all x1, waiting for transfers between devices, per_device(): lax.all_to_all(chunks.reshape(parts * WINDOW // 2, 2, LANES), ('gy', 'gx'...  12.1 us
    pallas_call x1, Pallas kernels, inverses(): pl.pallas_call(inverses_body, out_shape=jax.ShapeDtypeStruct((14, LANES,...  9.56 us
    pallas_call x1, Pallas kernels, cycle(): pl.pallas_call(cycle_body, out_shape=jax.ShapeDtypeStruct((EX * HALF * 2...  6.99 us
    ppermute x1, starting transfers between devices, per_device(): sibling = lax.ppermute(own, 'gz', pairs)  3.39 us
    ppermute x1, waiting for transfers between devices, per_device(): other = lax.ppermute(recv, ('gy', 'gz'), ways)  2.46 us
    ppermute x1, starting transfers between devices, per_device(): halo = settle(lax.ppermute(edge, 'gz', ties + [(j, i) for i, j in ties]))  1.92 us
  transfers between devices with their start and end apart: 4, of which 3 were waited for; matrix products, arithmetic and copies ran while one was open for 0% of the time, Pallas kernels for 13%

profile of v11, /device:TPU:8, one launch (start us, length us, event | category | flops | bytes accessed | tf_op | source)
XLA Modules:
  0.0 75.7 jit_solution(11773921439392876164)
XLA Ops:
  0.0 0.0 copy-start.3
  0.0 0.7 copy-done.3
  0.7 0.0 copy-start.2
  0.7 0.9 %copy-done.2 = f32[5,10,320]{2,1,0:T(8,128)S(1)} copy-done((f32[5,10,320]{2,1,0:T(8,128)S(1)}, f32[5,10,320]{2,1,0:T(8,128)}, u32[]{:S(2)}) %copy-start.2) | copy-done | bytes 64024
  1.6 0.3 pack.1
  1.9 1.9 %collective-permute-start.1 = (f32[2,16,128]{2,1,0:T(8,128)S(1)}, f32[2,16,128]{2,1,0:T(8,128)S(1)}, u32[]{:S(2)}, u32[]{:S(2)}) collective-permute-start(f32[2,16,128]{2,1,0:T(8,128)S(1)} %get-tuple-element.14), channel_id=1, source_target_pairs={{1,2},{3,4},{5,6},{7,8},{9,10},{11,12},{13,14},{2,1},{4,3},{6,5},{... | collective-permute-start | bytes 49160 | tf_op jit(solution)/shard_map/ppermute | solution.py:679
  3.9 3.4 %collective-permute-start = (f32[2,64,128]{2,1,0:T(8,128)S(1)}, f32[2,64,128]{2,1,0:T(8,128)S(1)}, u32[]{:S(2)}, u32[]{:S(2)}) collective-permute-start(f32[2,64,128]{2,1,0:T(8,128)S(1)} %get-tuple-element.13.refs_1_), channel_id=1, source_target_pairs={{0,1},{1,0},{2,3},{3,2},{4,5},{5,4},{6,7},{7,6},{8,9},{9,8},{10,11... | collective-permute-start | bytes 196616 | tf_op jit(solution)/shard_map/ppermute | solution.py:680
  7.2 0.0 collective-permute-done.1.in_ref
  7.3 0.9 %collective-permute-done.refs_2_ = f32[2,64,128]{2,1,0:T(8,128)S(1)} collective-permute-done((f32[2,64,128]{2,1,0:T(8,128)S(1)}, f32[2,64,128]{2,1,0:T(8,128)S(1)}, u32[]{:S(2)}, u32[]{:S(2)}) %collective-permute-start) | collective-permute-done | bytes 65568 | tf_op jit(solution)/shard_map/ppermute | solution.py:680
  8.1 0.9 %window.1 = f32[1088,128]{1,0:T(8,128)} custom-call(s32[1]{0:T(128)} %bitcast.refs_0_, f32[2,64,128]{2,1,0:T(8,128)S(1)} %get-tuple-element.13.refs_1_, f32[2,64,128]{2,1,0:T(8,128)S(1)} %collective-permute-done.refs_2_, f32[2,16,128]{2,1,0:T(8,128)S(1)} %settle.1.refs_3_), custom_call_target="tpu_custom_call" | custom-call | tf_op jit(solution)/shard_map/window/pallas_call | solution.py:176
  9.0 0.0 copy-start.4
  9.0 0.0 copy-start.5
  9.0 0.0 copy-start.6
  9.0 0.0 copy-start.7
  9.0 0.0 copy-start.8
  9.0 16.1 %all-to-all-start = ((f32[544,2,128]{2,1,0:T(2,128)}), f32[544,2,128]{2,1,0:T(2,128)S(1)}, u32[]{:S(2)}, u32[]{:S(2)}) async-start(f32[544,2,128]{2,1,0:T(2,128)} %bitcast.3), calls=%async_computation | async-start | bytes 1114112 | tf_op jit(solution)/shard_map/all_to_all | solution.py:683
  25.1 0.0 copy-done.4
  25.2 0.0 copy-done.5
  25.2 0.0 copy-done.6
  25.2 0.0 copy-done.7
  25.2 0.0 copy-done.8
  25.2 0.0 copy-start
  25.2 0.0 copy-start.1
  25.2 9.6 %inverses.1.tables_ref = bf16[14,128,256]{2,1,0:T(8,128)(2,1)S(1)} custom-call(f32[125,125]{1,0:T(8,128)S(1)} %copy-done.4, f32[27,27]{1,0:T(8,128)S(1)} %copy-done.5, f32[8,8]{1,0:T(8,128)S(1)} %copy-done.6, f32[4,128,128]{2,1,0:T(8,128)S(1)} %copy-done.7, f32[3,128,128]{2,1,0:T(8,128)S(1)} %copy-done.8), custom_call_target="tpu_custom_call" | custom-call | flops 2000000000 | bytes 20000000 | tf_op jit(solution)/shard_map/inverses/pallas_call | solution.py:337
  34.8 12.1 %all-to-all-done = f32[544,2,128]{2,1,0:T(2,128)S(1)} async-done(((f32[544,2,128]{2,1,0:T(2,128)}), f32[544,2,128]{2,1,0:T(2,128)S(1)}, u32[]{:S(2)}, u32[]{:S(2)}) %all-to-all-start) | async-done | bytes 557088 | tf_op jit(solution)/shard_map/all_to_all | solution.py:683
  46.9 1.3 %collective-permute-start.2 = (f32[1088,128]{1,0:T(8,128)S(1)}, f32[1088,128]{1,0:T(8,128)S(1)}, u32[]{:S(2)}, u32[]{:S(2)}) collective-permute-start(f32[1088,128]{1,0:T(8,128)S(1)} %bitcast.7), channel_id=1, source_target_pairs={{1,0},{3,2},{5,4},{7,6},{9,8},{11,10},{13,12},{15,14},{17,16},{19,... | collective-permute-start | bytes 1671176 | tf_op jit(solution)/shard_map/ppermute | solution.py:694
  48.2 0.1 pad_add_fusion.bounds_ref
  48.3 2.5 %collective-permute-done.2.other_ref = f32[1088,128]{1,0:T(8,128)S(1)} collective-permute-done((f32[1088,128]{1,0:T(8,128)S(1)}, f32[1088,128]{1,0:T(8,128)S(1)}, u32[]{:S(2)}, u32[]{:S(2)}) %collective-permute-start.2) | collective-permute-done | bytes 557088 | tf_op jit(solution)/shard_map/ppermute | solution.py:694
  50.8 0.0 copy-done
  50.8 0.0 copy-done.1
  50.8 7.0 %cycle.1 = f32[256,128]{1,0:T(8,128)S(1)} custom-call(s32[3]{0:T(128)S(1)} %pad_add_fusion.bounds_ref, f32[1088,128]{1,0:T(8,128)S(1)} %bitcast.8, f32[1088,128]{1,0:T(8,128)S(1)} %collective-permute-done.2.other_ref, bf16[14,128,256]{2,1,0:T(8,128)(2,1)S(1)} %inverses.1.tables_ref, bf16[4,128,256]{2,1,0:T(8,128)(2,1)S(1)} %copy-done.1, ...), custom_call_target="tpu_custom_call" | custom-call | tf_op jit(solution)/shard_map/cycle/pallas_call | solution.py:656
  57.8 16.8 %all_to_all.10 = f32[32,8,128]{2,1,0:T(8,128)S(1)} all-to-all(f32[32,8,128]{2,1,0:T(8,128)S(1)} %bitcast.9), channel_id=1, replica_groups=mesh['gx'=4,'gy'=8,'gz'=16] {'gy','gx'}, dimensions={0} | all-to-all | bytes 262144 | tf_op jit(solution)/shard_map/all_to_all | solution.py:704
  74.6 1.1 %unpack.1 = f32[5,10,320]{2,1,0:T(8,128)} custom-call(s32[1]{0:T(128)} %bitcast.refs_0_, f32[256,128]{1,0:T(8,128)S(1)} %bitcast.10, f32[1,2,64]{2,1,0:T(2,128)S(1)} %copy-done.3), custom_call_target="tpu_custom_call" | custom-call | tf_op jit(solution)/shard_map/unpack/pallas_call | solution.py:224
  (1 shorter events, 0.0 us)
Async XLA Ops:
  0.0 0.7 copy-start.3
  0.7 0.9 %copy-start.2 = (f32[5,10,320]{2,1,0:T(8,128)S(1)}, f32[5,10,320]{2,1,0:T(8,128)}, u32[]{:S(2)}) copy-start(f32[5,10,320]{2,1,0:T(8,128)} %refs_1_.1) | copy-start | bytes 192004
  1.9 5.3 %collective-permute-start.1 = (f32[2,16,128]{2,1,0:T(8,128)S(1)}, f32[2,16,128]{2,1,0:T(8,128)S(1)}, u32[]{:S(2)}, u32[]{:S(2)}) collective-permute-start(f32[2,16,128]{2,1,0:T(8,128)S(1)} %get-tuple-element.14), channel_id=1, source_target_pairs={{1,2},{3,4},{5,6},{7,8},{9,10},{11,12},{13,14},{2,1},{4,3},{6,5},{... | collective-permute-start | bytes 49160 | tf_op jit(solution)/shard_map/ppermute | solution.py:679
  3.9 4.3 %collective-permute-start = (f32[2,64,128]{2,1,0:T(8,128)S(1)}, f32[2,64,128]{2,1,0:T(8,128)S(1)}, u32[]{:S(2)}, u32[]{:S(2)}) collective-permute-start(f32[2,64,128]{2,1,0:T(8,128)S(1)} %get-tuple-element.13.refs_1_), channel_id=1, source_target_pairs={{0,1},{1,0},{2,3},{3,2},{4,5},{5,4},{6,7},{7,6},{8,9},{9,8},{10,11... | collective-permute-start | bytes 196616 | tf_op jit(solution)/shard_map/ppermute | solution.py:680
  9.0 16.1 %copy-start.4 = (f32[125,125]{1,0:T(8,128)S(1)}, f32[125,125]{1,0:T(8,128)}, u32[]{:S(2)}) copy-start(f32[125,125]{1,0:T(8,128)} %fine_ref) | copy-start | bytes 187504
  9.0 16.2 %copy-start.5 = (f32[27,27]{1,0:T(8,128)S(1)}, f32[27,27]{1,0:T(8,128)}, u32[]{:S(2)}) copy-start(f32[27,27]{1,0:T(8,128)} %mid_ref) | copy-start | bytes 8752
  9.0 16.2 %copy-start.6 = (f32[8,8]{1,0:T(8,128)S(1)}, f32[8,8]{1,0:T(8,128)}, u32[]{:S(2)}) copy-start(f32[8,8]{1,0:T(8,128)} %coarse_ref) | copy-start | bytes 772
  9.0 16.2 %copy-start.7 = (f32[4,128,128]{2,1,0:T(8,128)S(1)}, f32[4,128,128]{2,1,0:T(8,128)}, u32[]{:S(2)}) copy-start(f32[4,128,128]{2,1,0:T(8,128)} %constant.47.clone.low_ref) | copy-start | bytes 786436
  9.0 16.2 %copy-start.8 = (f32[3,128,128]{2,1,0:T(8,128)S(1)}, f32[3,128,128]{2,1,0:T(8,128)}, u32[]{:S(2)}) copy-start(f32[3,128,128]{2,1,0:T(8,128)} %constant.48.clone.high_ref) | copy-start | bytes 589828
  9.0 37.9 %all-to-all-start = ((f32[544,2,128]{2,1,0:T(2,128)}), f32[544,2,128]{2,1,0:T(2,128)S(1)}, u32[]{:S(2)}, u32[]{:S(2)}) async-start(f32[544,2,128]{2,1,0:T(2,128)} %bitcast.3), calls=%async_computation | async-start | bytes 1114112 | tf_op jit(solution)/shard_map/all_to_all | solution.py:683
  25.2 25.6 %copy-start = (bf16[4,128,256]{2,1,0:T(8,128)(2,1)S(1)}, bf16[4,128,256]{2,1,0:T(8,128)(2,1)}, u32[]{:S(2)}) copy-start(bf16[4,128,256]{2,1,0:T(8,128)(2,1)} %constant.50.clone.up_ref) | copy-start | bytes 786436
  25.2 25.6 %copy-start.1 = (bf16[4,128,256]{2,1,0:T(8,128)(2,1)S(1)}, bf16[4,128,256]{2,1,0:T(8,128)(2,1)}, u32[]{:S(2)}) copy-start(bf16[4,128,256]{2,1,0:T(8,128)(2,1)} %constant.49.clone.down_ref) | copy-start | bytes 786436
  46.9 3.8 %collective-permute-start.2 = (f32[1088,128]{1,0:T(8,128)S(1)}, f32[1088,128]{1,0:T(8,128)S(1)}, u32[]{:S(2)}, u32[]{:S(2)}) collective-permute-start(f32[1088,128]{1,0:T(8,128)S(1)} %bitcast.7), channel_id=1, source_target_pairs={{1,0},{3,2},{5,4},{7,6},{9,8},{11,10},{13,12},{15,14},{17,16},{19,... | collective-permute-start | bytes 1671176 | tf_op jit(solution)/shard_map/ppermute | solution.py:694

commit v12 on v8

--- a/solution.py
+++ b/solution.py
@@ -131,9 +131,24 @@
         in_specs=[pl.BlockSpec(memory_space=pltpu.SMEM), vmem, vmem],
         out_specs=(vmem, vmem),
         scratch_shapes=[pltpu.VMEM((LANES, width), f32), pltpu.VMEM((width, LANES), f32)],
-        compiler_params=pltpu.CompilerParams(vmem_limit_bytes=60 * MIB),
+        compiler_params=pltpu.CompilerParams(vmem_limit_bytes=8 * MIB),
         name="pack",
     )(core, field, scaling)
+
+
+def settle(halo):
+    def body(in_ref, out_ref):
+        out_ref[...] = in_ref[...]
+
+    return pl.pallas_call(
+        body,
+        out_shape=jax.ShapeDtypeStruct(halo.shape, f32),
+        cost_estimate=pl.CostEstimate(
+            flops=2_000_000_000, bytes_accessed=20_000_000, transcendentals=0
+        ),
+        compiler_params=pltpu.CompilerParams(vmem_limit_bytes=8 * MIB),
+        name="settle",
+    )(halo)
 
 
 PIECES = 4
@@ -166,7 +181,7 @@
                             block.at[place, :], out_ref.at[place, :], sems.at[piece]
                         )
                     )
-                    copies[-1].start()
+                    copies[-1].start(priority=piece % 2)
             for copy in copies:
                 copy.wait()
 
@@ -644,9 +659,22 @@
     for x in range(EX):
         rows = at(x, 12, WINDOW - 12)
         put(pong, rows, get(pong, rows) + times((lifted,), up_ref[x]))
-    fine_sweep(pong, ping, 13, WINDOW - 13, None)
-    fine_sweep(ping, pong, 14, WINDOW - 14, None)
-    fine_sweep(pong, ping, RADIUS, WINDOW - RADIUS, None)
+    def pair_sweep(source, target, margin):
+        a, b = margin, WINDOW - margin
+        count = (b - a) * EY
+        for x in range(0, EX, 2):
+            faces = [fine_gather(source, x + i, a, b) for i in range(2)]
+            faces = [jnp.concatenate(parts, axis=0) for parts in zip(*faces)]
+            moved = times(faces, *fine_tables)
+            for i in range(2):
+                rows = at(x + i, a, b)
+                part = 0.3 * get(source, rows) + get(start, rows)
+                part = part + moved[i * count : (i + 1) * count]
+                put(target, rows, part * get(mask, at(0, a, b)))
+
+    pair_sweep(pong, ping, 13)
+    pair_sweep(ping, pong, 14)
+    pair_sweep(pong, ping, RADIUS)
 
     for x in range(EX):
         for z in range(OWN):
@@ -683,7 +711,7 @@
     own, edge = pack(cores, fine_source_field, scaling)
     ties = [(i, i + 1) for i in range(1, groups - 1, 2)]
     pairs = [(i, i ^ 1) for i in range(groups)]
-    halo = lax.ppermute(edge, "gz", ties + [(j, i) for i, j in ties])
+    halo = settle(lax.ppermute(edge, "gz", ties + [(j, i) for i, j in ties]))
     sibling = lax.ppermute(own, "gz", pairs)
     chunks = window(cores, own, sibling, halo, parts)
     chunks, *matrices = lax.optimization_barrier((chunks, block_fine, block_mid, block_coarse))
@@ -691,7 +719,14 @@
         chunks.reshape(parts * WINDOW // 2, 2, LANES), ("gx", "gy"), 0, 0, tiled=True
     ).reshape(parts * WINDOW, LANES)
     recv, tables = lax.optimization_barrier((recv, inverses(*matrices, low, high)))
-    other = lax.ppermute(recv, "gz", pairs)
+    wide = lax.axis_size("gx")
+    ways = [
+        (x * groups + i, x * groups + (i ^ 1))
+        for x in range(wide)
+        for i in range(groups)
+        if i % 2 == (1 if 2 * x < wide else 0)
+    ]
+    other = lax.ppermute(recv, ("gx", "gz"), ways)
 
     part = lax.axis_index("gx") * lax.axis_size("gy") + lax.axis_index("gy")
     first = (group - core) * count_z + OWN * part - RADIUS

time: 78.9 us -> 75.5 us (0.957)
  the two profiles are of different devices: /device:TPU:4 before, /device:TPU:10 now
where the time goes in v12:
time: 75.5 us; the launch traced here: 75.2 us
  starting transfers between devices  22.7 us (30%)
  Pallas kernels  18.8 us (25%)
  blocking collectives  17.4 us (23%)
  waiting for transfers between devices  14.4 us (19%)
  local copies, waits for them, and re-layouts  1.63 us (2%)
    all_to_all x1, blocking collectives, per_device(): lax.all_to_all(result.reshape(parts, 2 * OWN, LANES), ('gx', 'gy'), 0, 0,...  17.4 us
    all_to_all x1, starting transfers between devices, per_device(): lax.all_to_all(chunks.reshape(parts * WINDOW // 2, 2, LANES), ('gx', 'gy'...  16.1 us
    all_to_all x1, waiting for transfers between devices, per_device(): lax.all_to_all(chunks.reshape(parts * WINDOW // 2, 2, LANES), ('gx', 'gy'...  11.1 us
    pallas_call x1, Pallas kernels, inverses(): pl.pallas_call(inverses_body, out_shape=jax.ShapeDtypeStruct((14, LANES,...  9.56 us
    pallas_call x1, Pallas kernels, cycle(): pl.pallas_call(cycle_body, out_shape=jax.ShapeDtypeStruct((EX * HALF * 2...  6.86 us
    ppermute x1, starting transfers between devices, per_device(): sibling = lax.ppermute(own, 'gz', pairs)  3.39 us
    ppermute x1, waiting for transfers between devices, per_device(): other = lax.ppermute(recv, ('gx', 'gz'), ways)  2.46 us
    ppermute x1, starting transfers between devices, per_device(): halo = settle(lax.ppermute(edge, 'gz', ties + [(j, i) for i, j in ties]))  1.92 us
  transfers between devices with their start and end apart: 4, of which 3 were waited for; matrix products, arithmetic and copies ran while one was open for 0% of the time, Pallas kernels for 13%

profile of v12, /device:TPU:10, one launch (start us, length us, event | category | flops | bytes accessed | tf_op | source)
XLA Modules:
  0.0 75.2 jit_solution(7380351719120369671)
XLA Ops:
  0.0 0.0 copy-start.3
  0.0 0.7 copy-done.3
  0.7 0.0 copy-start.2
  0.7 0.9 %copy-done.2 = f32[5,10,320]{2,1,0:T(8,128)S(1)} copy-done((f32[5,10,320]{2,1,0:T(8,128)S(1)}, f32[5,10,320]{2,1,0:T(8,128)}, u32[]{:S(2)}) %copy-start.2) | copy-done | bytes 64024
  1.6 0.3 pack.1
  1.9 1.9 %collective-permute-start.1 = (f32[2,16,128]{2,1,0:T(8,128)S(1)}, f32[2,16,128]{2,1,0:T(8,128)S(1)}, u32[]{:S(2)}, u32[]{:S(2)}) collective-permute-start(f32[2,16,128]{2,1,0:T(8,128)S(1)} %get-tuple-element.14), channel_id=1, source_target_pairs={{1,2},{3,4},{5,6},{7,8},{9,10},{11,12},{13,14},{2,1},{4,3},{6,5},{... | collective-permute-start | bytes 49160 | tf_op jit(solution)/shard_map/ppermute | solution.py:714
  3.9 3.4 %collective-permute-start = (f32[2,64,128]{2,1,0:T(8,128)S(1)}, f32[2,64,128]{2,1,0:T(8,128)S(1)}, u32[]{:S(2)}, u32[]{:S(2)}) collective-permute-start(f32[2,64,128]{2,1,0:T(8,128)S(1)} %get-tuple-element.13.refs_1_), channel_id=1, source_target_pairs={{0,1},{1,0},{2,3},{3,2},{4,5},{5,4},{6,7},{7,6},{8,9},{9,8},{10,11... | collective-permute-start | bytes 196616 | tf_op jit(solution)/shard_map/ppermute | solution.py:715
  7.2 0.0 collective-permute-done.1.in_ref
  7.3 0.9 %collective-permute-done.refs_2_ = f32[2,64,128]{2,1,0:T(8,128)S(1)} collective-permute-done((f32[2,64,128]{2,1,0:T(8,128)S(1)}, f32[2,64,128]{2,1,0:T(8,128)S(1)}, u32[]{:S(2)}, u32[]{:S(2)}) %collective-permute-start) | collective-permute-done | bytes 65568 | tf_op jit(solution)/shard_map/ppermute | solution.py:715
  8.1 0.9 %window.1 = f32[1088,128]{1,0:T(8,128)} custom-call(s32[1]{0:T(128)} %bitcast.refs_0_, f32[2,64,128]{2,1,0:T(8,128)S(1)} %get-tuple-element.13.refs_1_, f32[2,64,128]{2,1,0:T(8,128)S(1)} %collective-permute-done.refs_2_, f32[2,16,128]{2,1,0:T(8,128)S(1)} %settle.1.refs_3_), custom_call_target="tpu_custom_call" | custom-call | tf_op jit(solution)/shard_map/window/pallas_call | solution.py:194
  9.0 0.0 copy-start.4
  9.0 0.0 copy-start.5
  9.0 0.0 copy-start.6
  9.0 0.0 copy-start.7
  9.0 0.0 copy-start.8
  9.1 16.1 %all-to-all-start = ((f32[544,2,128]{2,1,0:T(2,128)}), f32[544,2,128]{2,1,0:T(2,128)S(1)}, u32[]{:S(2)}, u32[]{:S(2)}) async-start(f32[544,2,128]{2,1,0:T(2,128)} %bitcast.3), calls=%async_computation | async-start | bytes 1114112 | tf_op jit(solution)/shard_map/all_to_all | solution.py:718
  25.2 0.0 copy-done.4
  25.2 0.0 copy-done.5
  25.2 0.0 copy-done.6
  25.2 0.0 copy-done.7
  25.2 0.0 copy-done.8
  25.2 0.0 copy-start
  25.2 0.0 copy-start.1
  25.3 9.6 %inverses.1.tables_ref = bf16[14,128,256]{2,1,0:T(8,128)(2,1)S(1)} custom-call(f32[125,125]{1,0:T(8,128)S(1)} %copy-done.4, f32[27,27]{1,0:T(8,128)S(1)} %copy-done.5, f32[8,8]{1,0:T(8,128)S(1)} %copy-done.6, f32[4,128,128]{2,1,0:T(8,128)S(1)} %copy-done.7, f32[3,128,128]{2,1,0:T(8,128)S(1)} %copy-done.8), custom_call_target="tpu_custom_call" | custom-call | flops 2000000000 | bytes 20000000 | tf_op jit(solution)/shard_map/inverses/pallas_call | solution.py:359
  34.8 11.1 %all-to-all-done = f32[544,2,128]{2,1,0:T(2,128)S(1)} async-done(((f32[544,2,128]{2,1,0:T(2,128)}), f32[544,2,128]{2,1,0:T(2,128)S(1)}, u32[]{:S(2)}, u32[]{:S(2)}) %all-to-all-start) | async-done | bytes 557088 | tf_op jit(solution)/shard_map/all_to_all | solution.py:718
  45.9 1.3 %collective-permute-start.2 = (f32[1088,128]{1,0:T(8,128)S(1)}, f32[1088,128]{1,0:T(8,128)S(1)}, u32[]{:S(2)}, u32[]{:S(2)}) collective-permute-start(f32[1088,128]{1,0:T(8,128)S(1)} %bitcast.7), channel_id=1, source_target_pairs={{1,0},{3,2},{5,4},{7,6},{9,8},{11,10},{13,12},{15,14},{129,128},{1... | collective-permute-start | bytes 1671176 | tf_op jit(solution)/shard_map/ppermute | solution.py:729
  47.2 0.1 pad_add_fusion.bounds_ref
  47.3 2.5 %collective-permute-done.2.other_ref = f32[1088,128]{1,0:T(8,128)S(1)} collective-permute-done((f32[1088,128]{1,0:T(8,128)S(1)}, f32[1088,128]{1,0:T(8,128)S(1)}, u32[]{:S(2)}, u32[]{:S(2)}) %collective-permute-start.2) | collective-permute-done | bytes 557088 | tf_op jit(solution)/shard_map/ppermute | solution.py:729
  49.7 0.0 copy-done
  49.7 0.0 copy-done.1
  49.8 6.9 %cycle.1 = f32[256,128]{1,0:T(8,128)S(1)} custom-call(s32[3]{0:T(128)S(1)} %pad_add_fusion.bounds_ref, f32[1088,128]{1,0:T(8,128)S(1)} %bitcast.8, f32[1088,128]{1,0:T(8,128)S(1)} %collective-permute-done.2.other_ref, bf16[14,128,256]{2,1,0:T(8,128)(2,1)S(1)} %inverses.1.tables_ref, bf16[4,128,256]{2,1,0:T(8,128)(2,1)S(1)} %copy-done.1, ...), custom_call_target="tpu_custom_call" | custom-call | tf_op jit(solution)/shard_map/cycle/pallas_call | solution.py:691
  56.6 17.4 %all_to_all.10 = f32[32,8,128]{2,1,0:T(8,128)S(1)} all-to-all(f32[32,8,128]{2,1,0:T(8,128)S(1)} %bitcast.9), channel_id=1, replica_groups=mesh['gx'=4,'gy'=8,'gz'=16] {'gx','gy'}, dimensions={0} | all-to-all | bytes 262144 | tf_op jit(solution)/shard_map/all_to_all | solution.py:739
  74.0 1.1 %unpack.1 = f32[5,10,320]{2,1,0:T(8,128)} custom-call(s32[1]{0:T(128)} %bitcast.refs_0_, f32[256,128]{1,0:T(8,128)S(1)} %bitcast.10, f32[1,2,64]{2,1,0:T(2,128)S(1)} %copy-done.3), custom_call_target="tpu_custom_call" | custom-call | tf_op jit(solution)/shard_map/unpack/pallas_call | solution.py:246
  (1 shorter events, 0.0 us)
Async XLA Ops:
  0.0 0.7 copy-start.3
  0.7 0.9 %copy-start.2 = (f32[5,10,320]{2,1,0:T(8,128)S(1)}, f32[5,10,320]{2,1,0:T(8,128)}, u32[]{:S(2)}) copy-start(f32[5,10,320]{2,1,0:T(8,128)} %refs_1_.1) | copy-start | bytes 192004
  1.9 5.3 %collective-permute-start.1 = (f32[2,16,128]{2,1,0:T(8,128)S(1)}, f32[2,16,128]{2,1,0:T(8,128)S(1)}, u32[]{:S(2)}, u32[]{:S(2)}) collective-permute-start(f32[2,16,128]{2,1,0:T(8,128)S(1)} %get-tuple-element.14), channel_id=1, source_target_pairs={{1,2},{3,4},{5,6},{7,8},{9,10},{11,12},{13,14},{2,1},{4,3},{6,5},{... | collective-permute-start | bytes 49160 | tf_op jit(solution)/shard_map/ppermute | solution.py:714
  3.9 4.3 %collective-permute-start = (f32[2,64,128]{2,1,0:T(8,128)S(1)}, f32[2,64,128]{2,1,0:T(8,128)S(1)}, u32[]{:S(2)}, u32[]{:S(2)}) collective-permute-start(f32[2,64,128]{2,1,0:T(8,128)S(1)} %get-tuple-element.13.refs_1_), channel_id=1, source_target_pairs={{0,1},{1,0},{2,3},{3,2},{4,5},{5,4},{6,7},{7,6},{8,9},{9,8},{10,11... | collective-permute-start | bytes 196616 | tf_op jit(solution)/shard_map/ppermute | solution.py:715
  9.0 16.2 %copy-start.4 = (f32[125,125]{1,0:T(8,128)S(1)}, f32[125,125]{1,0:T(8,128)}, u32[]{:S(2)}) copy-start(f32[125,125]{1,0:T(8,128)} %fine_ref) | copy-start | bytes 187504
  9.0 16.2 %copy-start.5 = (f32[27,27]{1,0:T(8,128)S(1)}, f32[27,27]{1,0:T(8,128)}, u32[]{:S(2)}) copy-start(f32[27,27]{1,0:T(8,128)} %mid_ref) | copy-start | bytes 8752
  9.0 16.2 %copy-start.6 = (f32[8,8]{1,0:T(8,128)S(1)}, f32[8,8]{1,0:T(8,128)}, u32[]{:S(2)}) copy-start(f32[8,8]{1,0:T(8,128)} %coarse_ref) | copy-start | bytes 772
  9.0 16.2 %copy-start.7 = (f32[4,128,128]{2,1,0:T(8,128)S(1)}, f32[4,128,128]{2,1,0:T(8,128)}, u32[]{:S(2)}) copy-start(f32[4,128,128]{2,1,0:T(8,128)} %constant.49.clone.low_ref) | copy-start | bytes 786436
  9.0 16.2 %copy-start.8 = (f32[3,128,128]{2,1,0:T(8,128)S(1)}, f32[3,128,128]{2,1,0:T(8,128)}, u32[]{:S(2)}) copy-start(f32[3,128,128]{2,1,0:T(8,128)} %constant.50.clone.high_ref) | copy-start | bytes 589828
  9.1 36.8 %all-to-all-start = ((f32[544,2,128]{2,1,0:T(2,128)}), f32[544,2,128]{2,1,0:T(2,128)S(1)}, u32[]{:S(2)}, u32[]{:S(2)}) async-start(f32[544,2,128]{2,1,0:T(2,128)} %bitcast.3), calls=%async_computation | async-start | bytes 1114112 | tf_op jit(solution)/shard_map/all_to_all | solution.py:718
  25.2 24.5 %copy-start = (bf16[4,128,256]{2,1,0:T(8,128)(2,1)S(1)}, bf16[4,128,256]{2,1,0:T(8,128)(2,1)}, u32[]{:S(2)}) copy-start(bf16[4,128,256]{2,1,0:T(8,128)(2,1)} %constant.52.clone.up_ref) | copy-start | bytes 786436
  25.2 24.5 %copy-start.1 = (bf16[4,128,256]{2,1,0:T(8,128)(2,1)S(1)}, bf16[4,128,256]{2,1,0:T(8,128)(2,1)}, u32[]{:S(2)}) copy-start(bf16[4,128,256]{2,1,0:T(8,128)(2,1)} %constant.51.clone.down_ref) | copy-start | bytes 786436
  45.9 3.8 %collective-permute-start.2 = (f32[1088,128]{1,0:T(8,128)S(1)}, f32[1088,128]{1,0:T(8,128)S(1)}, u32[]{:S(2)}, u32[]{:S(2)}) collective-permute-start(f32[1088,128]{1,0:T(8,128)S(1)} %bitcast.7), channel_id=1, source_target_pairs={{1,0},{3,2},{5,4},{7,6},{9,8},{11,10},{13,12},{15,14},{129,128},{1... | collective-permute-start | bytes 1671176 | tf_op jit(solution)/shard_map/ppermute | solution.py:729

commit v13 on v10

--- a/solution.py
+++ b/solution.py
@@ -653,8 +653,17 @@
     big = pltpu.VMEM((EX * WINDOW, EY, LANES), f32)
     small = pltpu.VMEM((WINDOW, EY, LANES), f32)
     vmem = pl.BlockSpec(memory_space=pltpu.VMEM)
+    def body(bounds_ref, *refs):
+        @pl.when(bounds_ref[3] == 1)
+        def _():
+            cycle_body(bounds_ref, *refs)
+
+        @pl.when(bounds_ref[3] == 0)
+        def _():
+            refs[5][...] = jnp.zeros_like(refs[5])
+
     return pl.pallas_call(
-        cycle_body,
+        body,
         out_shape=jax.ShapeDtypeStruct((EX * HALF * 2 * OWN, LANES), f32),
         in_specs=[pl.BlockSpec(memory_space=pltpu.SMEM)] + [vmem] * 5,
         out_specs=vmem,
@@ -696,7 +705,12 @@
     part = lax.axis_index("gx") * lax.axis_size("gy") + lax.axis_index("gy")
     first = (group - core) * count_z + OWN * part - RADIUS
     bounds = jnp.stack(
-        [jnp.maximum(0, -first), jnp.minimum(WINDOW, groups * count_z - first), core]
+        [
+            jnp.maximum(0, -first),
+            jnp.minimum(WINDOW, groups * count_z - first),
+            core,
+            (core == part // (parts // 2)).astype(jnp.int32),
+        ]
     )
     result = cycle(
         bounds.astype(jnp.int32), recv, other, tables, down, up

time: 75.5 us -> 75.6 us (level)
  the two profiles are of different devices: /device:TPU:2 before, /device:TPU:10 now
where the time goes in v13:
time: 75.6 us; the launch traced here: 75.3 us
  starting transfers between devices  22.7 us (30%)
  Pallas kernels  18.8 us (25%)
  blocking collectives  17.5 us (23%)
  waiting for transfers between devices  14.4 us (19%)
  local copies, waits for them, and re-layouts  1.61 us (2%)
    all_to_all x1, blocking collectives, per_device(): lax.all_to_all(result.reshape(parts, 2 * OWN, LANES), ('gx', 'gy'), 0, 0,...  17.5 us
    all_to_all x1, starting transfers between devices, per_device(): lax.all_to_all(chunks.reshape(parts * WINDOW // 2, 2, LANES), ('gx', 'gy'...  16.1 us
    all_to_all x1, waiting for transfers between devices, per_device(): lax.all_to_all(chunks.reshape(parts * WINDOW // 2, 2, LANES), ('gx', 'gy'...  11.1 us
    pallas_call x1, Pallas kernels, inverses(): pl.pallas_call(inverses_body, out_shape=jax.ShapeDtypeStruct((14, LANES,...  9.56 us
    pallas_call x1, Pallas kernels, cycle(): pl.pallas_call(body, out_shape=jax.ShapeDtypeStruct((EX * HALF * 2 * OWN,...  6.91 us
    ppermute x1, starting transfers between devices, per_device(): sibling = lax.ppermute(own, 'gz', pairs)  3.39 us
    ppermute x1, waiting for transfers between devices, per_device(): other = lax.ppermute(recv, ('gx', 'gz'), ways)  2.44 us
    ppermute x1, starting transfers between devices, per_device(): halo = settle(lax.ppermute(edge, 'gz', ties + [(j, i) for i, j in ties]))  1.92 us
  transfers between devices with their start and end apart: 4, of which 3 were waited for; matrix products, arithmetic and copies ran while one was open for 0% of the time, Pallas kernels for 13%

profile of v13, /device:TPU:10, one launch (start us, length us, event | category | flops | bytes accessed | tf_op | source)
XLA Modules:
  0.0 75.3 jit_solution(10634938736536940887)
XLA Ops:
  0.0 0.0 copy-start.3
  0.0 0.7 copy-done.3
  0.7 0.0 copy-start.2
  0.7 0.9 %copy-done.2 = f32[5,10,320]{2,1,0:T(8,128)S(1)} copy-done((f32[5,10,320]{2,1,0:T(8,128)S(1)}, f32[5,10,320]{2,1,0:T(8,128)}, u32[]{:S(2)}) %copy-start.2) | copy-done | bytes 64024
  1.6 0.3 pack.1
  1.9 1.9 %collective-permute-start.1 = (f32[2,16,128]{2,1,0:T(8,128)S(1)}, f32[2,16,128]{2,1,0:T(8,128)S(1)}, u32[]{:S(2)}, u32[]{:S(2)}) collective-permute-start(f32[2,16,128]{2,1,0:T(8,128)S(1)} %get-tuple-element.14), channel_id=1, source_target_pairs={{1,2},{3,4},{5,6},{7,8},{9,10},{11,12},{13,14},{2,1},{4,3},{6,5},{... | collective-permute-start | bytes 49160 | tf_op jit(solution)/shard_map/ppermute | solution.py:688
  3.9 3.4 %collective-permute-start = (f32[2,64,128]{2,1,0:T(8,128)S(1)}, f32[2,64,128]{2,1,0:T(8,128)S(1)}, u32[]{:S(2)}, u32[]{:S(2)}) collective-permute-start(f32[2,64,128]{2,1,0:T(8,128)S(1)} %get-tuple-element.13.refs_1_), channel_id=1, source_target_pairs={{0,1},{1,0},{2,3},{3,2},{4,5},{5,4},{6,7},{7,6},{8,9},{9,8},{10,11... | collective-permute-start | bytes 196616 | tf_op jit(solution)/shard_map/ppermute | solution.py:689
  7.2 0.0 collective-permute-done.1.in_ref
  7.3 0.9 %collective-permute-done.refs_2_ = f32[2,64,128]{2,1,0:T(8,128)S(1)} collective-permute-done((f32[2,64,128]{2,1,0:T(8,128)S(1)}, f32[2,64,128]{2,1,0:T(8,128)S(1)}, u32[]{:S(2)}, u32[]{:S(2)}) %collective-permute-start) | collective-permute-done | bytes 65568 | tf_op jit(solution)/shard_map/ppermute | solution.py:689
  8.1 0.9 %window.1 = f32[1088,128]{1,0:T(8,128)} custom-call(s32[1]{0:T(128)} %bitcast.refs_0_, f32[2,64,128]{2,1,0:T(8,128)S(1)} %get-tuple-element.13.refs_1_, f32[2,64,128]{2,1,0:T(8,128)S(1)} %collective-permute-done.refs_2_, f32[2,16,128]{2,1,0:T(8,128)S(1)} %settle.1.refs_3_), custom_call_target="tpu_custom_call" | custom-call | tf_op jit(solution)/shard_map/window/pallas_call | solution.py:176
  9.0 0.0 copy-start.4
  9.0 0.0 copy-start.5
  9.0 0.0 copy-start.6
  9.0 0.0 copy-start.7
  9.0 0.0 copy-start.8
  9.0 16.1 %all-to-all-start = ((f32[544,2,128]{2,1,0:T(2,128)}), f32[544,2,128]{2,1,0:T(2,128)S(1)}, u32[]{:S(2)}, u32[]{:S(2)}) async-start(f32[544,2,128]{2,1,0:T(2,128)} %bitcast.4), calls=%async_computation | async-start | bytes 1114112 | tf_op jit(solution)/shard_map/all_to_all | solution.py:692
  25.1 0.0 copy-done.4
  25.2 0.0 copy-done.5
  25.2 0.0 copy-done.6
  25.2 0.0 copy-done.7
  25.2 0.0 copy-done.8
  25.2 0.0 copy-start
  25.2 0.0 copy-start.1
  25.2 9.6 %inverses.1.refs_2_ = bf16[14,128,256]{2,1,0:T(8,128)(2,1)S(1)} custom-call(f32[125,125]{1,0:T(8,128)S(1)} %copy-done.4, f32[27,27]{1,0:T(8,128)S(1)} %copy-done.5, f32[8,8]{1,0:T(8,128)S(1)} %copy-done.6, f32[4,128,128]{2,1,0:T(8,128)S(1)} %copy-done.7, f32[3,128,128]{2,1,0:T(8,128)S(1)} %copy-done.8), custom_call_target="tpu_custom_call" | custom-call | flops 2000000000 | bytes 20000000 | tf_op jit(solution)/shard_map/inverses/pallas_call | solution.py:337
  34.8 11.1 %all-to-all-done = f32[544,2,128]{2,1,0:T(2,128)S(1)} async-done(((f32[544,2,128]{2,1,0:T(2,128)}), f32[544,2,128]{2,1,0:T(2,128)S(1)}, u32[]{:S(2)}, u32[]{:S(2)}) %all-to-all-start) | async-done | bytes 557088 | tf_op jit(solution)/shard_map/all_to_all | solution.py:692
  45.9 1.3 %collective-permute-start.2 = (f32[1088,128]{1,0:T(8,128)S(1)}, f32[1088,128]{1,0:T(8,128)S(1)}, u32[]{:S(2)}, u32[]{:S(2)}) collective-permute-start(f32[1088,128]{1,0:T(8,128)S(1)} %bitcast.8), channel_id=1, source_target_pairs={{1,0},{3,2},{5,4},{7,6},{9,8},{11,10},{13,12},{15,14},{129,128},{1... | collective-permute-start | bytes 1671176 | tf_op jit(solution)/shard_map/ppermute | solution.py:703
  47.2 0.1 pad_add_fusion.bounds_ref
  47.3 2.4 %collective-permute-done.2.refs_1_ = f32[1088,128]{1,0:T(8,128)S(1)} collective-permute-done((f32[1088,128]{1,0:T(8,128)S(1)}, f32[1088,128]{1,0:T(8,128)S(1)}, u32[]{:S(2)}, u32[]{:S(2)}) %collective-permute-start.2) | collective-permute-done | bytes 557088 | tf_op jit(solution)/shard_map/ppermute | solution.py:703
  49.7 0.0 copy-done
  49.7 0.0 copy-done.1
  49.7 6.9 %cycle.1 = f32[256,128]{1,0:T(8,128)S(1)} custom-call(s32[4]{0:T(128)S(1)} %pad_add_fusion.bounds_ref, f32[1088,128]{1,0:T(8,128)S(1)} %bitcast.9, f32[1088,128]{1,0:T(8,128)S(1)} %collective-permute-done.2.refs_1_, bf16[14,128,256]{2,1,0:T(8,128)(2,1)S(1)} %inverses.1.refs_2_, bf16[4,128,256]{2,1,0:T(8,128)(2,1)S(1)} %copy-done.1, ...), custom_call_target="tpu_custom_call" | custom-call | tf_op jit(solution)/shard_map/cycle/pallas_call | solution.py:665
  56.6 17.5 %all_to_all.10 = f32[32,8,128]{2,1,0:T(8,128)S(1)} all-to-all(f32[32,8,128]{2,1,0:T(8,128)S(1)} %bitcast.10), channel_id=1, replica_groups=mesh['gx'=4,'gy'=8,'gz'=16] {'gx','gy'}, dimensions={0} | all-to-all | bytes 262144 | tf_op jit(solution)/shard_map/all_to_all | solution.py:718
  74.1 1.1 %unpack.1 = f32[5,10,320]{2,1,0:T(8,128)} custom-call(s32[1]{0:T(128)} %bitcast.refs_0_, f32[256,128]{1,0:T(8,128)S(1)} %bitcast.11, f32[1,2,64]{2,1,0:T(2,128)S(1)} %copy-done.3), custom_call_target="tpu_custom_call" | custom-call | tf_op jit(solution)/shard_map/unpack/pallas_call | solution.py:224
  (1 shorter events, 0.0 us)
Async XLA Ops:
  0.0 0.7 copy-start.3
  0.7 0.9 %copy-start.2 = (f32[5,10,320]{2,1,0:T(8,128)S(1)}, f32[5,10,320]{2,1,0:T(8,128)}, u32[]{:S(2)}) copy-start(f32[5,10,320]{2,1,0:T(8,128)} %refs_1_.1) | copy-start | bytes 192004
  1.9 5.3 %collective-permute-start.1 = (f32[2,16,128]{2,1,0:T(8,128)S(1)}, f32[2,16,128]{2,1,0:T(8,128)S(1)}, u32[]{:S(2)}, u32[]{:S(2)}) collective-permute-start(f32[2,16,128]{2,1,0:T(8,128)S(1)} %get-tuple-element.14), channel_id=1, source_target_pairs={{1,2},{3,4},{5,6},{7,8},{9,10},{11,12},{13,14},{2,1},{4,3},{6,5},{... | collective-permute-start | bytes 49160 | tf_op jit(solution)/shard_map/ppermute | solution.py:688
  3.9 4.3 %collective-permute-start = (f32[2,64,128]{2,1,0:T(8,128)S(1)}, f32[2,64,128]{2,1,0:T(8,128)S(1)}, u32[]{:S(2)}, u32[]{:S(2)}) collective-permute-start(f32[2,64,128]{2,1,0:T(8,128)S(1)} %get-tuple-element.13.refs_1_), channel_id=1, source_target_pairs={{0,1},{1,0},{2,3},{3,2},{4,5},{5,4},{6,7},{7,6},{8,9},{9,8},{10,11... | collective-permute-start | bytes 196616 | tf_op jit(solution)/shard_map/ppermute | solution.py:689
  9.0 16.1 %copy-start.4 = (f32[125,125]{1,0:T(8,128)S(1)}, f32[125,125]{1,0:T(8,128)}, u32[]{:S(2)}) copy-start(f32[125,125]{1,0:T(8,128)} %fine_ref) | copy-start | bytes 187504
  9.0 16.1 %copy-start.5 = (f32[27,27]{1,0:T(8,128)S(1)}, f32[27,27]{1,0:T(8,128)}, u32[]{:S(2)}) copy-start(f32[27,27]{1,0:T(8,128)} %mid_ref) | copy-start | bytes 8752
  9.0 16.2 %copy-start.6 = (f32[8,8]{1,0:T(8,128)S(1)}, f32[8,8]{1,0:T(8,128)}, u32[]{:S(2)}) copy-start(f32[8,8]{1,0:T(8,128)} %coarse_ref) | copy-start | bytes 772
  9.0 16.2 %copy-start.7 = (f32[4,128,128]{2,1,0:T(8,128)S(1)}, f32[4,128,128]{2,1,0:T(8,128)}, u32[]{:S(2)}) copy-start(f32[4,128,128]{2,1,0:T(8,128)} %constant.62.clone.low_ref) | copy-start | bytes 786436
  9.0 16.2 %copy-start.8 = (f32[3,128,128]{2,1,0:T(8,128)S(1)}, f32[3,128,128]{2,1,0:T(8,128)}, u32[]{:S(2)}) copy-start(f32[3,128,128]{2,1,0:T(8,128)} %constant.63.clone.high_ref) | copy-start | bytes 589828
  9.0 36.9 %all-to-all-start = ((f32[544,2,128]{2,1,0:T(2,128)}), f32[544,2,128]{2,1,0:T(2,128)S(1)}, u32[]{:S(2)}, u32[]{:S(2)}) async-start(f32[544,2,128]{2,1,0:T(2,128)} %bitcast.4), calls=%async_computation | async-start | bytes 1114112 | tf_op jit(solution)/shard_map/all_to_all | solution.py:692
  25.2 24.5 %copy-start = (bf16[4,128,256]{2,1,0:T(8,128)(2,1)S(1)}, bf16[4,128,256]{2,1,0:T(8,128)(2,1)}, u32[]{:S(2)}) copy-start(bf16[4,128,256]{2,1,0:T(8,128)(2,1)} %constant.65.clone.refs_4_) | copy-start | bytes 786436
  25.2 24.5 %copy-start.1 = (bf16[4,128,256]{2,1,0:T(8,128)(2,1)S(1)}, bf16[4,128,256]{2,1,0:T(8,128)(2,1)}, u32[]{:S(2)}) copy-start(bf16[4,128,256]{2,1,0:T(8,128)(2,1)} %constant.64.clone.refs_3_) | copy-start | bytes 786436
  45.9 3.8 %collective-permute-start.2 = (f32[1088,128]{1,0:T(8,128)S(1)}, f32[1088,128]{1,0:T(8,128)S(1)}, u32[]{:S(2)}, u32[]{:S(2)}) collective-permute-start(f32[1088,128]{1,0:T(8,128)S(1)} %bitcast.8), channel_id=1, source_target_pairs={{1,0},{3,2},{5,4},{7,6},{9,8},{11,10},{13,12},{15,14},{129,128},{1... | collective-permute-start | bytes 1671176 | tf_op jit(solution)/shard_map/ppermute | solution.py:703
